TPU v7x, 32 devices: a whole 2x2x4 slice. The times are simulated.
32 devices in a mesh: groups: 2 (over y), tile: 4 (over z), depth: 2 (over x), chan: 2 (over core).
Axes of the slice: x: 2, y: 2, z: 4, core: 2. Of those that a mesh axis runs over, the one named last changes fastest.
Arguments:
- log_features: bfloat16 [16, 64, 128, 128], P(('groups', 'tile', 'depth'), None, 'chan'), parts along dimension 0, may hold values from -3 to 3
- send_slot: int32 [16, 8, 16], P(('groups', 'tile', 'depth')), parts along dimension 0, may hold values from -1 to 63, as said below
- merge_slot: int32 [16, 8, 16], P(('groups', 'tile', 'depth')), parts along dimension 0, may hold values from -1 to 3, as said below
- halo_list: int32 [16, 4, 2], P(('groups', 'tile', 'depth')), parts along dimension 0, may hold values from 0 to 3, as said below
- in_rows: int32 [16, 27, 128], P(('groups', 'tile', 'depth')), parts along dimension 0, may hold values from 0 to 1535, as said below
- out_rows: int32 [16, 27, 128], P(('groups', 'tile', 'depth')), parts along dimension 0, may hold values from 0 to 511, as said below
- pair_count: int32 [16, 27], P(('groups', 'tile', 'depth')), parts along dimension 0, may hold values from 17 to 128
- weight: bfloat16 [27, 128, 128], replicated, may hold values from -0.1875 to 0.1875
- cotangent: bfloat16 [16, 4, 128, 128], P(('groups', 'tile', 'depth'), None, 'chan'), parts along dimension 0, may hold values from -6 to 6
Outputs:
- activations: bfloat16 [16, 4, 128, 128], P(('groups', 'tile', 'depth'), None, 'chan'), parts along dimension 0
- grad_log: bfloat16 [16, 64, 128, 128], P(('groups', 'tile', 'depth'), None, 'chan'), parts along dimension 0
- grad_weight: float32 [54, 128, 128], P('groups', 'chan'), parts along dimension 0
There are 2 independent parts, one for each index of `groups`. A program takes and returns all parts, laid end to end along the dimension named above; an argument that names none is the same for every part. Nothing has to cross between parts.
Inputs may be any that keep to these rules, and one draw needn't show every extreme that they name: send_slot[s, p, c] is the log block of shard s in slot c towards tile p, or -1 for an empty slot; every log block of a shard occupies exactly one slot; one tile, the same for every shard, receives a full 16 slots from every shard and the remaining blocks go to the other tiles. merge_slot[p, s, c] is -1 exactly where send_slot[s, p, c] is -1. The 2 entries of halo_list[t, d] are distinct; d = 0, 1, 2, 3 is the neighbour t - 2, t + 2, t - 1, t + 1. `in_rows`: entries of one tile and offset are distinct; entries at positions from pair_count on are padding. `out_rows`: entries of one tile and offset are distinct; entries at positions from pair_count on are padding.
All inputs are finite; a program needn't handle non-finite values.
Results may differ from a plain program's by a relative error of at most 0.0058.
Values may be sent and summed in bfloat16 or wider, within the bound.
No kernel may reach another device: no remote copies, remote signals or barrier semaphores. Data moves between devices by JAX's collectives and lax.ppermute only.
A program may use at most 64 MiB of HBM per device.

v0:
```python
import jax
import jax.numpy as jnp
from jax import lax
from jax.sharding import PartitionSpec as P


def extended_2(array, sides, width):
    for axis, dim in sides:
        size, length = (lax.axis_size(axis), array.shape[dim])
        up = [(i, (i + 1) % size) for i in range(size - 1)]
        down = [(j, i) for i, j in up]
        last = lax.slice_in_dim(array, length - width, length, axis=dim)
        initial = lax.slice_in_dim(array, 0, width, axis=dim)
        before = lax.ppermute(last, axis, up)
        after = lax.ppermute(initial, axis, down)
        array = jnp.concatenate([before, array, after], axis=dim)
    return array


def relay(outgoing):
    return lax.all_to_all(outgoing, ("tile", "depth"), split_axis=0, concat_axis=0, tiled=True)


def rims(along_tile, along_depth):
    tile_padded = extended_2(along_tile, (("tile", 0),), 1)
    depth_padded = extended_2(along_depth, (("depth", 0),), 1)
    return (tile_padded[0], tile_padded[3], depth_padded[0], depth_padded[3])


def select_table(row_ids, row_total):
    return (jnp.arange(row_total, dtype=jnp.int32)[:, None] == row_ids[None, :]).astype(
        jnp.bfloat16
    )


def apply_offsets(ext_matrix, kernel, source_rows, target_rows, out_total):
    ext_total = ext_matrix.shape[1]

    def forward(running, offset):
        source_table = select_table(source_rows[offset], ext_total)
        columns = jnp.dot(ext_matrix, source_table, preferred_element_type=jnp.float32).astype(
            jnp.bfloat16
        )
        target_table = select_table(target_rows[offset], out_total)
        placed = lax.dot_general(
            columns, target_table, (((1,), (1,)), ((), ())), preferred_element_type=jnp.float32
        ).astype(jnp.bfloat16)
        product = lax.dot_general(
            kernel[offset], placed, (((0,), (0,)), ((), ())), preferred_element_type=jnp.float32
        )
        return (running + product, None)

    start_total = jnp.zeros((kernel.shape[2], out_total), jnp.float32)
    running, _ = lax.scan(forward, start_total, jnp.arange(kernel.shape[0], dtype=jnp.int32))
    return running


def local(
    log_features, send_slot, merge_slot, halo_list, in_rows, out_rows, pair_count, weight, cotangent
):
    tile_rows = lax.axis_size("tile")
    depths = lax.axis_size("depth")
    tile_count = tile_rows * depths
    log_blocks = log_features[0]
    log_count, half_width, block_rows = log_blocks.shape
    tile_blocks = cotangent.shape[1]
    offsets, channels, _ = weight.shape
    capacity = send_slot.shape[2]
    rim_count = halo_list.shape[2]
    pair_slots = in_rows.shape[2]
    ext_blocks = tile_blocks + 4 * rim_count
    row_width = half_width * block_rows
    ext_total = (ext_blocks + 1) * block_rows
    out_total = (tile_blocks + 1) * block_rows
    own_total = tile_blocks * block_rows
    send_slots = send_slot[0].reshape(-1)
    pick_table = (send_slots[:, None] == jnp.arange(log_count, dtype=jnp.int32)[None, :]).astype(
        jnp.bfloat16
    )
    outgoing = jnp.dot(
        pick_table, log_blocks.reshape(log_count, row_width), preferred_element_type=jnp.float32
    ).astype(jnp.bfloat16)
    incoming = relay(outgoing.reshape(tile_count, capacity, half_width, block_rows))
    merge_targets = merge_slot[0].reshape(-1)
    place_table = (
        jnp.arange(tile_blocks, dtype=jnp.int32)[:, None] == merge_targets[None, :]
    ).astype(jnp.bfloat16)
    features = jnp.dot(
        place_table,
        incoming.reshape(tile_count * capacity, row_width),
        preferred_element_type=jnp.float32,
    )
    features = features.astype(jnp.bfloat16).reshape(tile_blocks, half_width, block_rows)
    rim_lists = halo_list[0]
    lower_tile, upper_tile, lower_depth, upper_depth = rims(
        jnp.stack([features[rim_lists[0]], features[rim_lists[1]]]),
        jnp.stack([features[rim_lists[2]], features[rim_lists[3]]]),
    )
    zero_block = jnp.zeros((1, half_width, block_rows), jnp.bfloat16)
    extended = jnp.concatenate(
        [features, lower_tile, upper_tile, lower_depth, upper_depth, zero_block], 0
    )
    ext_matrix = extended.transpose(1, 0, 2).reshape(half_width, ext_total)
    live_mask = jnp.arange(pair_slots, dtype=jnp.int32)[None, :] < pair_count[0][:, None]
    source_rows = jnp.where(live_mask, in_rows[0], ext_blocks * block_rows)
    target_rows = jnp.where(live_mask, out_rows[0], own_total)
    channel_start = lax.axis_index("chan") * half_width
    w_rows = lax.dynamic_slice_in_dim(weight, channel_start, half_width, 1)
    w_cols = lax.dynamic_slice_in_dim(weight, channel_start, half_width, 2)
    preact_matrix = apply_offsets(
        lax.all_gather(ext_matrix, "chan", axis=0, tiled=True),
        w_cols,
        source_rows,
        target_rows,
        out_total,
    )[:, :own_total]
    preact = preact_matrix.reshape(half_width, tile_blocks, block_rows).transpose(1, 0, 2)
    activations = jax.nn.silu(preact).astype(jnp.bfloat16)
    sigmoid_pre = jax.nn.sigmoid(preact_matrix)
    cotangent_matrix = (
        cotangent[0].transpose(1, 0, 2).reshape(half_width, own_total).astype(jnp.float32)
    )
    grad_half = (
        cotangent_matrix * sigmoid_pre * (1.0 + preact_matrix * (1.0 - sigmoid_pre))
    ).astype(jnp.bfloat16)
    grad_full = lax.all_gather(grad_half, "chan", axis=0, tiled=True)
    grad_matrix = jnp.concatenate([grad_full, jnp.zeros((channels, block_rows), jnp.bfloat16)], 1)

    def backward(grad_extended, offset):
        source_table = select_table(source_rows[offset], ext_total)
        target_table = select_table(target_rows[offset], out_total)
        columns = jnp.dot(ext_matrix, source_table, preferred_element_type=jnp.float32).astype(
            jnp.bfloat16
        )
        grad_columns = jnp.dot(
            grad_matrix, target_table, preferred_element_type=jnp.float32
        ).astype(jnp.bfloat16)
        spread = lax.dot_general(
            grad_columns, source_table, (((1,), (1,)), ((), ())), preferred_element_type=jnp.float32
        ).astype(jnp.bfloat16)
        returned = jnp.dot(w_rows[offset], spread, preferred_element_type=jnp.float32)
        weight_term = lax.dot_general(
            columns, grad_columns, (((1,), (1,)), ((), ())), preferred_element_type=jnp.float32
        )
        return (grad_extended + returned, weight_term)

    grad_start = jnp.zeros((half_width, ext_total), jnp.float32)
    grad_matrix_ext, weight_terms = lax.scan(
        backward, grad_start, jnp.arange(offsets, dtype=jnp.int32)
    )
    grad_extended = grad_matrix_ext.reshape(half_width, ext_blocks + 1, block_rows).transpose(
        1, 0, 2
    )
    rim_grads = (
        grad_extended[tile_blocks:ext_blocks]
        .astype(jnp.bfloat16)
        .reshape(4, rim_count, half_width, block_rows)
    )
    from_lower, from_upper, from_left, from_right = rims(
        jnp.stack([rim_grads[0], rim_grads[1]]), jnp.stack([rim_grads[2], rim_grads[3]])
    )
    tile_grad = grad_extended[:tile_blocks]
    tile_grad = tile_grad.at[rim_lists[0]].add(from_lower.astype(jnp.float32))
    tile_grad = tile_grad.at[rim_lists[1]].add(from_upper.astype(jnp.float32))
    tile_grad = tile_grad.at[rim_lists[2]].add(from_left.astype(jnp.float32))
    tile_grad = tile_grad.at[rim_lists[3]].add(from_right.astype(jnp.float32))
    tile_grad = tile_grad.astype(jnp.bfloat16)
    back_blocks = jnp.dot(
        place_table.T, tile_grad.reshape(tile_blocks, row_width), preferred_element_type=jnp.float32
    ).astype(jnp.bfloat16)
    returned_blocks = relay(back_blocks.reshape(tile_count, capacity, half_width, block_rows))
    grad_log = jnp.dot(
        pick_table.T,
        returned_blocks.reshape(tile_count * capacity, row_width),
        preferred_element_type=jnp.float32,
    ).astype(jnp.bfloat16)
    weight_total = lax.psum(weight_terms, ("tile", "depth"))
    grad_weight = weight_total * float(tile_count * pair_slots) ** (-0.5)
    return (activations[None], grad_log.reshape(1, log_count, half_width, block_rows), grad_weight)


def solution(mesh):
    in_specs = (
        P(("groups", "tile", "depth"), None, "chan", None),
        P(("groups", "tile", "depth"), None, None),
        P(("groups", "tile", "depth"), None, None),
        P(("groups", "tile", "depth"), None, None),
        P(("groups", "tile", "depth"), None, None),
        P(("groups", "tile", "depth"), None, None),
        P(("groups", "tile", "depth"), None),
        P(),
        P(("groups", "tile", "depth"), None, "chan", None),
    )
    out_specs = (
        P(("groups", "tile", "depth"), None, "chan", None),
        P(("groups", "tile", "depth"), None, "chan", None),
        P("groups", "chan", None),
    )
    return jax.shard_map(local, mesh=mesh, in_specs=in_specs, out_specs=out_specs, check_vma=False)
```

profile of v0, /device:TPU:0, one launch (start us, length us, event | category | flops | bytes accessed | tf_op | source)
XLA Modules:
  0.0 519.1 jit_solution(3507981507668924728)
XLA Ops:
  8.0 2.1 fusion.27
  12.1 7.4 %all-to-all-start = ((bf16[8,16,64,128]{3,2,1,0:T(8,128)(2,1)}), bf16[8,16,64,128]{3,2,1,0:T(8,128)(2,1)S(1)}, u32[]{:S(2)}, u32[]{:S(2)}) async-start(bf16[8,16,64,128]{3,2,1,0:T(8,128)(2,1)} %bitcast.197), calls=%async_computation | async-start | bytes 4194304 | tf_op jit(solution)/shard_map/all_to_all | solution.py:21
  23.6 44.1 %all-to-all-done = bf16[8,16,64,128]{3,2,1,0:T(8,128)(2,1)S(1)} async-done(((bf16[8,16,64,128]{3,2,1,0:T(8,128)(2,1)}), bf16[8,16,64,128]{3,2,1,0:T(8,128)(2,1)S(1)}, u32[]{:S(2)}, u32[]{:S(2)}) %all-to-all-start) | async-done | bytes 2097184 | tf_op jit(solution)/shard_map/all_to_all | solution.py:21
  74.0 3.2 collective-permute-start.2
  79.2 4.4 collective-permute-done.3
  83.7 2.1 all_gather.6
  85.8 135.3 %while.24 = (s32[]{:T(128)}, f32[64,640]{1,0:T(8,128)}, s32[27]{0:T(128)S(1)}, bf16[27,128,64]{2,1,0:T(8,128)(2,1)}, s32[27,128]{1,0:T(8,128)S(1)}, /*index=5*/b...) while((s32[]{:T(128)}, f32[64,640]{1,0:T(8,128)}, ...), condition=%wide.region_1.2_spmd.clone, body=%wide.region_0.1_spmd.clone.sunk | while | flops 86671360 | bytes 855205 | solution.py:54
  93.7 2.0 convolution_add_fusion.4
  98.7 2.0 convolution_add_fusion.4
  103.7 2.0 convolution_add_fusion.4
  113.7 2.0 convolution_add_fusion.4
  118.8 2.0 convolution_add_fusion.4
  123.8 2.0 convolution_add_fusion.4
  128.8 2.0 convolution_add_fusion.4
  133.8 2.0 convolution_add_fusion.4
  138.8 2.0 convolution_add_fusion.4
  143.9 2.0 convolution_add_fusion.4
  153.9 2.0 convolution_add_fusion.4
  158.9 2.0 convolution_add_fusion.4
  169.0 2.0 convolution_add_fusion.4
  174.0 2.0 convolution_add_fusion.4
  179.0 2.0 convolution_add_fusion.4
  184.0 2.0 convolution_add_fusion.4
  189.0 2.0 convolution_add_fusion.4
  194.0 2.0 convolution_add_fusion.4
  199.1 2.0 convolution_add_fusion.4
  209.1 2.0 convolution_add_fusion.4
  224.6 155.7 %while.25 = (s32[]{:T(128)}, f32[64,1664]{1,0:T(8,128)S(1)}, f32[27,64,128]{2,1,0:T(8,128)}, s32[27]{0:T(128)S(1)}, bf16[27,64,128]{2,1,0:T(8,128)(2,1)}, /*inde...) while((s32[]{:T(128)}, f32[64,1664]{1,0:T(8,128)S(1)}, ...), condition=%wide.region_3.4_spmd.clone, body=%wide.region_2.3_spmd.clone.sunk | while | flops 133160960 | bytes 1380533 | solution.py:148
  380.5 4.6 collective-permute-start.4
  397.2 6.0 %all-to-all-start.1 = ((bf16[8,16,64,128]{3,2,1,0:T(8,128)(2,1)}), bf16[8,16,64,128]{3,2,1,0:T(8,128)(2,1)S(1)}, u32[]{:S(2)}, u32[]{:S(2)}) async-start(bf16[8,16,64,128]{3,2,1,0:T(8,128)(2,1)} %bitcast.199), calls=%async_computation.1 | async-start | bytes 4194304 | tf_op jit(solution)/shard_map/all_to_all | solution.py:21
  404.7 102.6 %all-reduce.3.cloned.1.call-done = f32[27,64,128]{2,1,0:T(8,128)} async-done(((f32[27,64,128]{2,1,0:T(8,128)}), f32[27,64,128]{2,1,0:T(8,128)}) %all-reduce.3.cloned.1.call-update) | async-done | bytes 884752 | tf_op jit(solution)/shard_map/psum | solution.py:177
  507.3 2.2 broadcast_multiply_fusion
  (331 shorter events, 177.7 us)
Async XLA Ops:
  7.2 14.3 %copy-start = (bf16[27,128,128]{2,1,0:T(8,128)(2,1)S(1)}, bf16[27,128,128]{2,1,0:T(8,128)(2,1)}, u32[]{:S(2)}) copy-start(bf16[27,128,128]{2,1,0:T(8,128)(2,1)} %param.20) | copy-start | bytes 2654212
  8.0 4.1 copy-start.15
  12.1 7.5 %copy-start.17 = (s32[1,8,16]{2,1,0:T(8,128)S(1)}, s32[1,8,16]{2,1,0:T(8,128)}, u32[]{:S(2)}) copy-start(s32[1,8,16]{2,1,0:T(8,128)} %param.15) | copy-start | bytes 1540
  12.1 8.1 %copy-start.3 = (s32[1,4,2]{1,2,0:T(2,128)S(1)}, s32[1,4,2]{1,2,0:T(2,128)}, u32[]{:S(2)}) copy-start(s32[1,4,2]{1,2,0:T(2,128)} %param.16) | copy-start | bytes 100
  12.1 55.6 %all-to-all-start = ((bf16[8,16,64,128]{3,2,1,0:T(8,128)(2,1)}), bf16[8,16,64,128]{3,2,1,0:T(8,128)(2,1)S(1)}, u32[]{:S(2)}, u32[]{:S(2)}) async-start(bf16[8,16,64,128]{3,2,1,0:T(8,128)(2,1)} %bitcast.197), calls=%async_computation | async-start | bytes 4194304 | tf_op jit(solution)/shard_map/all_to_all | solution.py:21
  19.5 4.1 copy-start.4
  19.5 4.1 copy-start.5
  19.5 4.0 copy-start.18
  20.4 0.6 copy-start.9
  20.4 0.6 copy-start.11
  21.0 0.5 copy-start.7
  21.0 46.8 %copy-start.13 = (s32[2]{0:T(128)}, s32[2]{0:T(128)S(1)}, u32[]{:S(2)}) copy-start(s32[2]{0:T(128)S(1)} %get-tuple-element.202) | copy-start | bytes 28
  70.1 9.0 %collective-permute-start = (bf16[1,2,64,128]{3,2,1,0:T(8,128)(2,1)S(1)}, bf16[1,2,64,128]{3,2,1,0:T(8,128)(2,1)S(1)}, u32[]{:S(2)}, u32[]{:S(2)}) collective-permute-start(bf16[1,2,64,128]{3,2,1,0:T(8,128)(2,1)S(1)} %bitcast.207), channel_id=1, source_target_pairs={{0,4},{4,8},{8,12},{1,5},{5,9},{9,13},{2,6},{6,10},{10,14},{3,7},{... | collective-permute-start | bytes 98312 | tf_op jit(solution)/shard_map/ppermute | solution.py:14
  72.2 7.0 %collective-permute-start.1 = (bf16[1,2,64,128]{3,2,1,0:T(8,128)(2,1)S(1)}, bf16[1,2,64,128]{3,2,1,0:T(8,128)(2,1)S(1)}, u32[]{:S(2)}, u32[]{:S(2)}) collective-permute-start(bf16[1,2,64,128]{3,2,1,0:T(8,128)(2,1)S(1)} %bitcast.209), channel_id=1, source_target_pairs={{4,0},{8,4},{12,8},{5,1},{9,5},{13,9},{6,2},{10,6},{14,10},{7,3},{... | collective-permute-start | bytes 98312 | tf_op jit(solution)/shard_map/ppermute | solution.py:15
  74.0 5.1 collective-permute-start.2
  77.8 5.8 %collective-permute-start.3 = (bf16[1,2,64,128]{3,2,1,0:T(8,128)(2,1)S(1)}, bf16[1,2,64,128]{3,2,1,0:T(8,128)(2,1)S(1)}, u32[]{:S(2)}, u32[]{:S(2)}) collective-permute-start(bf16[1,2,64,128]{3,2,1,0:T(8,128)(2,1)S(1)} %bitcast.206), channel_id=1, source_target_pairs={{2,0},{3,1},{6,4},{7,5},{10,8},{11,9},{14,12},{15,13},{18,16},{19,... | collective-permute-start | bytes 98312 | tf_op jit(solution)/shard_map/ppermute | solution.py:15
  85.8 135.9 %copy-start.1 = (bf16[1,4,64,128]{3,2,1,0:T(8,128)(2,1)S(1)}, bf16[1,4,64,128]{3,2,1,0:T(8,128)(2,1)}, u32[]{:S(2)}) copy-start(bf16[1,4,64,128]{3,2,1,0:T(8,128)(2,1)} %param.21) | copy-start | bytes 196612
  221.1 0.6 copy-start.2
  380.4 10.6 %copy-start.12 = (s32[2]{0:T(128)S(1)}, s32[2]{0:T(128)}, u32[]{:S(2)}) copy-start(s32[2]{0:T(128)} %copy-done.11) | copy-start | bytes 28
  380.4 11.2 %copy-start.10 = (s32[2]{0:T(128)S(1)}, s32[2]{0:T(128)}, u32[]{:S(2)}) copy-start(s32[2]{0:T(128)} %copy-done.9) | copy-start | bytes 28
  380.4 11.8 %copy-start.14 = (s32[2]{0:T(128)S(1)}, s32[2]{0:T(128)}, u32[]{:S(2)}) copy-start(s32[2]{0:T(128)} %copy-done.13) | copy-start | bytes 28
  380.4 13.4 %copy-start.8 = (s32[2]{0:T(128)S(1)}, s32[2]{0:T(128)}, u32[]{:S(2)}) copy-start(s32[2]{0:T(128)} %copy-done.7) | copy-start | bytes 28
  380.4 14.1 %copy-start.6 = (s32[128]{0:T(128)S(1)}, s32[128]{0:T(128)}, u32[]{:S(2)}) copy-start(s32[128]{0:T(128)} %eq.91) | copy-start | bytes 1540
  380.5 8.8 %collective-permute-start.4 = (bf16[1,2,64,128]{3,2,1,0:T(8,128)(2,1)S(1)}, bf16[1,2,64,128]{3,2,1,0:T(8,128)(2,1)S(1)}, u32[]{:S(2)}, u32[]{:S(2)}) collective-permute-start(bf16[1,2,64,128]{3,2,1,0:T(8,128)(2,1)S(1)} %get-tuple-element.194), channel_id=1, source_target_pairs={{0,4},{4,8},{8,12},{1,5},{5,9},{9,13},{2,6},{6,10},{10,14},{3,7},{... | collective-permute-start | bytes 98312 | tf_op jit(solution)/shard_map/ppermute | solution.py:14
  385.1 5.8 %collective-permute-start.5 = (bf16[1,2,64,128]{3,2,1,0:T(8,128)(2,1)S(1)}, bf16[1,2,64,128]{3,2,1,0:T(8,128)(2,1)S(1)}, u32[]{:S(2)}, u32[]{:S(2)}) collective-permute-start(bf16[1,2,64,128]{3,2,1,0:T(8,128)(2,1)S(1)} %get-tuple-element.193), channel_id=1, source_target_pairs={{4,0},{8,4},{12,8},{5,1},{9,5},{13,9},{6,2},{10,6},{14,10},{7,3},{... | collective-permute-start | bytes 98312 | tf_op jit(solution)/shard_map/ppermute | solution.py:15
  386.4 4.5 collective-permute-start.6
  388.0 5.8 %collective-permute-start.7 = (bf16[1,2,64,128]{3,2,1,0:T(8,128)(2,1)S(1)}, bf16[1,2,64,128]{3,2,1,0:T(8,128)(2,1)S(1)}, u32[]{:S(2)}, u32[]{:S(2)}) collective-permute-start(bf16[1,2,64,128]{3,2,1,0:T(8,128)(2,1)S(1)} %get-tuple-element.191), channel_id=1, source_target_pairs={{2,0},{3,1},{6,4},{7,5},{10,8},{11,9},{14,12},{15,13},{18,16},{19,... | collective-permute-start | bytes 98312 | tf_op jit(solution)/shard_map/ppermute | solution.py:15
  397.2 112.3 %all-to-all-start.1 = ((bf16[8,16,64,128]{3,2,1,0:T(8,128)(2,1)}), bf16[8,16,64,128]{3,2,1,0:T(8,128)(2,1)S(1)}, u32[]{:S(2)}, u32[]{:S(2)}) async-start(bf16[8,16,64,128]{3,2,1,0:T(8,128)(2,1)} %bitcast.199), calls=%async_computation.1 | async-start | bytes 4194304 | tf_op jit(solution)/shard_map/all_to_all | solution.py:21
  403.2 106.3 %copy-start.16 = (s32[128]{0:T(128)S(1)}, s32[128]{0:T(128)}, u32[]{:S(2)}) copy-start(s32[128]{0:T(128)} %copy-done.15) | copy-start | bytes 1540
  403.2 104.1 %all-reduce.3.cloned.1.call-start = ((), (), s32[]{:S(2)}) async-start(), calls=%async_computation.2 | async-start | bytes 1769472 | tf_op jit(solution)/shard_map/psum | solution.py:177
Sparse Core Ops, SparseCore 0:
  408.1 99.1 all-reduce.2
where the time goes:
time: 524 us; the launch traced here: 519 us
  waiting for transfers between devices  154 us (29%)
  matrix products  136 us (26%)
  loops' own time  109 us (21%)
  local copies, waits for them, and re-layouts  66.3 us (13%)
  starting transfers between devices  29.4 us (6%)
  between operations  14.5 us (3%)
  other arithmetic  5.84 us (1%)
    psum x1, waiting for transfers between devices, local(): weight_total = lax.psum(weight_terms, ('tile', 'depth'))  103 us
    another operation x1, loops' own time, apply_offsets(): lax.scan(forward, start_total, jnp.arange(kernel.shape[0], dtype=jnp.int32))  55.5 us
    another operation x1, loops' own time, local(): lax.scan(backward, grad_start, jnp.arange(offsets, dtype=jnp.int32))  53.3 us
    dot_general x27, matrix products, forward(): lax.dot_general(kernel[offset], placed, (((0,), (0,)), ((), ())), preferr...  53.1 us
    all_to_all x2, waiting for transfers between devices, relay(): lax.all_to_all(outgoing, ('tile', 'depth'), split_axis=0, concat_axis=0,...  44.1 us
    dynamic_slice x54, local copies, waits for them, and re-layouts, apply_offsets(): lax.scan(forward, start_total, jnp.arange(kernel.shape[0], dtype=jnp.int32))  33.5 us
    dot_general x27, matrix products, backward(): jnp.dot(w_rows[offset], spread, preferred_element_type=jnp.float32)  33.4 us
    dot_general x27, matrix products, backward(): lax.dot_general(columns, grad_columns, (((1,), (1,)), ((), ())), preferre...  28 us
  transfers between devices with their start and end apart: 11, of which 5 were waited for; matrix products, arithmetic and copies ran while one was open for 2% of the time, Pallas kernels for 0%

commit v1 on v0

v1 whole, which is shorter than its diff:
```python
import functools

import jax
import jax.numpy as jnp
from jax import lax
from jax.experimental import pallas as pl
from jax.experimental.pallas import tpu as pltpu
from jax.sharding import PartitionSpec as P

F32 = jnp.float32
BF16 = jnp.bfloat16
TILES_AXES = ("tile", "depth")
VMEM = pl.BlockSpec(memory_space=pltpu.VMEM)
SMEM = pl.BlockSpec(memory_space=pltpu.SMEM)
PARAMS = pltpu.CompilerParams(vmem_limit_bytes=24 * 1024 * 1024)


def shape(dims, dtype):
    return jax.ShapeDtypeStruct(dims, dtype)


def pair_lists(size):
    return [
        [pair for i in range(first, size - 1, 2) for pair in ((i, i + 1), (i + 1, i))]
        for first in (0, 1)
    ]


def exchanges(tile_rows, depths):
    found = []
    for axis, size in (("tile", tile_rows), ("depth", depths)):
        for parity, pairs in enumerate(pair_lists(size)):
            if pairs:
                found.append((axis, parity, pairs))
    return found


def direction(axis, parity):
    place = lax.axis_index(axis) % 2
    upper = (place == parity).astype(jnp.int32)
    return upper + (0 if axis == "tile" else 2)


def xor_pairs(size, distance):
    return [(i, i ^ distance) for i in range(size)]


def premerge_kernel(tile_rows, depths, tile_blocks, *refs):
    send_ref, own_ref = refs[0], refs[1]
    near = refs[2 : 2 + tile_rows - 1]
    far = refs[2 + tile_rows - 1 : 2 + tile_rows - 1 + depths - 1]
    log_ref, out_ref, place_ref = refs[-3:]
    log_count, half, width = log_ref.shape
    capacity = send_ref.shape[1]
    i, j = lax.axis_index("tile"), lax.axis_index("depth")
    me = i * depths + j
    for jx in range(depths):
        for d in range(tile_rows):
            p = (i ^ d) * depths + (j ^ jx)
            q = jx * tile_rows + d
            totals = [jnp.zeros((half, width), F32) for _ in range(tile_blocks)]
            for c in range(capacity):
                block = send_ref[p, c]
                if jx:
                    target = far[jx - 1][d, me, c]
                elif d:
                    target = near[d - 1][me, c]
                else:
                    target = own_ref[me, c]
                live = block >= 0
                place_ref[jnp.where(live, block, log_count)] = q * tile_blocks + target
                rows = log_ref[jnp.maximum(block, 0)].astype(F32)
                wanted = jnp.where(live, target, -1)
                for m in range(tile_blocks):
                    totals[m] = totals[m] + rows * jnp.where(wanted == m, 1.0, 0.0)
            for m in range(tile_blocks):
                out_ref[p * tile_blocks + m] = totals[m].astype(BF16)


def merge_kernel(swaps, incoming_ref, halo_ref, features_ref, *sends):
    sources, tile_blocks = incoming_ref.shape[:2]
    for m in range(tile_blocks):
        total = incoming_ref[0, m].astype(F32)
        for s in range(1, sources):
            total = total + incoming_ref[s, m].astype(F32)
        features_ref[m] = total.astype(BF16)
    pick_blocks(swaps, features_ref, halo_ref, sends)


def pick_blocks(swaps, features_ref, halo_ref, sends):
    for (axis, parity, _), send_ref in zip(swaps, sends):
        group = direction(axis, parity)
        for b in range(send_ref.shape[0]):
            send_ref[b] = features_ref[halo_ref[group, b]]


def table_row(ref, k):
    return ref[k : k + 1, :]


def one_hot(low, height):
    rows = lax.broadcasted_iota(jnp.int32, (height, low.shape[1]), 0)
    return jnp.where(rows == low, 1.0, 0.0).astype(BF16)


def forward_kernel(swap_count, chunk, *refs):
    features_ref = refs[0]
    received = refs[1 : 1 + swap_count]
    source_ref, target_ref, weight_ref = refs[1 + swap_count : 4 + swap_count]
    part_ref, columns_ref, values, places = refs[4 + swap_count :]
    tile_blocks, half, width = features_ref.shape
    offsets = weight_ref.shape[0]
    channels = weight_ref.shape[1]
    span = 2 * width
    blocks = [features_ref[b] for b in range(tile_blocks)]
    for ref in received:
        blocks += [ref[b] for b in range(ref.shape[0])]
    folds = len(blocks) // 2
    folded = jnp.concatenate(
        [jnp.concatenate([blocks[2 * f], blocks[2 * f + 1]], 1) for f in range(folds)], 0
    )
    for first in range(0, offsets, chunk):
        ks = range(first, first + chunk)
        rows = [table_row(source_ref, k) for k in ks]
        table = jnp.concatenate([one_hot(r & (span - 1), span) for r in rows], 1)
        gathered = jnp.dot(folded, table, preferred_element_type=F32)
        for n, k in enumerate(ks):
            lanes = slice(n * width, (n + 1) * width)
            fold = rows[n] // span
            picked = jnp.zeros((half, width), F32)
            for f in range(folds):
                picked = jnp.where(fold == f, gathered[f * half : (f + 1) * half, lanes], picked)
            picked = picked.astype(BF16)
            columns_ref[:, k * width : (k + 1) * width] = picked
            product = jnp.dot(weight_ref[k], picked, preferred_element_type=F32)
            target = table_row(target_ref, k)
            fold = target // span
            places[:, k * width : (k + 1) * width] = one_hot(target & (span - 1), span)
            for f in range(2):
                values[f * channels : (f + 1) * channels, k * width : (k + 1) * width] = jnp.where(
                    fold == f, product, 0.0
                ).astype(BF16)
    total = lax.dot_general(
        values[...], places[...], (((1,), (1,)), ((), ())), preferred_element_type=F32
    )
    part_ref[:, :span] = total[:channels]
    part_ref[:, span:] = total[channels:]


def activation_kernel(chunk, *refs):
    part_ref, other_ref, cotangent_ref, target_ref, columns_ref = refs[:5]
    act_ref, weight_grad_ref, grad_columns_ref = refs[5:]
    tile_blocks, channels, width = cotangent_ref.shape
    half = columns_ref.shape[0]
    offsets = weight_grad_ref.shape[0] // half
    span = 2 * width
    start = pl.multiple_of(lax.axis_index("chan") * half, half)
    own = part_ref[pl.ds(start, half), :] + other_ref[pl.ds(start, half), :]
    own = own / (1.0 + jnp.exp(-own))
    for b in range(tile_blocks):
        act_ref[b] = own[:, b * width : (b + 1) * width].astype(BF16)
    preact = part_ref[...] + other_ref[...]
    gate = 1.0 / (1.0 + jnp.exp(-preact))
    cotangent = jnp.concatenate([cotangent_ref[b] for b in range(tile_blocks)], 1).astype(F32)
    grad = (cotangent * gate * (1.0 + preact * (1.0 - gate))).astype(BF16)
    folded = jnp.concatenate([grad[:, :span], grad[:, span:]], 0)
    for first in range(0, offsets, chunk):
        ks = range(first, first + chunk)
        rows = [table_row(target_ref, k) for k in ks]
        table = jnp.concatenate([one_hot(r & (span - 1), span) for r in rows], 1)
        gathered = jnp.dot(folded, table, preferred_element_type=F32)
        for n, k in enumerate(ks):
            lanes = slice(n * width, (n + 1) * width)
            fold = rows[n] // span
            picked = jnp.where(
                fold == 0,
                gathered[:channels, lanes],
                jnp.where(fold == 1, gathered[channels:, lanes], 0.0),
            ).astype(BF16)
            grad_columns_ref[:, k * width : (k + 1) * width] = picked
            term = lax.dot_general(
                columns_ref[:, k * width : (k + 1) * width],
                picked,
                (((1,), (1,)), ((), ())),
                preferred_element_type=F32,
            )
            weight_grad_ref[k * half : (k + 1) * half, :] = term.astype(weight_grad_ref.dtype)


def input_grad_kernel(tile_blocks, grad_columns_ref, source_ref, weight_ref, own_ref, *refs):
    rims, (values, places) = refs[:-2], refs[-2:]
    offsets, half, _ = weight_ref.shape
    width = source_ref.shape[1]
    span = 2 * width
    folds = values.shape[0] // half
    for k in range(offsets):
        lanes = slice(k * width, (k + 1) * width)
        source = table_row(source_ref, k)
        fold = source // span
        returned = jnp.dot(weight_ref[k], grad_columns_ref[:, lanes], preferred_element_type=F32)
        places[:, lanes] = one_hot(source & (span - 1), span)
        for f in range(folds):
            values[f * half : (f + 1) * half, lanes] = jnp.where(fold == f, returned, 0.0).astype(
                BF16
            )
    total = lax.dot_general(
        values[...], places[...], (((1,), (1,)), ((), ())), preferred_element_type=F32
    )

    def block(b):
        return total[(b // 2) * half : (b // 2 + 1) * half, (b % 2) * width : (b % 2 + 1) * width]

    for b in range(tile_blocks):
        own_ref[b] = block(b)
    place = tile_blocks
    for rim in rims:
        for b in range(rim.shape[0]):
            rim[b] = block(place).astype(BF16)
            place += 1


def tile_grad_kernel(swaps, own_ref, halo_ref, *refs):
    received, (out_ref, total) = refs[:-2], refs[-2:]
    total[...] = own_ref[...]
    for (axis, parity, _), ref in zip(swaps, received):
        group = direction(axis, parity)
        for b in range(ref.shape[0]):
            where = halo_ref[group, b]
            total[where] = total[where] + ref[b].astype(F32)
    out_ref[...] = total[...].astype(BF16)


def spread_kernel(place_ref, *refs):
    parts, (out_ref, held) = refs[:-2], refs[-2:]
    first = 0
    for ref in parts:
        count = ref.shape[0]
        held[first : first + count] = ref[...]
        first += count
    for b in range(out_ref.shape[0]):
        out_ref[b] = held[place_ref[b]]


def weight_kernel(tile_rows, depths, scale, *refs):
    parts, (out_ref, held) = refs[:-2], refs[-2:]
    i, j = lax.axis_index("tile"), lax.axis_index("depth")
    rows = parts[0].shape[0]
    for jx in range(depths):
        for d in range(tile_rows):
            p = (i ^ d) * depths + (j ^ jx)
            start = pl.multiple_of(p * rows, rows)
            held[pl.ds(start, rows), :] = parts[jx * tile_rows + d][...].astype(F32) * scale
    out_ref[...] = held[: out_ref.shape[0], :]


def swap_all(swaps, arrays):
    return [
        lax.ppermute(array, axis, pairs) for (axis, _, pairs), array in zip(swaps, arrays)
    ]


def share(own, tile_rows, depths):
    near = [own] + [
        lax.ppermute(own, "tile", xor_pairs(tile_rows, d)) for d in range(1, tile_rows)
    ]
    found = list(near)
    for jx in range(1, depths):
        found += [lax.ppermute(part, "depth", xor_pairs(depths, jx)) for part in near]
    return found


def relay(outgoing):
    return lax.all_to_all(outgoing, TILES_AXES, split_axis=0, concat_axis=0, tiled=True)


def local(
    log_features, send_slot, merge_slot, halo_list, in_rows, out_rows, pair_count, weight, cotangent
):
    tile_rows = lax.axis_size("tile")
    depths = lax.axis_size("depth")
    tile_count = tile_rows * depths
    log_blocks = log_features[0]
    log_count, half, width = log_blocks.shape
    tile_blocks = cotangent.shape[1]
    offsets, channels, _ = weight.shape
    capacity = send_slot.shape[2]
    rim_count = halo_list.shape[2]
    pair_slots = in_rows.shape[2]
    own_total = tile_blocks * width
    span = 2 * width
    chunk = 4
    padded = -(-offsets // chunk) * chunk
    swaps = exchanges(tile_rows, depths)
    powers = all(n & (n - 1) == 0 for n in (tile_rows, depths))
    merged = powers and tile_count <= 8 and capacity >= tile_blocks
    send, merge, halo = send_slot[0], merge_slot[0], halo_list[0]

    block_of = in_rows[0] // width
    group_of = (block_of - tile_blocks) // rim_count
    held_total = tile_blocks + len(swaps) * rim_count
    new_block = jnp.where(block_of < tile_blocks, block_of, held_total)
    for place, (axis, parity, _) in enumerate(swaps):
        hit = (block_of >= tile_blocks) & (group_of == direction(axis, parity))
        inside = (block_of - tile_blocks) % rim_count
        new_block = jnp.where(hit, tile_blocks + place * rim_count + inside, new_block)
    live = jnp.arange(pair_slots, dtype=jnp.int32)[None, :] < pair_count[0][:, None]
    source_rows = jnp.where(live, new_block * width + in_rows[0] % width, held_total * width)
    target_rows = jnp.where(live, out_rows[0], own_total)
    extra = ((0, padded - offsets), (0, 0))
    source_rows = jnp.pad(source_rows, extra, constant_values=held_total * width)
    target_rows = jnp.pad(target_rows, extra, constant_values=own_total)
    w_rows = lax.dynamic_slice_in_dim(weight, lax.axis_index("chan") * half, half, 1)
    w_rows = jnp.pad(w_rows, ((0, padded - offsets), (0, 0), (0, 0)))
    w_rows_t = w_rows.transpose(0, 2, 1)
    cotangent_full = lax.all_gather(cotangent[0], "chan", axis=1, tiled=True)

    rim_shape = shape((rim_count, half, width), BF16)
    block_shape = shape((tile_blocks, half, width), BF16)
    if merged:
        near = [merge] + [
            lax.ppermute(merge, "tile", xor_pairs(tile_rows, d)) for d in range(1, tile_rows)
        ]
        stacked = jnp.stack(near)
        far = [
            lax.ppermute(stacked, "depth", xor_pairs(depths, jx)) for jx in range(1, depths)
        ]
        outgoing, place = pl.pallas_call(
            functools.partial(premerge_kernel, tile_rows, depths, tile_blocks),
            out_shape=(
                shape((tile_count * tile_blocks, half, width), BF16),
                shape((log_count + 1,), jnp.int32),
            ),
            in_specs=[SMEM] * (1 + len(near) + len(far)) + [VMEM],
            out_specs=(VMEM, SMEM),
            compiler_params=PARAMS,
        )(send, *near, *far, log_blocks)
        incoming = relay(outgoing.reshape(tile_count, tile_blocks, half, width))
    else:
        pick_table = (
            send.reshape(-1)[:, None] == jnp.arange(log_count, dtype=jnp.int32)[None, :]
        ).astype(BF16)
        outgoing = jnp.dot(
            pick_table, log_blocks.reshape(log_count, half * width), preferred_element_type=F32
        ).astype(BF16)
        incoming = relay(outgoing.reshape(tile_count, capacity, half, width))
        place_table = (
            jnp.arange(tile_blocks, dtype=jnp.int32)[:, None] == merge.reshape(-1)[None, :]
        ).astype(BF16)
        incoming = jnp.dot(
            place_table,
            incoming.reshape(tile_count * capacity, half * width),
            preferred_element_type=F32,
        )
        incoming = incoming.astype(BF16).reshape(1, tile_blocks, half, width)
    features, *sends = pl.pallas_call(
        functools.partial(merge_kernel, swaps),
        out_shape=(block_shape,) + (rim_shape,) * len(swaps),
        in_specs=[VMEM, SMEM],
        out_specs=(VMEM,) * (1 + len(swaps)),
        compiler_params=PARAMS,
    )(incoming, halo)
    received = swap_all(swaps, sends)

    pairs_total = padded * pair_slots
    part, columns = pl.pallas_call(
        functools.partial(forward_kernel, len(swaps), chunk),
        out_shape=(shape((channels, own_total), F32), shape((half, pairs_total), BF16)),
        in_specs=[VMEM] * (4 + len(swaps)),
        out_specs=(VMEM, VMEM),
        scratch_shapes=[
            pltpu.VMEM((2 * channels, pairs_total), BF16),
            pltpu.VMEM((span, pairs_total), BF16),
        ],
        compiler_params=PARAMS,
    )(features, *received, source_rows, target_rows, w_rows_t)
    other = lax.ppermute(part, "chan", [(0, 1), (1, 0)])

    weight_type = BF16 if merged else F32
    activations, weight_terms, grad_columns = pl.pallas_call(
        functools.partial(activation_kernel, chunk),
        out_shape=(
            block_shape,
            shape((padded * half, channels), weight_type),
            shape((channels, pairs_total), BF16),
        ),
        in_specs=[VMEM] * 5,
        out_specs=(VMEM,) * 3,
        compiler_params=PARAMS,
    )(part, other, cotangent_full, target_rows, columns)

    scale = float(tile_count * pair_slots) ** (-0.5)
    if merged:
        shards = relay(weight_terms.reshape(tile_count, -1, channels))
    own_grad, *rims = pl.pallas_call(
        functools.partial(input_grad_kernel, tile_blocks),
        out_shape=(shape((tile_blocks, half, width), F32),) + (rim_shape,) * len(swaps),
        in_specs=[VMEM] * 3,
        out_specs=(VMEM,) * (1 + len(swaps)),
        scratch_shapes=[
            pltpu.VMEM((held_total // 2 * half, pairs_total), BF16),
            pltpu.VMEM((span, pairs_total), BF16),
        ],
        compiler_params=PARAMS,
    )(grad_columns, source_rows, w_rows)
    returned = swap_all(swaps, rims)
    tile_grad = pl.pallas_call(
        functools.partial(tile_grad_kernel, swaps),
        out_shape=block_shape,
        in_specs=[VMEM, SMEM] + [VMEM] * len(swaps),
        out_specs=VMEM,
        scratch_shapes=[pltpu.VMEM((tile_blocks, half, width), F32)],
        compiler_params=PARAMS,
    )(own_grad, halo, *returned)

    if merged:
        parts = share(tile_grad, tile_rows, depths)
        grad_log = pl.pallas_call(
            spread_kernel,
            out_shape=shape((log_count, half, width), BF16),
            in_specs=[SMEM] + [VMEM] * len(parts),
            out_specs=VMEM,
            scratch_shapes=[pltpu.VMEM((tile_count * tile_blocks, half, width), BF16)],
            compiler_params=PARAMS,
        )(place, *parts)
        shard = shards.astype(F32).sum(0).astype(BF16)
        shares = share(shard, tile_rows, depths)
        grad_weight = pl.pallas_call(
            functools.partial(weight_kernel, tile_rows, depths, scale),
            out_shape=shape((offsets * half, channels), F32),
            in_specs=[VMEM] * len(shares),
            out_specs=VMEM,
            scratch_shapes=[pltpu.VMEM((padded * half, channels), F32)],
            compiler_params=PARAMS,
        )(*shares)
    else:
        back_blocks = jnp.dot(
            place_table.T,
            tile_grad.reshape(tile_blocks, half * width),
            preferred_element_type=F32,
        ).astype(BF16)
        back = relay(back_blocks.reshape(tile_count, capacity, half, width))
        grad_log = jnp.dot(
            pick_table.T,
            back.reshape(tile_count * capacity, half * width),
            preferred_element_type=F32,
        ).astype(BF16)
        grad_weight = lax.psum(weight_terms[: offsets * half], TILES_AXES) * scale
    return (
        activations[None],
        grad_log.reshape(1, log_count, half, width),
        grad_weight.reshape(offsets, half, channels),
    )


def solution(mesh):
    split = ("groups", "tile", "depth")
    in_specs = (
        P(split, None, "chan", None),
        P(split, None, None),
        P(split, None, None),
        P(split, None, None),
        P(split, None, None),
        P(split, None, None),
        P(split, None),
        P(),
        P(split, None, "chan", None),
    )
    out_specs = (
        P(split, None, "chan", None),
        P(split, None, "chan", None),
        P("groups", "chan", None),
    )
    return jax.shard_map(local, mesh=mesh, in_specs=in_specs, out_specs=out_specs, check_vma=False)
```

time: 524 us -> 92.9 us (0.18)
  matrix products: 136 us -> 0 us
  waiting for transfers between devices: 154 us -> 25.2 us
  loops' own time: 109 us -> 0 us
  local copies, waits for them, and re-layouts: 66.3 us -> 3.3 us
  starting transfers between devices: 29.4 us -> 45.9 us
  Pallas kernels: 0 us -> 15.2 us
  between operations: 14.5 us -> 0.8 us
  other arithmetic: 5.84 us -> 0.14 us
    dot_general x139 -> x0, matrix products: 136 us -> none  [the longest x27 53.1 us: forward(): lax.dot_general(kernel[offset], placed, (((0,), (0,)), ((), ())), preferr...]
    another operation x2 -> x0, loops' own time: 109 us -> none  [the longest x1 55.5 us: apply_offsets(): lax.scan(forward, start_total, jnp.arange(kernel.shape[0], dtype=jnp.int32))]
    psum x1 -> x0, waiting for transfers between devices: 103 us -> none  [local(): weight_total = lax.psum(weight_terms, ('tile', 'depth'))]
    dynamic_slice x56 -> x1, local copies, waits for them, and re-layouts: 35.5 us -> 0.03 us  [local(): lax.dynamic_slice_in_dim(weight, lax.axis_index('chan') * half, half, 1)]
    all_to_all x2, waiting for transfers between devices: 44.1 us -> 10.2 us  [relay(): lax.all_to_all(outgoing, TILES_AXES, split_axis=0, concat_axis=0, tiled=T...]
    eq x56 -> x0, local copies, waits for them, and re-layouts: 20.6 us -> none  [the longest x54 19.2 us: select_table(): jnp.arange(row_total, dtype=jnp.int32)[:, None] == row_ids[None, :]]
    ppermute x8 -> x25, starting transfers between devices: 16 us -> 35.5 us  [the longest x6 13.5 us: share(): lax.ppermute(own, 'tile', xor_pairs(tile_rows, d))]
    pallas_call x0 -> x8, Pallas kernels: none -> 15.2 us  [the longest x1 3.4 us: local(): pl.pallas_call(functools.partial(forward_kernel, len(swaps), chunk), out_...]
  transfers between devices with their start and end apart: 11 -> 27, of which waited for: 5 -> 10; matrix products, arithmetic and copies ran while one was open for 2% -> 1% of each run, Pallas kernels for 0% -> 4%
where the time goes in v1:
time: 92.9 us; the launch traced here: 92.5 us
  starting transfers between devices  45.9 us (49%)
  waiting for transfers between devices  25.2 us (27%)
  Pallas kernels  15.2 us (16%)
  local copies, waits for them, and re-layouts  3.3 us (4%)
  blocking collectives  2.03 us (2%)
    ppermute x6, starting transfers between devices, share(): lax.ppermute(own, 'tile', xor_pairs(tile_rows, d))  13.5 us
    all_to_all x2, starting transfers between devices, relay(): lax.all_to_all(outgoing, TILES_AXES, split_axis=0, concat_axis=0, tiled=T...  10.4 us
    all_to_all x2, waiting for transfers between devices, relay(): lax.all_to_all(outgoing, TILES_AXES, split_axis=0, concat_axis=0, tiled=T...  10.2 us
    ppermute x8, starting transfers between devices, share(): lax.ppermute(part, 'depth', xor_pairs(depths, jx))  8.11 us
    ppermute x6, starting transfers between devices, swap_all(): lax.ppermute(array, axis, pairs)  6.48 us
    ppermute x3, starting transfers between devices, local(): lax.ppermute(merge, 'tile', xor_pairs(tile_rows, d))  5.76 us
    ppermute x6, waiting for transfers between devices, swap_all(): lax.ppermute(array, axis, pairs)  5.54 us
    ppermute x3, waiting for transfers between devices, local(): lax.ppermute(merge, 'tile', xor_pairs(tile_rows, d))  4.08 us
  transfers between devices with their start and end apart: 27, of which 10 were waited for; matrix products, arithmetic and copies ran while one was open for 1% of the time, Pallas kernels for 4%

profile of v1, /device:TPU:0, one launch (start us, length us, event | category | flops | bytes accessed | tf_op | source)
XLA Modules:
  0.0 92.5 jit_solution(11173774771864979061)
XLA Ops:
  0.7 5.1 %collective-permute-start.2 = (s32[8,16]{1,0:T(8,128)}, s32[8,16]{1,0:T(8,128)S(1)}, u32[]{:S(2)}, u32[]{:S(2)}) collective-permute-start(s32[8,16]{1,0:T(8,128)} %bitcast.38), channel_id=1, source_target_pairs={{0,12},{4,8},{8,4},{12,0},{1,13},{5,9},{9,5},{13,1},{2,14},{6,10},... | collective-permute-start | bytes 1544 | tf_op jit(solution)/shard_map/ppermute | solution.py:321
  6.4 1.2 %collective-permute-done.2.refs_4_ = s32[8,16]{1,0:T(8,128)S(1)} collective-permute-done((s32[8,16]{1,0:T(8,128)}, s32[8,16]{1,0:T(8,128)S(1)}, u32[]{:S(2)}, u32[]{:S(2)}) %collective-permute-start.2) | collective-permute-done | bytes 544 | tf_op jit(solution)/shard_map/ppermute | solution.py:321
  7.6 2.9 %collective-permute-done.1.refs_3_ = s32[8,16]{1,0:T(8,128)S(1)} collective-permute-done((s32[8,16]{1,0:T(8,128)}, s32[8,16]{1,0:T(8,128)S(1)}, u32[]{:S(2)}, u32[]{:S(2)}) %collective-permute-start.1) | collective-permute-done | bytes 544 | tf_op jit(solution)/shard_map/ppermute | solution.py:321
  10.5 1.6 %collective-permute-start.3 = (s32[4,8,16]{2,1,0:T(8,128)S(1)}, s32[4,8,16]{2,1,0:T(8,128)S(1)}, u32[]{:S(2)}, u32[]{:S(2)}) collective-permute-start(s32[4,8,16]{2,1,0:T(8,128)S(1)} %pad_add_fusion), channel_id=1, source_target_pairs={{0,2},{2,0},{1,3},{3,1},{4,6},{6,4},{5,7},{7,5},{8,10},{10,8},{9,1... | collective-permute-start | bytes 6152 | tf_op jit(solution)/shard_map/ppermute | solution.py:325
  12.1 2.2 %collective-permute-done.3.refs_5_ = s32[4,8,16]{2,1,0:T(8,128)S(1)} collective-permute-done((s32[4,8,16]{2,1,0:T(8,128)S(1)}, s32[4,8,16]{2,1,0:T(8,128)S(1)}, u32[]{:S(2)}, u32[]{:S(2)}) %collective-permute-start.3) | collective-permute-done | bytes 2080 | tf_op jit(solution)/shard_map/ppermute | solution.py:325
  14.3 1.2 %copy-done.1 = bf16[1,64,64,128]{3,2,1,0:T(8,128)(2,1)S(1)} copy-done((bf16[1,64,64,128]{3,2,1,0:T(8,128)(2,1)S(1)}, bf16[1,64,64,128]{3,2,1,0:T(8,128)(2,1)}, u32[]{:S(2)}) %copy-start.1) | copy-done | bytes 1048600
  15.5 3.3 %shard_map.112 = (bf16[32,64,128]{2,1,0:T(8,128)(2,1)}, s32[65]{0:T(128)S(1)}) custom-call(s32[8,16]{1,0:T(8,128)S(1)} %bitcast.45, s32[8,16]{1,0:T(8,128)S(1)} %bitcast.41, s32[8,16]{1,0:T(8,128)S(1)} %collective-permute-done.refs_2_, s32[8,16]{1,0:T(8,128)S(1)} %collective-permute-done.1.refs_3_, s32[8,16]{1,0:T(8,128)S(1)} %collective-permute-done.2.refs_4_, ...), custom_call_target="tpu_custom_call" | custom-call | tf_op jit(solution)/shard_map/pallas_call | solution.py:327
  18.9 4.2 %all-to-all-start = ((bf16[8,4,64,128]{3,2,1,0:T(8,128)(2,1)}), bf16[8,4,64,128]{3,2,1,0:T(8,128)(2,1)S(1)}, u32[]{:S(2)}, u32[]{:S(2)}) async-start(bf16[8,4,64,128]{3,2,1,0:T(8,128)(2,1)} %bitcast.6), calls=%async_computation | async-start | bytes 1048576 | tf_op jit(solution)/shard_map/all_to_all | solution.py:273
  24.7 10.2 %all-to-all-done.incoming_ref = bf16[8,4,64,128]{3,2,1,0:T(8,128)(2,1)S(1)} async-done(((bf16[8,4,64,128]{3,2,1,0:T(8,128)(2,1)}), bf16[8,4,64,128]{3,2,1,0:T(8,128)(2,1)S(1)}, u32[]{:S(2)}, u32[]{:S(2)}) %all-to-all-start) | async-done | bytes 524320 | tf_op jit(solution)/shard_map/all_to_all | solution.py:273
  38.4 1.2 %collective-permute-done.4.refs_1_ = bf16[2,64,128]{2,1,0:T(8,128)(2,1)S(1)} collective-permute-done((bf16[2,64,128]{2,1,0:T(8,128)(2,1)S(1)}, bf16[2,64,128]{2,1,0:T(8,128)(2,1)S(1)}, u32[]{:S(2)}, u32[]{:S(2)}) %collective-permute-start.4) | collective-permute-done | bytes 32800 | tf_op jit(solution)/shard_map/ppermute | solution.py:258
  39.5 1.4 %collective-permute-done.6.refs_3_ = bf16[2,64,128]{2,1,0:T(8,128)(2,1)S(1)} collective-permute-done((bf16[2,64,128]{2,1,0:T(8,128)(2,1)S(1)}, bf16[2,64,128]{2,1,0:T(8,128)(2,1)S(1)}, u32[]{:S(2)}, u32[]{:S(2)}) %collective-permute-start.6) | collective-permute-done | bytes 32800 | tf_op jit(solution)/shard_map/ppermute | solution.py:258
  41.0 3.4 %shard_map.114 = (f32[128,512]{1,0:T(8,128)S(1)}, bf16[64,3584]{1,0:T(8,128)(2,1)S(1)}) custom-call(bf16[4,64,128]{2,1,0:T(8,128)(2,1)S(1)} %get-tuple-element.19.refs_0_, bf16[2,64,128]{2,1,0:T(8,128)(2,1)S(1)} %collective-permute-done.4.refs_1_, bf16[2,64,128]{2,1,0:T(8,128)(2,1)S(1)} %collective-permute-done.5.refs_2_, ...), custom_call_target="tpu_custom_call" | custom-call | tf_op jit(solution)/shard_map/pallas_call | solution.py:365
  44.5 2.0 %all-gather = bf16[1,4,128,128]{3,2,1,0:T(8,128)(2,1)S(1)} all-gather(bf16[1,4,64,128]{3,2,1,0:T(8,128)(2,1)S(1)} %copy-done.4), channel_id=2, replica_groups=mesh['groups'=2,'tile'=4,'depth'=2,'chan'=2] {'chan'}, dimensions={2}, use_global_device_ids=true | all-gather | bytes 196608 | tf_op jit(solution)/shard_map/all_gather | solution.py:315
  46.5 3.0 %shard_map.115 = (bf16[4,64,128]{2,1,0:T(8,128)(2,1)}, bf16[1792,128]{1,0:T(8,128)(2,1)}, bf16[128,3584]{1,0:T(8,128)(2,1)S(1)}) custom-call(f32[128,512]{1,0:T(8,128)S(1)} %get-tuple-element.23.refs_0_, f32[128,512]{1,0:T(8,128)S(1)} %collective-permute-done.7.refs_1_, bf16[4,128,128]{2,1,0:T(8,128)(2,1)S(1)} %bitcast.37, ...), custom_call_target="tpu_custom_call" | custom-call | tf_op jit(solution)/shard_map/pallas_call | solution.py:379
  49.5 6.1 %all-to-all-start.1 = ((bf16[8,224,128]{2,1,0:T(8,128)(2,1)}), bf16[8,224,128]{2,1,0:T(8,128)(2,1)S(1)}, u32[]{:S(2)}, u32[]{:S(2)}) async-start(bf16[8,224,128]{2,1,0:T(8,128)(2,1)} %bitcast.13), calls=%async_computation.1 | async-start | bytes 917504 | tf_op jit(solution)/shard_map/all_to_all | solution.py:273
  55.6 1.5 %shard_map.116 = (f32[4,64,128]{2,1,0:T(8,128)S(1)}, bf16[2,64,128]{2,1,0:T(8,128)(2,1)S(1)}, bf16[2,64,128]{2,1,0:T(8,128)(2,1)S(1)}, bf16[2,64,128]{2,1,0:T(8,128)(2,1)S(1)}) custom-call(bf16[128,3584]{1,0:T(8,128)(2,1)S(1)} %get-tuple-element.27.grad_columns_ref, s32[28,128]{1,0:T(8,128)S(1)} %pad.11.refs_4_.source_ref, ...), custom_call_target="tpu_custom_call" | custom-call | tf_op jit(solution)/shard_map/pallas_call | solution.py:394
  57.1 2.1 %collective-permute-start.8 = (bf16[2,64,128]{2,1,0:T(8,128)(2,1)S(1)}, bf16[2,64,128]{2,1,0:T(8,128)(2,1)S(1)}, u32[]{:S(2)}, u32[]{:S(2)}) collective-permute-start(bf16[2,64,128]{2,1,0:T(8,128)(2,1)S(1)} %get-tuple-element.29), channel_id=1, source_target_pairs={{0,4},{4,0},{8,12},{12,8},{1,5},{5,1},{9,13},{13,9},{2,6},{6,2},{1... | collective-permute-start | bytes 98312 | tf_op jit(solution)/shard_map/ppermute | solution.py:258
  59.9 1.5 %collective-permute-start.10 = (bf16[2,64,128]{2,1,0:T(8,128)(2,1)S(1)}, bf16[2,64,128]{2,1,0:T(8,128)(2,1)S(1)}, u32[]{:S(2)}, u32[]{:S(2)}) collective-permute-start(bf16[2,64,128]{2,1,0:T(8,128)(2,1)S(1)} %get-tuple-element.31), channel_id=1, source_target_pairs={{0,2},{2,0},{1,3},{3,1},{4,6},{6,4},{5,7},{7,5},{8,10},{10,8},{9,1... | collective-permute-start | bytes 98312 | tf_op jit(solution)/shard_map/ppermute | solution.py:258
  61.4 2.9 %collective-permute-done.8.refs_0_ = bf16[2,64,128]{2,1,0:T(8,128)(2,1)S(1)} collective-permute-done((bf16[2,64,128]{2,1,0:T(8,128)(2,1)S(1)}, bf16[2,64,128]{2,1,0:T(8,128)(2,1)S(1)}, u32[]{:S(2)}, u32[]{:S(2)}) %collective-permute-start.8) | collective-permute-done | bytes 32800 | tf_op jit(solution)/shard_map/ppermute | solution.py:258
  65.0 3.6 %collective-permute-start.13 = (bf16[4,64,128]{2,1,0:T(8,128)(2,1)S(1)}, bf16[4,64,128]{2,1,0:T(8,128)(2,1)S(1)}, u32[]{:S(2)}, u32[]{:S(2)}) collective-permute-start(bf16[4,64,128]{2,1,0:T(8,128)(2,1)S(1)} %shard_map.117.refs_0_), channel_id=1, source_target_pairs={{0,12},{4,8},{8,4},{12,0},{1,13},{5,9},{9,5},{13,1},{2,14},{6,10},... | collective-permute-start | bytes 196616 | tf_op jit(solution)/shard_map/ppermute | solution.py:264
  68.6 5.4 %collective-permute-start.12 = (bf16[4,64,128]{2,1,0:T(8,128)(2,1)S(1)}, bf16[4,64,128]{2,1,0:T(8,128)(2,1)S(1)}, u32[]{:S(2)}, u32[]{:S(2)}) collective-permute-start(bf16[4,64,128]{2,1,0:T(8,128)(2,1)S(1)} %shard_map.117.refs_0_), channel_id=1, source_target_pairs={{0,8},{4,12},{8,0},{12,4},{1,9},{5,13},{9,1},{13,5},{2,10},{6,14},... | collective-permute-start | bytes 196616 | tf_op jit(solution)/shard_map/ppermute | solution.py:264
  74.8 1.3 %collective-permute-start.17 = (bf16[4,64,128]{2,1,0:T(8,128)(2,1)S(1)}, bf16[4,64,128]{2,1,0:T(8,128)(2,1)S(1)}, u32[]{:S(2)}, u32[]{:S(2)}) collective-permute-start(bf16[4,64,128]{2,1,0:T(8,128)(2,1)S(1)} %collective-permute-done.13.refs_3_), channel_id=1, source_target_pairs={{0,2},{2,0},{1,3},{3,1},{4,6},{6,4},{5,7},{7,5},{8,10},{10,8},{9,1... | collective-permute-start | bytes 196616 | tf_op jit(solution)/shard_map/ppermute | solution.py:268
  76.1 1.6 %collective-permute-done.12.refs_2_ = bf16[4,64,128]{2,1,0:T(8,128)(2,1)S(1)} collective-permute-done((bf16[4,64,128]{2,1,0:T(8,128)(2,1)S(1)}, bf16[4,64,128]{2,1,0:T(8,128)(2,1)S(1)}, u32[]{:S(2)}, u32[]{:S(2)}) %collective-permute-start.12) | collective-permute-done | bytes 65568 | tf_op jit(solution)/shard_map/ppermute | solution.py:264
  78.8 1.0 %collective-permute-start.20 = (bf16[224,128]{1,0:T(8,128)(2,1)S(1)}, bf16[224,128]{1,0:T(8,128)(2,1)S(1)}, u32[]{:S(2)}, u32[]{:S(2)}) collective-permute-start(bf16[224,128]{1,0:T(8,128)(2,1)S(1)} %reduce_sum.12.refs_0_), channel_id=1, source_target_pairs={{0,12},{4,8},{8,4},{12,0},{1,13},{5,9},{9,5},{13,1},{2,14},{6,10},... | collective-permute-start | bytes 172040 | tf_op jit(solution)/shard_map/ppermute | solution.py:264
  80.5 2.7 %collective-permute-start.18 = (bf16[224,128]{1,0:T(8,128)(2,1)S(1)}, bf16[224,128]{1,0:T(8,128)(2,1)S(1)}, u32[]{:S(2)}, u32[]{:S(2)}) collective-permute-start(bf16[224,128]{1,0:T(8,128)(2,1)S(1)} %reduce_sum.12.refs_0_), channel_id=1, source_target_pairs={{0,4},{4,0},{8,12},{12,8},{1,5},{5,1},{9,13},{13,9},{2,6},{6,2},{1... | collective-permute-start | bytes 172040 | tf_op jit(solution)/shard_map/ppermute | solution.py:264
  83.2 1.0 %collective-permute-start.15 = (bf16[4,64,128]{2,1,0:T(8,128)(2,1)S(1)}, bf16[4,64,128]{2,1,0:T(8,128)(2,1)S(1)}, u32[]{:S(2)}, u32[]{:S(2)}) collective-permute-start(bf16[4,64,128]{2,1,0:T(8,128)(2,1)S(1)} %collective-permute-done.11.refs_1_), channel_id=1, source_target_pairs={{0,2},{2,0},{1,3},{3,1},{4,6},{6,4},{5,7},{7,5},{8,10},{10,8},{9,1... | collective-permute-start | bytes 196616 | tf_op jit(solution)/shard_map/ppermute | solution.py:268
  84.2 1.0 %collective-permute-start.21 = (bf16[224,128]{1,0:T(8,128)(2,1)S(1)}, bf16[224,128]{1,0:T(8,128)(2,1)S(1)}, u32[]{:S(2)}, u32[]{:S(2)}) collective-permute-start(bf16[224,128]{1,0:T(8,128)(2,1)S(1)} %reduce_sum.12.refs_0_), channel_id=1, source_target_pairs={{0,2},{2,0},{1,3},{3,1},{4,6},{6,4},{5,7},{7,5},{8,10},{10,8},{9,1... | collective-permute-start | bytes 172040 | tf_op jit(solution)/shard_map/ppermute | solution.py:268
  85.2 1.0 %collective-permute-start.24 = (bf16[224,128]{1,0:T(8,128)(2,1)S(1)}, bf16[224,128]{1,0:T(8,128)(2,1)S(1)}, u32[]{:S(2)}, u32[]{:S(2)}) collective-permute-start(bf16[224,128]{1,0:T(8,128)(2,1)S(1)} %collective-permute-done.20.refs_3_), channel_id=1, source_target_pairs={{0,2},{2,0},{1,3},{3,1},{4,6},{6,4},{5,7},{7,5},{8,10},{10,8},{9,1... | collective-permute-start | bytes 172040 | tf_op jit(solution)/shard_map/ppermute | solution.py:268
  87.3 1.0 %collective-permute-start.22 = (bf16[224,128]{1,0:T(8,128)(2,1)S(1)}, bf16[224,128]{1,0:T(8,128)(2,1)S(1)}, u32[]{:S(2)}, u32[]{:S(2)}) collective-permute-start(bf16[224,128]{1,0:T(8,128)(2,1)S(1)} %collective-permute-done.18.refs_1_), channel_id=1, source_target_pairs={{0,2},{2,0},{1,3},{3,1},{4,6},{6,4},{5,7},{7,5},{8,10},{10,8},{9,1... | collective-permute-start | bytes 172040 | tf_op jit(solution)/shard_map/ppermute | solution.py:268
  88.3 1.6 %shard_map.118 = bf16[64,64,128]{2,1,0:T(8,128)(2,1)} custom-call(s32[65]{0:T(128)S(1)} %get-tuple-element.26.place_ref, bf16[4,64,128]{2,1,0:T(8,128)(2,1)S(1)} %shard_map.117.refs_0_, bf16[4,64,128]{2,1,0:T(8,128)(2,1)S(1)} %collective-permute-done.11.refs_1_, bf16[4,64,128]{2,1,0:T(8,128)(2,1)S(1)} %collective-permute-done.12.refs_2_, ...), custom_call_target="tpu_custom_call" | custom-call | tf_op jit(solution)/shard_map/pallas_call | solution.py:417
  90.5 1.0 %collective-permute-done.22.refs_5_ = bf16[224,128]{1,0:T(8,128)(2,1)S(1)} collective-permute-done((bf16[224,128]{1,0:T(8,128)(2,1)S(1)}, bf16[224,128]{1,0:T(8,128)(2,1)S(1)}, u32[]{:S(2)}, u32[]{:S(2)}) %collective-permute-start.22) | collective-permute-done | bytes 57376 | tf_op jit(solution)/shard_map/ppermute | solution.py:268
  91.5 1.0 %shard_map.119 = f32[1728,128]{1,0:T(8,128)} custom-call(bf16[224,128]{1,0:T(8,128)(2,1)S(1)} %reduce_sum.12.refs_0_, bf16[224,128]{1,0:T(8,128)(2,1)S(1)} %collective-permute-done.18.refs_1_, bf16[224,128]{1,0:T(8,128)(2,1)S(1)} %collective-permute-done.19.refs_2_, bf16[224,128]{1,0:T(8,128)(2,1)S(1)} %collective-permute-done.20.refs_3_, ...), custom_call_target="tpu_custom_call" | custom-call | tf_op jit(solution)/shard_map/pallas_call | solution.py:427
  (58 shorter events, 11.1 us)
Async XLA Ops:
  0.6 23.3 %copy-start = (bf16[27,128,128]{2,1,0:T(8,128)(2,1)S(1)}, bf16[27,128,128]{2,1,0:T(8,128)(2,1)}, u32[]{:S(2)}) copy-start(bf16[27,128,128]{2,1,0:T(8,128)(2,1)} %param.16) | copy-start | bytes 2654212
  0.6 9.8 %copy-start.2 = (s32[1,8,16]{2,1,0:T(8,128)S(1)}, s32[1,8,16]{2,1,0:T(8,128)}, u32[]{:S(2)}) copy-start(s32[1,8,16]{2,1,0:T(8,128)} %param.11) | copy-start | bytes 1540
  0.7 6.9 %collective-permute-start.2 = (s32[8,16]{1,0:T(8,128)}, s32[8,16]{1,0:T(8,128)S(1)}, u32[]{:S(2)}, u32[]{:S(2)}) collective-permute-start(s32[8,16]{1,0:T(8,128)} %bitcast.38), channel_id=1, source_target_pairs={{0,12},{4,8},{8,4},{12,0},{1,13},{5,9},{9,5},{13,1},{2,14},{6,10},... | collective-permute-start | bytes 1544 | tf_op jit(solution)/shard_map/ppermute | solution.py:321
  5.8 4.7 %collective-permute-start.1 = (s32[8,16]{1,0:T(8,128)}, s32[8,16]{1,0:T(8,128)S(1)}, u32[]{:S(2)}, u32[]{:S(2)}) collective-permute-start(s32[8,16]{1,0:T(8,128)} %bitcast.39), channel_id=1, source_target_pairs={{0,8},{4,12},{8,0},{12,4},{1,9},{5,13},{9,1},{13,5},{2,10},{6,14},... | collective-permute-start | bytes 1544 | tf_op jit(solution)/shard_map/ppermute | solution.py:321
  5.8 4.7 %collective-permute-start = (s32[8,16]{1,0:T(8,128)}, s32[8,16]{1,0:T(8,128)S(1)}, u32[]{:S(2)}, u32[]{:S(2)}) collective-permute-start(s32[8,16]{1,0:T(8,128)} %bitcast.40), channel_id=1, source_target_pairs={{0,4},{4,0},{8,12},{12,8},{1,5},{5,1},{9,13},{13,9},{2,6},{6,2},{1... | collective-permute-start | bytes 1544 | tf_op jit(solution)/shard_map/ppermute | solution.py:321
  10.5 3.8 %copy-start.3 = (s32[1,8,16]{2,1,0:T(8,128)S(1)}, s32[1,8,16]{2,1,0:T(8,128)}, u32[]{:S(2)}) copy-start(s32[1,8,16]{2,1,0:T(8,128)} %param.10) | copy-start | bytes 1540
  10.5 3.8 %collective-permute-start.3 = (s32[4,8,16]{2,1,0:T(8,128)S(1)}, s32[4,8,16]{2,1,0:T(8,128)S(1)}, u32[]{:S(2)}, u32[]{:S(2)}) collective-permute-start(s32[4,8,16]{2,1,0:T(8,128)S(1)} %pad_add_fusion), channel_id=1, source_target_pairs={{0,2},{2,0},{1,3},{3,1},{4,6},{6,4},{5,7},{7,5},{8,10},{10,8},{9,1... | collective-permute-start | bytes 6152 | tf_op jit(solution)/shard_map/ppermute | solution.py:325
  14.3 1.2 %copy-start.1 = (bf16[1,64,64,128]{3,2,1,0:T(8,128)(2,1)S(1)}, bf16[1,64,64,128]{3,2,1,0:T(8,128)(2,1)}, u32[]{:S(2)}) copy-start(bf16[1,64,64,128]{3,2,1,0:T(8,128)(2,1)} %param.9) | copy-start | bytes 3145732
  18.9 16.0 %all-to-all-start = ((bf16[8,4,64,128]{3,2,1,0:T(8,128)(2,1)}), bf16[8,4,64,128]{3,2,1,0:T(8,128)(2,1)S(1)}, u32[]{:S(2)}, u32[]{:S(2)}) async-start(bf16[8,4,64,128]{3,2,1,0:T(8,128)(2,1)} %bitcast.6), calls=%async_computation | async-start | bytes 1048576 | tf_op jit(solution)/shard_map/all_to_all | solution.py:273
  35.5 4.0 %collective-permute-start.4 = (bf16[2,64,128]{2,1,0:T(8,128)(2,1)S(1)}, bf16[2,64,128]{2,1,0:T(8,128)(2,1)S(1)}, u32[]{:S(2)}, u32[]{:S(2)}) collective-permute-start(bf16[2,64,128]{2,1,0:T(8,128)(2,1)S(1)} %get-tuple-element.20), channel_id=1, source_target_pairs={{0,4},{4,0},{8,12},{12,8},{1,5},{5,1},{9,13},{13,9},{2,6},{6,2},{1... | collective-permute-start | bytes 98312 | tf_op jit(solution)/shard_map/ppermute | solution.py:258
  36.3 3.2 %collective-permute-start.5 = (bf16[2,64,128]{2,1,0:T(8,128)(2,1)S(1)}, bf16[2,64,128]{2,1,0:T(8,128)(2,1)S(1)}, u32[]{:S(2)}, u32[]{:S(2)}) collective-permute-start(bf16[2,64,128]{2,1,0:T(8,128)(2,1)S(1)} %get-tuple-element.21), channel_id=1, source_target_pairs={{4,8},{8,4},{5,9},{9,5},{6,10},{10,6},{7,11},{11,7},{20,24},{24,20... | collective-permute-start | bytes 98312 | tf_op jit(solution)/shard_map/ppermute | solution.py:258
  37.0 4.0 %collective-permute-start.6 = (bf16[2,64,128]{2,1,0:T(8,128)(2,1)S(1)}, bf16[2,64,128]{2,1,0:T(8,128)(2,1)S(1)}, u32[]{:S(2)}, u32[]{:S(2)}) collective-permute-start(bf16[2,64,128]{2,1,0:T(8,128)(2,1)S(1)} %get-tuple-element.22), channel_id=1, source_target_pairs={{0,2},{2,0},{1,3},{3,1},{4,6},{6,4},{5,7},{7,5},{8,10},{10,8},{9,1... | collective-permute-start | bytes 98312 | tf_op jit(solution)/shard_map/ppermute | solution.py:258
  41.0 3.5 %copy-start.4 = (bf16[1,4,64,128]{3,2,1,0:T(8,128)(2,1)S(1)}, bf16[1,4,64,128]{3,2,1,0:T(8,128)(2,1)}, u32[]{:S(2)}) copy-start(bf16[1,4,64,128]{3,2,1,0:T(8,128)(2,1)} %param.17) | copy-start | bytes 196612
  44.4 2.1 %collective-permute-start.7 = (f32[128,512]{1,0:T(8,128)S(1)}, f32[128,512]{1,0:T(8,128)S(1)}, u32[]{:S(2)}, u32[]{:S(2)}) collective-permute-start(f32[128,512]{1,0:T(8,128)S(1)} %get-tuple-element.23.refs_0_), channel_id=1, source_target_pairs={{0,1},{1,0},{2,3},{3,2},{4,5},{5,4},{6,7},{7,6},{8,9},{9,8},{10,11... | collective-permute-start | bytes 786440 | tf_op jit(solution)/shard_map/ppermute | solution.py:376
  49.5 29.2 %all-to-all-start.1 = ((bf16[8,224,128]{2,1,0:T(8,128)(2,1)}), bf16[8,224,128]{2,1,0:T(8,128)(2,1)S(1)}, u32[]{:S(2)}, u32[]{:S(2)}) async-start(bf16[8,224,128]{2,1,0:T(8,128)(2,1)} %bitcast.13), calls=%async_computation.1 | async-start | bytes 917504 | tf_op jit(solution)/shard_map/all_to_all | solution.py:273
  57.1 7.2 %collective-permute-start.8 = (bf16[2,64,128]{2,1,0:T(8,128)(2,1)S(1)}, bf16[2,64,128]{2,1,0:T(8,128)(2,1)S(1)}, u32[]{:S(2)}, u32[]{:S(2)}) collective-permute-start(bf16[2,64,128]{2,1,0:T(8,128)(2,1)S(1)} %get-tuple-element.29), channel_id=1, source_target_pairs={{0,4},{4,0},{8,12},{12,8},{1,5},{5,1},{9,13},{13,9},{2,6},{6,2},{1... | collective-permute-start | bytes 98312 | tf_op jit(solution)/shard_map/ppermute | solution.py:258
  59.2 5.1 %collective-permute-start.9 = (bf16[2,64,128]{2,1,0:T(8,128)(2,1)S(1)}, bf16[2,64,128]{2,1,0:T(8,128)(2,1)S(1)}, u32[]{:S(2)}, u32[]{:S(2)}) collective-permute-start(bf16[2,64,128]{2,1,0:T(8,128)(2,1)S(1)} %get-tuple-element.30), channel_id=1, source_target_pairs={{4,8},{8,4},{5,9},{9,5},{6,10},{10,6},{7,11},{11,7},{20,24},{24,20... | collective-permute-start | bytes 98312 | tf_op jit(solution)/shard_map/ppermute | solution.py:258
  59.9 4.5 %collective-permute-start.10 = (bf16[2,64,128]{2,1,0:T(8,128)(2,1)S(1)}, bf16[2,64,128]{2,1,0:T(8,128)(2,1)S(1)}, u32[]{:S(2)}, u32[]{:S(2)}) collective-permute-start(bf16[2,64,128]{2,1,0:T(8,128)(2,1)S(1)} %get-tuple-element.31), channel_id=1, source_target_pairs={{0,2},{2,0},{1,3},{3,1},{4,6},{6,4},{5,7},{7,5},{8,10},{10,8},{9,1... | collective-permute-start | bytes 98312 | tf_op jit(solution)/shard_map/ppermute | solution.py:258
  65.0 9.8 %collective-permute-start.13 = (bf16[4,64,128]{2,1,0:T(8,128)(2,1)S(1)}, bf16[4,64,128]{2,1,0:T(8,128)(2,1)S(1)}, u32[]{:S(2)}, u32[]{:S(2)}) collective-permute-start(bf16[4,64,128]{2,1,0:T(8,128)(2,1)S(1)} %shard_map.117.refs_0_), channel_id=1, source_target_pairs={{0,12},{4,8},{8,4},{12,0},{1,13},{5,9},{9,5},{13,1},{2,14},{6,10},... | collective-permute-start | bytes 196616 | tf_op jit(solution)/shard_map/ppermute | solution.py:264
  68.6 9.1 %collective-permute-start.12 = (bf16[4,64,128]{2,1,0:T(8,128)(2,1)S(1)}, bf16[4,64,128]{2,1,0:T(8,128)(2,1)S(1)}, u32[]{:S(2)}, u32[]{:S(2)}) collective-permute-start(bf16[4,64,128]{2,1,0:T(8,128)(2,1)S(1)} %shard_map.117.refs_0_), channel_id=1, source_target_pairs={{0,8},{4,12},{8,0},{12,4},{1,9},{5,13},{9,1},{13,5},{2,10},{6,14},... | collective-permute-start | bytes 196616 | tf_op jit(solution)/shard_map/ppermute | solution.py:264
  74.0 5.8 %collective-permute-start.14 = (bf16[4,64,128]{2,1,0:T(8,128)(2,1)S(1)}, bf16[4,64,128]{2,1,0:T(8,128)(2,1)S(1)}, u32[]{:S(2)}, u32[]{:S(2)}) collective-permute-start(bf16[4,64,128]{2,1,0:T(8,128)(2,1)S(1)} %shard_map.117.refs_0_), channel_id=1, source_target_pairs={{0,2},{2,0},{1,3},{3,1},{4,6},{6,4},{5,7},{7,5},{8,10},{10,8},{9,1... | collective-permute-start | bytes 196616 | tf_op jit(solution)/shard_map/ppermute | solution.py:268
  74.8 5.7 %collective-permute-start.11 = (bf16[4,64,128]{2,1,0:T(8,128)(2,1)S(1)}, bf16[4,64,128]{2,1,0:T(8,128)(2,1)S(1)}, u32[]{:S(2)}, u32[]{:S(2)}) collective-permute-start(bf16[4,64,128]{2,1,0:T(8,128)(2,1)S(1)} %shard_map.117.refs_0_), channel_id=1, source_target_pairs={{0,4},{4,0},{8,12},{12,8},{1,5},{5,1},{9,13},{13,9},{2,6},{6,2},{1... | collective-permute-start | bytes 196616 | tf_op jit(solution)/shard_map/ppermute | solution.py:264
  74.8 8.4 %collective-permute-start.17 = (bf16[4,64,128]{2,1,0:T(8,128)(2,1)S(1)}, bf16[4,64,128]{2,1,0:T(8,128)(2,1)S(1)}, u32[]{:S(2)}, u32[]{:S(2)}) collective-permute-start(bf16[4,64,128]{2,1,0:T(8,128)(2,1)S(1)} %collective-permute-done.13.refs_3_), channel_id=1, source_target_pairs={{0,2},{2,0},{1,3},{3,1},{4,6},{6,4},{5,7},{7,5},{8,10},{10,8},{9,1... | collective-permute-start | bytes 196616 | tf_op jit(solution)/shard_map/ppermute | solution.py:268
  77.7 6.6 %collective-permute-start.16 = (bf16[4,64,128]{2,1,0:T(8,128)(2,1)S(1)}, bf16[4,64,128]{2,1,0:T(8,128)(2,1)S(1)}, u32[]{:S(2)}, u32[]{:S(2)}) collective-permute-start(bf16[4,64,128]{2,1,0:T(8,128)(2,1)S(1)} %collective-permute-done.12.refs_2_), channel_id=1, source_target_pairs={{0,2},{2,0},{1,3},{3,1},{4,6},{6,4},{5,7},{7,5},{8,10},{10,8},{9,1... | collective-permute-start | bytes 196616 | tf_op jit(solution)/shard_map/ppermute | solution.py:268
  78.8 6.5 %collective-permute-start.20 = (bf16[224,128]{1,0:T(8,128)(2,1)S(1)}, bf16[224,128]{1,0:T(8,128)(2,1)S(1)}, u32[]{:S(2)}, u32[]{:S(2)}) collective-permute-start(bf16[224,128]{1,0:T(8,128)(2,1)S(1)} %reduce_sum.12.refs_0_), channel_id=1, source_target_pairs={{0,12},{4,8},{8,4},{12,0},{1,13},{5,9},{9,5},{13,1},{2,14},{6,10},... | collective-permute-start | bytes 172040 | tf_op jit(solution)/shard_map/ppermute | solution.py:264
  79.8 6.5 %collective-permute-start.19 = (bf16[224,128]{1,0:T(8,128)(2,1)S(1)}, bf16[224,128]{1,0:T(8,128)(2,1)S(1)}, u32[]{:S(2)}, u32[]{:S(2)}) collective-permute-start(bf16[224,128]{1,0:T(8,128)(2,1)S(1)} %reduce_sum.12.refs_0_), channel_id=1, source_target_pairs={{0,8},{4,12},{8,0},{12,4},{1,9},{5,13},{9,1},{13,5},{2,10},{6,14},... | collective-permute-start | bytes 172040 | tf_op jit(solution)/shard_map/ppermute | solution.py:264
  80.5 6.8 %collective-permute-start.18 = (bf16[224,128]{1,0:T(8,128)(2,1)S(1)}, bf16[224,128]{1,0:T(8,128)(2,1)S(1)}, u32[]{:S(2)}, u32[]{:S(2)}) collective-permute-start(bf16[224,128]{1,0:T(8,128)(2,1)S(1)} %reduce_sum.12.refs_0_), channel_id=1, source_target_pairs={{0,4},{4,0},{8,12},{12,8},{1,5},{5,1},{9,13},{13,9},{2,6},{6,2},{1... | collective-permute-start | bytes 172040 | tf_op jit(solution)/shard_map/ppermute | solution.py:264
  83.2 5.1 %collective-permute-start.15 = (bf16[4,64,128]{2,1,0:T(8,128)(2,1)S(1)}, bf16[4,64,128]{2,1,0:T(8,128)(2,1)S(1)}, u32[]{:S(2)}, u32[]{:S(2)}) collective-permute-start(bf16[4,64,128]{2,1,0:T(8,128)(2,1)S(1)} %collective-permute-done.11.refs_1_), channel_id=1, source_target_pairs={{0,2},{2,0},{1,3},{3,1},{4,6},{6,4},{5,7},{7,5},{8,10},{10,8},{9,1... | collective-permute-start | bytes 196616 | tf_op jit(solution)/shard_map/ppermute | solution.py:268
  84.2 5.7 %collective-permute-start.21 = (bf16[224,128]{1,0:T(8,128)(2,1)S(1)}, bf16[224,128]{1,0:T(8,128)(2,1)S(1)}, u32[]{:S(2)}, u32[]{:S(2)}) collective-permute-start(bf16[224,128]{1,0:T(8,128)(2,1)S(1)} %reduce_sum.12.refs_0_), channel_id=1, source_target_pairs={{0,2},{2,0},{1,3},{3,1},{4,6},{6,4},{5,7},{7,5},{8,10},{10,8},{9,1... | collective-permute-start | bytes 172040 | tf_op jit(solution)/shard_map/ppermute | solution.py:268
  85.2 4.7 %collective-permute-start.24 = (bf16[224,128]{1,0:T(8,128)(2,1)S(1)}, bf16[224,128]{1,0:T(8,128)(2,1)S(1)}, u32[]{:S(2)}, u32[]{:S(2)}) collective-permute-start(bf16[224,128]{1,0:T(8,128)(2,1)S(1)} %collective-permute-done.20.refs_3_), channel_id=1, source_target_pairs={{0,2},{2,0},{1,3},{3,1},{4,6},{6,4},{5,7},{7,5},{8,10},{10,8},{9,1... | collective-permute-start | bytes 172040 | tf_op jit(solution)/shard_map/ppermute | solution.py:268
  86.3 4.2 %collective-permute-start.23 = (bf16[224,128]{1,0:T(8,128)(2,1)S(1)}, bf16[224,128]{1,0:T(8,128)(2,1)S(1)}, u32[]{:S(2)}, u32[]{:S(2)}) collective-permute-start(bf16[224,128]{1,0:T(8,128)(2,1)S(1)} %collective-permute-done.19.refs_2_), channel_id=1, source_target_pairs={{0,2},{2,0},{1,3},{3,1},{4,6},{6,4},{5,7},{7,5},{8,10},{10,8},{9,1... | collective-permute-start | bytes 172040 | tf_op jit(solution)/shard_map/ppermute | solution.py:268
  87.3 4.2 %collective-permute-start.22 = (bf16[224,128]{1,0:T(8,128)(2,1)S(1)}, bf16[224,128]{1,0:T(8,128)(2,1)S(1)}, u32[]{:S(2)}, u32[]{:S(2)}) collective-permute-start(bf16[224,128]{1,0:T(8,128)(2,1)S(1)} %collective-permute-done.18.refs_1_), channel_id=1, source_target_pairs={{0,2},{2,0},{1,3},{3,1},{4,6},{6,4},{5,7},{7,5},{8,10},{10,8},{9,1... | collective-permute-start | bytes 172040 | tf_op jit(solution)/shard_map/ppermute | solution.py:268
  (4 other events, 2.8 us)

commit v2 on v1

v2 whole, which is shorter than its diff:
```python
import functools

import jax
import jax.numpy as jnp
from jax import lax
from jax.experimental import pallas as pl
from jax.experimental.pallas import tpu as pltpu
from jax.sharding import PartitionSpec as P

F32 = jnp.float32
BF16 = jnp.bfloat16
TILES_AXES = ("tile", "depth")
VMEM = pl.BlockSpec(memory_space=pltpu.VMEM)
SMEM = pl.BlockSpec(memory_space=pltpu.SMEM)
PARAMS = pltpu.CompilerParams(vmem_limit_bytes=24 * 1024 * 1024)


def shape(dims, dtype):
    return jax.ShapeDtypeStruct(dims, dtype)


def pair_lists(size):
    return [
        [pair for i in range(first, size - 1, 2) for pair in ((i, i + 1), (i + 1, i))]
        for first in (0, 1)
    ]


def exchanges(tile_rows, depths):
    found = []
    for axis, size in (("tile", tile_rows), ("depth", depths)):
        for parity, pairs in enumerate(pair_lists(size)):
            if pairs:
                found.append((axis, parity, pairs))
    return found


def direction(axis, parity):
    place = lax.axis_index(axis) % 2
    upper = (place == parity).astype(jnp.int32)
    return upper + (0 if axis == "tile" else 2)


def xor_pairs(size, distance):
    return [(i, i ^ distance) for i in range(size)]


def merge_column(jx, rows_away, depths, tile_blocks, send_ref, tables, log_ref, emit):
    i, j = lax.axis_index("tile"), lax.axis_index("depth")
    me = i * depths + j
    half, width = log_ref.shape[1:]
    for d in rows_away:
        p = (i ^ d) * depths + (j ^ jx)
        totals = [jnp.zeros((half, width), F32) for _ in range(tile_blocks)]
        for c in range(send_ref.shape[1]):
            block = send_ref[p, c]
            wanted = jnp.where(block >= 0, tables(d, me, c), -1)
            rows = log_ref[jnp.maximum(block, 0)].astype(F32)
            for m in range(tile_blocks):
                totals[m] = totals[m] + rows * jnp.where(wanted == m, 1.0, 0.0)
        for m in range(tile_blocks):
            emit(d, m, totals[m])


def copy_kernel(in_ref, out_ref):
    out_ref[...] = in_ref[...]


def far_kernel(rows_away, depths, tile_blocks, send_ref, far_ref, log_ref, out_ref):
    def emit(d, m, total):
        out_ref[(d - rows_away[0]) * tile_blocks + m] = total.astype(BF16)

    merge_column(
        1, rows_away, depths, tile_blocks, send_ref, lambda *at: far_ref[at], log_ref, emit
    )


def near_kernel(tile_rows, depths, tile_blocks, *refs):
    send_ref, tables, far_ref = refs[0], refs[1 : 1 + tile_rows], refs[1 + tile_rows]
    log_ref, (*outs, place_ref) = refs[2 + tile_rows], refs[3 + tile_rows :]
    per = tile_rows // len(outs)
    i, j = lax.axis_index("tile"), lax.axis_index("depth")
    me = i * depths + j

    def emit(d, m, total):
        outs[d // per][(d % per) * tile_blocks + m] = total

    merge_column(
        0,
        range(tile_rows),
        depths,
        tile_blocks,
        send_ref,
        lambda d, *at: tables[d][at],
        log_ref,
        emit,
    )
    for jx in range(depths):
        for d in range(tile_rows):
            p = (i ^ d) * depths + (j ^ jx)
            for c in range(send_ref.shape[1]):
                block = send_ref[p, c]
                target = far_ref[d, me, c] if jx else tables[d][me, c]
                spot = jnp.where(block >= 0, block, log_ref.shape[0])
                place_ref[spot] = (jx * tile_rows + d) * tile_blocks + target


def add_kernel(near_ref, far_ref, *outs):
    count = near_ref.shape[0] // len(outs)
    for n, ref in enumerate(outs):
        for m in range(count):
            at = n * count + m
            ref[m] = (near_ref[at] + far_ref[at].astype(F32)).astype(ref.dtype)


def merge_kernel(swaps, halo_ref, *refs):
    incoming, features_ref = refs[: -1 - len(swaps)], refs[-1 - len(swaps)]
    sends = refs[-len(swaps) :] if swaps else ()
    for m in range(features_ref.shape[0]):
        total = incoming[0][m].astype(F32)
        for ref in incoming[1:]:
            total = total + ref[m].astype(F32)
        features_ref[m] = total.astype(BF16)
    pick_blocks(swaps, features_ref, halo_ref, sends)


def pick_blocks(swaps, features_ref, halo_ref, sends):
    for (axis, parity, _), send_ref in zip(swaps, sends):
        group = direction(axis, parity)
        for b in range(send_ref.shape[0]):
            send_ref[b] = features_ref[halo_ref[group, b]]


def table_row(ref, k):
    return ref[k : k + 1, :]


def one_hot(low, height):
    rows = lax.broadcasted_iota(jnp.int32, (height, low.shape[1]), 0).astype(F32).astype(BF16)
    low = low.astype(F32).astype(BF16)
    return jnp.where(rows == low, jnp.ones((), BF16), jnp.zeros((), BF16))


def pick_fold(fold, parts):
    picked = jnp.zeros_like(parts[0])
    for f, part in enumerate(parts):
        picked = jnp.where(fold == f, part, picked)
    return picked


def mask_fold(fold, f, part):
    return jnp.where(fold == f, part, jnp.zeros_like(part))


def forward_kernel(swap_count, chunk, *refs):
    features_ref = refs[0]
    received = refs[1 : 1 + swap_count]
    source_ref, target_ref, weight_ref = refs[1 + swap_count : 4 + swap_count]
    part_ref, columns_ref, values, places = refs[4 + swap_count :]
    tile_blocks, half, width = features_ref.shape
    offsets = weight_ref.shape[0]
    channels = weight_ref.shape[1]
    span = 2 * width
    blocks = [features_ref[b] for b in range(tile_blocks)]
    for ref in received:
        blocks += [ref[b] for b in range(ref.shape[0])]
    folds = len(blocks) // 2
    folded = jnp.concatenate(
        [jnp.concatenate([blocks[2 * f], blocks[2 * f + 1]], 1) for f in range(folds)], 0
    )
    for first in range(0, offsets, chunk):
        ks = range(first, first + chunk)
        rows = [table_row(source_ref, k) for k in ks]
        table = jnp.concatenate([one_hot(r & (span - 1), span) for r in rows], 1)
        gathered = jnp.dot(folded, table, preferred_element_type=F32).astype(BF16)
        for n, k in enumerate(ks):
            lanes = slice(n * width, (n + 1) * width)
            fold = (rows[n] // span).astype(F32).astype(BF16)
            picked = pick_fold(
                fold, [gathered[f * half : (f + 1) * half, lanes] for f in range(folds)]
            )
            columns_ref[:, k * width : (k + 1) * width] = picked
            product = jnp.dot(weight_ref[k], picked, preferred_element_type=F32)
            product = product.astype(BF16)
            target = table_row(target_ref, k)
            fold = (target // span).astype(F32).astype(BF16)
            places[:, k * width : (k + 1) * width] = one_hot(target & (span - 1), span)
            for f in range(2):
                values[f * channels : (f + 1) * channels, k * width : (k + 1) * width] = mask_fold(
                    fold, f, product
                )
    total = lax.dot_general(
        values[...], places[...], (((1,), (1,)), ((), ())), preferred_element_type=F32
    )
    part_ref[:, :span] = total[:channels]
    part_ref[:, span:] = total[channels:]


def input_grad_kernel(chunk, *refs):
    part_ref, other_ref, cotangent_ref, source_ref, target_ref, weight_ref = refs[:6]
    grad_columns_ref, own_ref = refs[6:8]
    rims, (values, places) = refs[8:-2], refs[-2:]
    tile_blocks, channels, width = cotangent_ref.shape
    offsets, half, _ = weight_ref.shape
    span = 2 * width
    folds = values.shape[0] // half
    preact = part_ref[...] + other_ref[...]
    gate = 1.0 / (1.0 + jnp.exp(-preact))
    cotangent = jnp.concatenate([cotangent_ref[b] for b in range(tile_blocks)], 1).astype(F32)
    grad = (cotangent * gate * (1.0 + preact * (1.0 - gate))).astype(BF16)
    folded = jnp.concatenate([grad[:, :span], grad[:, span:]], 0)
    for first in range(0, offsets, chunk):
        ks = range(first, first + chunk)
        rows = [table_row(target_ref, k) for k in ks]
        table = jnp.concatenate([one_hot(r & (span - 1), span) for r in rows], 1)
        gathered = jnp.dot(folded, table, preferred_element_type=F32).astype(BF16)
        for n, k in enumerate(ks):
            inside = slice(n * width, (n + 1) * width)
            lanes = slice(k * width, (k + 1) * width)
            fold = (rows[n] // span).astype(F32).astype(BF16)
            picked = pick_fold(fold, [gathered[:channels, inside], gathered[channels:, inside]])
            grad_columns_ref[:, lanes] = picked
            returned = jnp.dot(weight_ref[k], picked, preferred_element_type=F32).astype(BF16)
            source = table_row(source_ref, k)
            fold = (source // span).astype(F32).astype(BF16)
            places[:, lanes] = one_hot(source & (span - 1), span)
            for f in range(folds):
                values[f * half : (f + 1) * half, lanes] = mask_fold(fold, f, returned)
    total = lax.dot_general(
        values[...], places[...], (((1,), (1,)), ((), ())), preferred_element_type=F32
    )

    def block(b):
        return total[(b // 2) * half : (b // 2 + 1) * half, (b % 2) * width : (b % 2 + 1) * width]

    for b in range(tile_blocks):
        own_ref[b] = block(b)
    place = tile_blocks
    for rim in rims:
        for b in range(rim.shape[0]):
            rim[b] = block(place).astype(BF16)
            place += 1


def weight_grad_kernel(part_ref, other_ref, columns_ref, grad_columns_ref, act_ref, *refs):
    portions, held = refs[:-1], refs[-1]
    half = columns_ref.shape[0]
    tile_blocks, _, width = act_ref.shape
    offsets = columns_ref.shape[1] // width
    portion = offsets // len(portions)
    here = lax.axis_index("depth") if len(portions) > 1 else 0
    for k in range(offsets):
        lanes = slice(k * width, (k + 1) * width)
        term = lax.dot_general(
            columns_ref[:, lanes],
            grad_columns_ref[:, lanes],
            (((1,), (1,)), ((), ())),
            preferred_element_type=F32,
        )
        row = (k % portion) * half
        held[(k // portion) ^ here, row : row + half, :] = term
    for n, ref in enumerate(portions):
        ref[...] = held[n].astype(ref.dtype)
    start = pl.multiple_of(lax.axis_index("chan") * half, half)
    own = part_ref[pl.ds(start, half), :] + other_ref[pl.ds(start, half), :]
    own = own / (1.0 + jnp.exp(-own))
    for b in range(tile_blocks):
        act_ref[b] = own[:, b * width : (b + 1) * width].astype(BF16)


def tile_grad_kernel(swaps, halo_ref, own_ref, *refs):
    received, (out_ref, total) = refs[:-2], refs[-2:]
    total[...] = own_ref[...]
    for (axis, parity, _), ref in zip(swaps, received):
        group = direction(axis, parity)
        for b in range(ref.shape[0]):
            where = halo_ref[group, b]
            total[where] = total[where] + ref[b].astype(F32)
    out_ref[...] = total[...].astype(BF16)


def row_sum_kernel(keep_ref, crossed_ref, *refs):
    outs, total = refs[:-1], refs[-1]
    total[...] = keep_ref[...] + crossed_ref[...].astype(F32)
    i = lax.axis_index("tile")
    rows = outs[0].shape[0]
    for d, ref in enumerate(outs):
        start = pl.multiple_of((i ^ d) * rows, rows)
        ref[...] = total[pl.ds(start, rows), :].astype(ref.dtype)


def column_kernel(tile_rows, *refs):
    grads, terms, (bulk_ref, shard_ref) = refs[:tile_rows], refs[tile_rows:-2], refs[-2:]
    row = 0
    for ref in grads:
        for b in range(ref.shape[0]):
            bulk_ref[row : row + ref.shape[1], :] = ref[b]
            row += ref.shape[1]
    total = terms[0][...]
    for ref in terms[1:]:
        total = total + ref[...].astype(F32)
    shard_ref[...] = total.astype(BF16)
    bulk_ref[row:, :] = shard_ref[...]


def row_sum_kernel(keep_ref, crossed_ref, *refs):
    outs, total = refs[:-1], refs[-1]
    total[...] = keep_ref[...] + crossed_ref[...].astype(F32)
    i = lax.axis_index("tile")
    rows = outs[0].shape[0]
    for d, ref in enumerate(outs):
        start = pl.multiple_of((i ^ d) * rows, rows)
        ref[...] = total[pl.ds(start, rows), :].astype(ref.dtype)


def column_kernel(tile_rows, *refs):
    grads, terms, (bulk_ref, shard_ref) = refs[:tile_rows], refs[tile_rows:-2], refs[-2:]
    row = 0
    for ref in grads:
        for b in range(ref.shape[0]):
            bulk_ref[row : row + ref.shape[1], :] = ref[b]
            row += ref.shape[1]
    total = terms[0][...]
    for ref in terms[1:]:
        total = total + ref[...].astype(F32)
    shard_ref[...] = total.astype(BF16)
    bulk_ref[row:, :] = shard_ref[...]


def spread_kernel(place_ref, own_ref, other_ref, out_ref, held):
    rows = held.shape[0] // 2
    height = out_ref.shape[1]
    held[:rows, :] = own_ref[:rows, :]
    held[rows:, :] = other_ref[:rows, :]
    for b in range(out_ref.shape[0]):
        first = pl.multiple_of(place_ref[b] * height, height)
        out_ref[b] = held[pl.ds(first, height), :]


def weight_kernel(scale, tile_rows, *refs):
    near, (bulk_ref, far_ref, out_ref, held) = refs[:tile_rows], refs[tile_rows:]
    i, j = lax.axis_index("tile"), lax.axis_index("depth")
    rows = near[0].shape[0]
    for jx in range(2):
        for d in range(tile_rows):
            if jx == 0:
                shard = near[d][...]
            elif d == 0:
                shard = bulk_ref[bulk_ref.shape[0] - rows :, :]
            else:
                shard = far_ref[(d - 1) * rows : d * rows, :]
            start = pl.multiple_of(((j ^ jx) * tile_rows + (i ^ d)) * rows, rows)
            held[pl.ds(start, rows), :] = shard.astype(F32) * scale
    out_ref[...] = held[: out_ref.shape[0], :]


def swap_all(swaps, arrays):
    return [
        lax.ppermute(array, axis, pairs) for (axis, _, pairs), array in zip(swaps, arrays)
    ]


def to_rows(arrays, tile_rows):
    return [arrays[0]] + [
        lax.ppermute(arrays[d], "tile", xor_pairs(tile_rows, d)) for d in range(1, tile_rows)
    ]


def across(array):
    return lax.ppermute(array, "depth", [(0, 1), (1, 0)])


def relay(outgoing):
    return lax.all_to_all(outgoing, TILES_AXES, split_axis=0, concat_axis=0, tiled=True)


def local(
    log_features, send_slot, merge_slot, halo_list, in_rows, out_rows, pair_count, weight, cotangent
):
    tile_rows = lax.axis_size("tile")
    depths = lax.axis_size("depth")
    tile_count = tile_rows * depths
    log_blocks = log_features[0]
    log_count, half, width = log_blocks.shape
    tile_blocks = cotangent.shape[1]
    offsets, channels, _ = weight.shape
    capacity = send_slot.shape[2]
    rim_count = halo_list.shape[2]
    pair_slots = in_rows.shape[2]
    own_total = tile_blocks * width
    span = 2 * width
    chunk = 4
    padded = -(-offsets // chunk) * chunk
    swaps = exchanges(tile_rows, depths)
    merged = (tile_rows, depths) == (4, 2) and capacity >= tile_blocks
    send, merge, halo = send_slot[0], merge_slot[0], halo_list[0]

    block_of = in_rows[0] // width
    group_of = (block_of - tile_blocks) // rim_count
    held_total = tile_blocks + len(swaps) * rim_count
    new_block = jnp.where(block_of < tile_blocks, block_of, held_total)
    for place, (axis, parity, _) in enumerate(swaps):
        hit = (block_of >= tile_blocks) & (group_of == direction(axis, parity))
        inside = (block_of - tile_blocks) % rim_count
        new_block = jnp.where(hit, tile_blocks + place * rim_count + inside, new_block)
    live = jnp.arange(pair_slots, dtype=jnp.int32)[None, :] < pair_count[0][:, None]
    source_rows = jnp.where(live, new_block * width + in_rows[0] % width, held_total * width)
    target_rows = jnp.where(live, out_rows[0], own_total)
    extra = ((0, padded - offsets), (0, 0))
    source_rows = jnp.pad(source_rows, extra, constant_values=held_total * width)
    target_rows = jnp.pad(target_rows, extra, constant_values=own_total)
    w_rows = lax.dynamic_slice_in_dim(weight, lax.axis_index("chan") * half, half, 1)
    w_rows = jnp.pad(w_rows, ((0, padded - offsets), (0, 0), (0, 0)))
    w_rows_t = w_rows.transpose(0, 2, 1)
    cotangent_full = lax.all_gather(cotangent[0], "chan", axis=1, tiled=True)

    rim_shape = shape((rim_count, half, width), BF16)
    block_shape = shape((tile_blocks, half, width), BF16)
    if merged:
        near = to_rows([merge] * tile_rows, tile_rows)
        log_blocks = pl.pallas_call(
            copy_kernel,
            out_shape=shape(log_blocks.shape, BF16),
            in_specs=[VMEM],
            out_specs=VMEM,
            compiler_params=PARAMS,
        )(log_blocks)
        stacked, log_blocks = lax.optimization_barrier((jnp.stack(near), log_blocks))
        far = across(stacked)
        held_blocks = (tile_rows // 2 * tile_blocks, half, width)
        def far_sums(rows_away):
            return across(
                pl.pallas_call(
                    functools.partial(far_kernel, rows_away, depths, tile_blocks),
                    out_shape=shape(held_blocks, BF16),
                    in_specs=[SMEM] * 2 + [VMEM],
                    out_specs=VMEM,
                    compiler_params=PARAMS,
                )(send, far, log_blocks)
            )

        far_high = far_sums(range(tile_rows // 2, tile_rows))
        far_low = far_sums(range(tile_rows // 2))
        near_low, near_high, place = pl.pallas_call(
            functools.partial(near_kernel, tile_rows, depths, tile_blocks),
            out_shape=(shape(held_blocks, F32),) * 2 + (shape((log_count + 1,), jnp.int32),),
            in_specs=[SMEM] * (2 + tile_rows) + [VMEM],
            out_specs=(VMEM,) * 2 + (SMEM,),
            compiler_params=PARAMS,
        )(send, *near, far, log_blocks)
        add = functools.partial(
            pl.pallas_call,
            add_kernel,
            in_specs=[VMEM] * 2,
            out_specs=(VMEM,) * 2,
            compiler_params=PARAMS,
        )
        high = add(out_shape=(block_shape,) * 2)(near_high, far_high)
        low = add(out_shape=(shape((tile_blocks, half, width), F32), block_shape))(
            near_low, far_low
        )
        incoming = to_rows([*low, *high], tile_rows)
    else:
        pick_table = (
            send.reshape(-1)[:, None] == jnp.arange(log_count, dtype=jnp.int32)[None, :]
        ).astype(BF16)
        outgoing = jnp.dot(
            pick_table, log_blocks.reshape(log_count, half * width), preferred_element_type=F32
        ).astype(BF16)
        incoming = relay(outgoing.reshape(tile_count, capacity, half, width))
        place_table = (
            jnp.arange(tile_blocks, dtype=jnp.int32)[:, None] == merge.reshape(-1)[None, :]
        ).astype(BF16)
        incoming = jnp.dot(
            place_table,
            incoming.reshape(tile_count * capacity, half * width),
            preferred_element_type=F32,
        )
        incoming = [incoming.astype(BF16).reshape(tile_blocks, half, width)]
    features, *sends = pl.pallas_call(
        functools.partial(merge_kernel, swaps),
        out_shape=(block_shape,) + (rim_shape,) * len(swaps),
        in_specs=[SMEM] + [VMEM] * len(incoming),
        out_specs=(VMEM,) * (1 + len(swaps)),
        compiler_params=PARAMS,
    )(halo, *incoming)
    received = swap_all(swaps, sends)

    pairs_total = padded * pair_slots
    part, columns = pl.pallas_call(
        functools.partial(forward_kernel, len(swaps), chunk),
        out_shape=(shape((channels, own_total), F32), shape((half, pairs_total), BF16)),
        in_specs=[VMEM] * (4 + len(swaps)),
        out_specs=(VMEM, VMEM),
        scratch_shapes=[
            pltpu.VMEM((2 * channels, pairs_total), BF16),
            pltpu.VMEM((span, pairs_total), BF16),
        ],
        compiler_params=PARAMS,
    )(features, *received, source_rows, target_rows, w_rows_t)
    other = lax.ppermute(part, "chan", [(0, 1), (1, 0)])

    grad_columns, own_grad, *rims = pl.pallas_call(
        functools.partial(input_grad_kernel, chunk),
        out_shape=(
            shape((channels, pairs_total), BF16),
            shape((tile_blocks, half, width), F32),
        )
        + (rim_shape,) * len(swaps),
        in_specs=[VMEM] * 6,
        out_specs=(VMEM,) * (2 + len(swaps)),
        scratch_shapes=[
            pltpu.VMEM((held_total // 2 * half, pairs_total), BF16),
            pltpu.VMEM((span, pairs_total), BF16),
        ],
        compiler_params=PARAMS,
    )(part, other, cotangent_full, source_rows, target_rows, w_rows)
    returned = swap_all(swaps, rims)
    portions = depths if merged else 1
    portion = (padded // portions * half, channels)
    activations, keep, *cross = pl.pallas_call(
        weight_grad_kernel,
        out_shape=(block_shape, shape(portion, F32)) + (shape(portion, BF16),) * (portions - 1),
        in_specs=[VMEM] * 4,
        out_specs=(VMEM,) * (1 + portions),
        scratch_shapes=[pltpu.VMEM((portions, *portion), F32)],
        compiler_params=PARAMS,
    )(part, other, columns, grad_columns)
    scale = float(tile_count * pair_slots) ** (-0.5)
    if merged:
        cross, returned = lax.optimization_barrier((cross, returned))
    tile_grad = pl.pallas_call(
        functools.partial(tile_grad_kernel, swaps),
        out_shape=block_shape,
        in_specs=[SMEM] + [VMEM] * (1 + len(swaps)),
        out_specs=VMEM,
        scratch_shapes=[pltpu.VMEM((tile_blocks, half, width), F32)],
        compiler_params=PARAMS,
    )(halo, own_grad, *returned)

    if merged:
        rows = portion[0] // tile_rows
        row_terms = pl.pallas_call(
            row_sum_kernel,
            out_shape=(shape((rows, channels), F32),)
            + (shape((rows, channels), BF16),) * (tile_rows - 1),
            in_specs=[VMEM] * 2,
            out_specs=(VMEM,) * tile_rows,
            scratch_shapes=[pltpu.VMEM(portion, F32)],
            compiler_params=PARAMS,
        )(keep, across(cross[0]))
        column_rows = tile_rows * tile_blocks * half
        bulk, shard = pl.pallas_call(
            functools.partial(column_kernel, tile_rows),
            out_shape=(shape((column_rows + rows, channels), BF16), shape((rows, channels), BF16)),
            in_specs=[VMEM] * (2 * tile_rows),
            out_specs=(VMEM,) * 2,
            compiler_params=PARAMS,
        )(*to_rows([tile_grad] * tile_rows, tile_rows), *to_rows(row_terms, tile_rows))
        other_bulk = across(bulk)
        shards = to_rows([shard] * tile_rows, tile_rows)
        last, other_bulk = lax.optimization_barrier((jnp.concatenate(shards[1:]), other_bulk))
        grad_log = pl.pallas_call(
            spread_kernel,
            out_shape=shape((log_count, half, width), BF16),
            in_specs=[SMEM] + [VMEM] * 2,
            out_specs=VMEM,
            scratch_shapes=[pltpu.VMEM((2 * column_rows, width), BF16)],
            compiler_params=PARAMS,
        )(place, bulk, other_bulk)
        grad_weight = pl.pallas_call(
            functools.partial(weight_kernel, scale, tile_rows),
            out_shape=shape((offsets * half, channels), F32),
            in_specs=[VMEM] * (tile_rows + 2),
            out_specs=VMEM,
            scratch_shapes=[pltpu.VMEM((padded * half, channels), F32)],
            compiler_params=PARAMS,
        )(*shards, other_bulk, across(last))
    else:
        back_blocks = jnp.dot(
            place_table.T,
            tile_grad.reshape(tile_blocks, half * width),
            preferred_element_type=F32,
        ).astype(BF16)
        back = relay(back_blocks.reshape(tile_count, capacity, half, width))
        grad_log = jnp.dot(
            pick_table.T,
            back.reshape(tile_count * capacity, half * width),
            preferred_element_type=F32,
        ).astype(BF16)
        grad_weight = lax.psum(keep[: offsets * half], TILES_AXES) * scale
    return (
        activations[None],
        grad_log.reshape(1, log_count, half, width),
        grad_weight.reshape(offsets, half, channels),
    )


def solution(mesh):
    split = ("groups", "tile", "depth")
    in_specs = (
        P(split, None, "chan", None),
        P(split, None, None),
        P(split, None, None),
        P(split, None, None),
        P(split, None, None),
        P(split, None, None),
        P(split, None),
        P(),
        P(split, None, "chan", None),
    )
    out_specs = (
        P(split, None, "chan", None),
        P(split, None, "chan", None),
        P("groups", "chan", None),
    )
    return jax.shard_map(local, mesh=mesh, in_specs=in_specs, out_specs=out_specs, check_vma=False)
```

time: 92.9 us -> 85.4 us (0.919)
  starting transfers between devices: 45.9 us -> 39.4 us
  waiting for transfers between devices: 25.2 us -> 22.6 us
  Pallas kernels: 15.2 us -> 17.5 us
    all_to_all x2 -> x0, starting transfers between devices: 10.4 us -> none  [relay(): lax.all_to_all(outgoing, TILES_AXES, split_axis=0, concat_axis=0, tiled=T...]
    all_to_all x2 -> x0, waiting for transfers between devices: 10.2 us -> none  [relay(): lax.all_to_all(outgoing, TILES_AXES, split_axis=0, concat_axis=0, tiled=T...]
    ppermute x18 -> x21, waiting for transfers between devices: 9.49 us -> 19.4 us  [the longest x15 14.8 us: to_rows(): lax.ppermute(arrays[d], 'tile', xor_pairs(tile_rows, d))]
    pallas_call x4 -> x11, Pallas kernels: 8.87 us -> 11.2 us  [the longest x1 3.48 us: local(): pl.pallas_call(functools.partial(input_grad_kernel, chunk), out_shape=(sh...]
    ppermute x6, waiting for transfers between devices: 5.54 us -> 3.24 us  [swap_all(): lax.ppermute(array, axis, pairs)]
    ppermute x18 -> x21, starting transfers between devices: 28.9 us -> 31.2 us  [the longest x15 24 us: to_rows(): lax.ppermute(arrays[d], 'tile', xor_pairs(tile_rows, d))]
    ppermute x6, starting transfers between devices: 6.48 us -> 8.15 us  [swap_all(): lax.ppermute(array, axis, pairs)]
  transfers between devices with their start and end apart: 27 -> 28, of which waited for: 10 -> 16; matrix products, arithmetic and copies ran while one was open for 1% -> 1% of each run, Pallas kernels for 4% -> 9%
where the time goes in v2:
time: 85.4 us; the launch traced here: 85.2 us
  starting transfers between devices  39.4 us (46%)
  waiting for transfers between devices  22.6 us (26%)
  Pallas kernels  17.5 us (20%)
  local copies, waits for them, and re-layouts  2.67 us (3%)
  blocking collectives  2.03 us (2%)
  between operations  0.89 us (1%)
    ppermute x15, starting transfers between devices, to_rows(): lax.ppermute(arrays[d], 'tile', xor_pairs(tile_rows, d))  24 us
    ppermute x15, waiting for transfers between devices, to_rows(): lax.ppermute(arrays[d], 'tile', xor_pairs(tile_rows, d))  14.8 us
    ppermute x6, starting transfers between devices, swap_all(): lax.ppermute(array, axis, pairs)  8.15 us
    ppermute x6, starting transfers between devices, across(): return lax.ppermute(array, 'depth', [(0, 1), (1, 0)])  7.13 us
    ppermute x6, waiting for transfers between devices, across(): return lax.ppermute(array, 'depth', [(0, 1), (1, 0)])  4.56 us
    pallas_call x1, Pallas kernels, local(): pl.pallas_call(functools.partial(input_grad_kernel, chunk), out_shape=(sh...  3.48 us
    pallas_call x1, Pallas kernels, local(): pl.pallas_call(functools.partial(forward_kernel, len(swaps), chunk), out_...  3.42 us
    ppermute x6, waiting for transfers between devices, swap_all(): lax.ppermute(array, axis, pairs)  3.24 us
  transfers between devices with their start and end apart: 28, of which 16 were waited for; matrix products, arithmetic and copies ran while one was open for 1% of the time, Pallas kernels for 9%

profile of v2, /device:TPU:0, one launch (start us, length us, event | category | flops | bytes accessed | tf_op | source)
XLA Modules:
  0.0 85.2 jit_solution(13219986629182067739)
XLA Ops:
  0.6 3.1 %collective-permute-start = (s32[8,16]{1,0:T(8,128)}, s32[8,16]{1,0:T(8,128)S(1)}, u32[]{:S(2)}, u32[]{:S(2)}) collective-permute-start(s32[8,16]{1,0:T(8,128)} %bitcast.39), channel_id=1, source_target_pairs={{0,4},{4,0},{8,12},{12,8},{1,5},{5,1},{9,13},{13,9},{2,6},{6,2},{1... | collective-permute-start | bytes 1544 | tf_op jit(solution)/shard_map/ppermute | solution.py:365
  3.7 2.6 %collective-permute-start.1 = (s32[8,16]{1,0:T(8,128)}, s32[8,16]{1,0:T(8,128)S(1)}, u32[]{:S(2)}, u32[]{:S(2)}) collective-permute-start(s32[8,16]{1,0:T(8,128)} %bitcast.40), channel_id=1, source_target_pairs={{0,8},{4,12},{8,0},{12,4},{1,9},{5,13},{9,1},{13,5},{2,10},{6,14},... | collective-permute-start | bytes 1544 | tf_op jit(solution)/shard_map/ppermute | solution.py:365
  6.3 1.2 %copy-done.1 = bf16[1,64,64,128]{3,2,1,0:T(8,128)(2,1)S(1)} copy-done((bf16[1,64,64,128]{3,2,1,0:T(8,128)(2,1)S(1)}, bf16[1,64,64,128]{3,2,1,0:T(8,128)(2,1)}, u32[]{:S(2)}) %copy-start.1) | copy-done | bytes 1048600
  8.5 3.5 %collective-permute-done.2.refs_4_ = s32[8,16]{1,0:T(8,128)S(1)} collective-permute-done((s32[8,16]{1,0:T(8,128)}, s32[8,16]{1,0:T(8,128)S(1)}, u32[]{:S(2)}, u32[]{:S(2)}) %collective-permute-start.2) | collective-permute-done | bytes 544 | tf_op jit(solution)/shard_map/ppermute | solution.py:365
  12.0 1.6 %collective-permute-start.3 = (s32[4,8,16]{2,1,0:T(8,128)S(1)}, s32[4,8,16]{2,1,0:T(8,128)S(1)}, u32[]{:S(2)}, u32[]{:S(2)}) collective-permute-start(s32[4,8,16]{2,1,0:T(8,128)S(1)} %pad_add_fusion), channel_id=1, source_target_pairs={{0,2},{2,0},{1,3},{3,1},{4,6},{6,4},{5,7},{7,5},{8,10},{10,8},{9,1... | collective-permute-start | bytes 6152 | tf_op jit(solution)/shard_map/ppermute | solution.py:370
  14.3 1.5 %collective-permute-done.3.refs_5_.far_ref = s32[4,8,16]{2,1,0:T(8,128)S(1)} collective-permute-done((s32[4,8,16]{2,1,0:T(8,128)S(1)}, s32[4,8,16]{2,1,0:T(8,128)S(1)}, u32[]{:S(2)}, u32[]{:S(2)}) %collective-permute-start.3) | collective-permute-done | bytes 2080 | tf_op jit(solution)/shard_map/ppermute | solution.py:370
  15.8 1.2 %shard_map.116 = bf16[8,64,128]{2,1,0:T(8,128)(2,1)S(1)} custom-call(s32[8,16]{1,0:T(8,128)S(1)} %bitcast.36, s32[4,8,16]{2,1,0:T(8,128)S(1)} %collective-permute-done.3.refs_5_.far_ref, bf16[64,64,128]{2,1,0:T(8,128)(2,1)S(1)} %shard_map.112.refs_6_.log_ref), custom_call_target="tpu_custom_call" | custom-call | tf_op jit(solution)/shard_map/pallas_call | solution.py:433
  17.0 1.6 %collective-permute-start.6 = (bf16[8,64,128]{2,1,0:T(8,128)(2,1)S(1)}, bf16[8,64,128]{2,1,0:T(8,128)(2,1)S(1)}, u32[]{:S(2)}, u32[]{:S(2)}) collective-permute-start(bf16[8,64,128]{2,1,0:T(8,128)(2,1)S(1)} %shard_map.116), channel_id=1, source_target_pairs={{0,2},{2,0},{1,3},{3,1},{4,6},{6,4},{5,7},{7,5},{8,10},{10,8},{9,1... | collective-permute-start | bytes 393224 | tf_op jit(solution)/shard_map/ppermute | solution.py:370
  20.5 2.6 %shard_map.113 = (f32[8,64,128]{2,1,0:T(8,128)S(1)}, f32[8,64,128]{2,1,0:T(8,128)S(1)}, s32[65]{0:T(128)S(1)}) custom-call(s32[8,16]{1,0:T(8,128)S(1)} %bitcast.38, s32[8,16]{1,0:T(8,128)S(1)} %bitcast.42, s32[8,16]{1,0:T(8,128)S(1)} %collective-permute-done.refs_2_, s32[8,16]{1,0:T(8,128)S(1)} %collective-permute-done.1.refs_3_, ...), custom_call_target="tpu_custom_call" | custom-call | tf_op jit(solution)/shard_map/pallas_call | solution.py:444
  24.8 2.0 %collective-permute-start.5 = (bf16[4,64,128]{2,1,0:T(8,128)(2,1)S(1)}, bf16[4,64,128]{2,1,0:T(8,128)(2,1)S(1)}, u32[]{:S(2)}, u32[]{:S(2)}) collective-permute-start(bf16[4,64,128]{2,1,0:T(8,128)(2,1)S(1)} %get-tuple-element.42), channel_id=1, source_target_pairs={{0,4},{4,0},{8,12},{12,8},{1,5},{5,1},{9,13},{13,9},{2,6},{6,2},{1... | collective-permute-start | bytes 196616 | tf_op jit(solution)/shard_map/ppermute | solution.py:365
  26.9 1.5 %collective-permute-done.7.refs_2_ = bf16[4,64,128]{2,1,0:T(8,128)(2,1)S(1)} collective-permute-done((bf16[4,64,128]{2,1,0:T(8,128)(2,1)S(1)}, bf16[4,64,128]{2,1,0:T(8,128)(2,1)S(1)}, u32[]{:S(2)}, u32[]{:S(2)}) %collective-permute-start.7) | collective-permute-done | bytes 65568 | tf_op jit(solution)/shard_map/ppermute | solution.py:365
  31.2 1.5 %collective-permute-start.11 = (bf16[2,64,128]{2,1,0:T(8,128)(2,1)S(1)}, bf16[2,64,128]{2,1,0:T(8,128)(2,1)S(1)}, u32[]{:S(2)}, u32[]{:S(2)}) collective-permute-start(bf16[2,64,128]{2,1,0:T(8,128)(2,1)S(1)} %get-tuple-element.49), channel_id=1, source_target_pairs={{0,2},{2,0},{1,3},{3,1},{4,6},{6,4},{5,7},{7,5},{8,10},{10,8},{9,1... | collective-permute-start | bytes 98312 | tf_op jit(solution)/shard_map/ppermute | solution.py:359
  32.6 2.6 %collective-permute-start.9 = (bf16[2,64,128]{2,1,0:T(8,128)(2,1)S(1)}, bf16[2,64,128]{2,1,0:T(8,128)(2,1)S(1)}, u32[]{:S(2)}, u32[]{:S(2)}) collective-permute-start(bf16[2,64,128]{2,1,0:T(8,128)(2,1)S(1)} %get-tuple-element.47), channel_id=1, source_target_pairs={{0,4},{4,0},{8,12},{12,8},{1,5},{5,1},{9,13},{13,9},{2,6},{6,2},{1... | collective-permute-start | bytes 98312 | tf_op jit(solution)/shard_map/ppermute | solution.py:359
  35.9 1.3 %collective-permute-done.9.refs_1_ = bf16[2,64,128]{2,1,0:T(8,128)(2,1)S(1)} collective-permute-done((bf16[2,64,128]{2,1,0:T(8,128)(2,1)S(1)}, bf16[2,64,128]{2,1,0:T(8,128)(2,1)S(1)}, u32[]{:S(2)}, u32[]{:S(2)}) %collective-permute-start.9) | collective-permute-done | bytes 32800 | tf_op jit(solution)/shard_map/ppermute | solution.py:359
  37.2 3.4 %shard_map.119 = (f32[128,512]{1,0:T(8,128)S(1)}, bf16[64,3584]{1,0:T(8,128)(2,1)S(1)}) custom-call(bf16[4,64,128]{2,1,0:T(8,128)(2,1)S(1)} %get-tuple-element.46.refs_0_, bf16[2,64,128]{2,1,0:T(8,128)(2,1)S(1)} %collective-permute-done.9.refs_1_, bf16[2,64,128]{2,1,0:T(8,128)(2,1)S(1)} %collective-permute-done.10.refs_2_, ...), custom_call_target="tpu_custom_call" | custom-call | tf_op jit(solution)/shard_map/pallas_call | solution.py:490
  40.7 2.0 %all-gather = bf16[1,4,128,128]{3,2,1,0:T(8,128)(2,1)S(1)} all-gather(bf16[1,4,64,128]{3,2,1,0:T(8,128)(2,1)S(1)} %copy-done.4), channel_id=2, replica_groups=mesh['groups'=2,'tile'=4,'depth'=2,'chan'=2] {'chan'}, dimensions={2}, use_global_device_ids=true | all-gather | bytes 196608 | tf_op jit(solution)/shard_map/all_gather | solution.py:415
  42.7 3.5 %shard_map.120 = (bf16[128,3584]{1,0:T(8,128)(2,1)S(1)}, f32[4,64,128]{2,1,0:T(8,128)S(1)}, bf16[2,64,128]{2,1,0:T(8,128)(2,1)S(1)}, bf16[2,64,128]{2,1,0:T(8,128)(2,1)S(1)}, bf16[2,64,128]{2,1,0:T(8,128)(2,1)S(1)}) custom-call(f32[128,512]{1,0:T(8,128)S(1)} %get-tuple-element.50.refs_0_.part_ref, f32[128,512]{1,0:T(8,128)S(1)} %collective-permute-done.12.refs_1_.other_ref, ...), custom_call_target="tpu_custom_call" | custom-call | tf_op jit(solution)/shard_map/pallas_call | solution.py:503
  46.2 2.1 %collective-permute-start.13 = (bf16[2,64,128]{2,1,0:T(8,128)(2,1)S(1)}, bf16[2,64,128]{2,1,0:T(8,128)(2,1)S(1)}, u32[]{:S(2)}, u32[]{:S(2)}) collective-permute-start(bf16[2,64,128]{2,1,0:T(8,128)(2,1)S(1)} %get-tuple-element.57), channel_id=1, source_target_pairs={{0,4},{4,0},{8,12},{12,8},{1,5},{5,1},{9,13},{13,9},{2,6},{6,2},{1... | collective-permute-start | bytes 98312 | tf_op jit(solution)/shard_map/ppermute | solution.py:359
  49.6 1.4 %shard_map.121 = (bf16[4,64,128]{2,1,0:T(8,128)(2,1)}, f32[896,128]{1,0:T(8,128)S(1)}, bf16[896,128]{1,0:T(8,128)(2,1)S(1)}) custom-call(f32[128,512]{1,0:T(8,128)S(1)} %get-tuple-element.50.refs_0_.part_ref, f32[128,512]{1,0:T(8,128)S(1)} %collective-permute-done.12.refs_1_.other_ref, bf16[64,3584]{1,0:T(8,128)(2,1)S(1)} %get-tuple-element.51.columns_ref, ...), custom_call_target="tpu_custom_call" | custom-call | tf_op jit(solution)/shard_map/pallas_call | solution.py:521
  51.0 2.0 %collective-permute-done.15.refs_2_ = bf16[2,64,128]{2,1,0:T(8,128)(2,1)S(1)} collective-permute-done((bf16[2,64,128]{2,1,0:T(8,128)(2,1)S(1)}, bf16[2,64,128]{2,1,0:T(8,128)(2,1)S(1)}, u32[]{:S(2)}, u32[]{:S(2)}) %collective-permute-start.15) | collective-permute-done | bytes 32800 | tf_op jit(solution)/shard_map/ppermute | solution.py:359
  54.1 3.2 %collective-permute-start.16 = (bf16[4,64,128]{2,1,0:T(8,128)(2,1)S(1)}, bf16[4,64,128]{2,1,0:T(8,128)(2,1)S(1)}, u32[]{:S(2)}, u32[]{:S(2)}) collective-permute-start(bf16[4,64,128]{2,1,0:T(8,128)(2,1)S(1)} %shard_map.122.refs_0_), channel_id=1, source_target_pairs={{0,4},{4,0},{8,12},{12,8},{1,5},{5,1},{9,13},{13,9},{2,6},{6,2},{1... | collective-permute-start | bytes 196616 | tf_op jit(solution)/shard_map/ppermute | solution.py:365
  57.6 2.2 %collective-permute-start.18 = (bf16[4,64,128]{2,1,0:T(8,128)(2,1)S(1)}, bf16[4,64,128]{2,1,0:T(8,128)(2,1)S(1)}, u32[]{:S(2)}, u32[]{:S(2)}) collective-permute-start(bf16[4,64,128]{2,1,0:T(8,128)(2,1)S(1)} %shard_map.122.refs_0_), channel_id=1, source_target_pairs={{0,12},{4,8},{8,4},{12,0},{1,13},{5,9},{9,5},{13,1},{2,14},{6,10},... | collective-permute-start | bytes 196616 | tf_op jit(solution)/shard_map/ppermute | solution.py:365
  59.9 2.8 %collective-permute-start.20 = (bf16[224,128]{1,0:T(8,128)(2,1)S(1)}, bf16[224,128]{1,0:T(8,128)(2,1)S(1)}, u32[]{:S(2)}, u32[]{:S(2)}) collective-permute-start(bf16[224,128]{1,0:T(8,128)(2,1)S(1)} %get-tuple-element.66), channel_id=1, source_target_pairs={{0,4},{4,0},{8,12},{12,8},{1,5},{5,1},{9,13},{13,9},{2,6},{6,2},{1... | collective-permute-start | bytes 172040 | tf_op jit(solution)/shard_map/ppermute | solution.py:365
  62.9 2.2 %collective-permute-start.22 = (bf16[224,128]{1,0:T(8,128)(2,1)S(1)}, bf16[224,128]{1,0:T(8,128)(2,1)S(1)}, u32[]{:S(2)}, u32[]{:S(2)}) collective-permute-start(bf16[224,128]{1,0:T(8,128)(2,1)S(1)} %get-tuple-element.68), channel_id=1, source_target_pairs={{0,12},{4,8},{8,4},{12,0},{1,13},{5,9},{9,5},{13,1},{2,14},{6,10},... | collective-permute-start | bytes 172040 | tf_op jit(solution)/shard_map/ppermute | solution.py:365
  65.7 2.7 %collective-permute-done.21.refs_6_ = bf16[224,128]{1,0:T(8,128)(2,1)S(1)} collective-permute-done((bf16[224,128]{1,0:T(8,128)(2,1)S(1)}, bf16[224,128]{1,0:T(8,128)(2,1)S(1)}, u32[]{:S(2)}, u32[]{:S(2)}) %collective-permute-start.21) | collective-permute-done | bytes 57376 | tf_op jit(solution)/shard_map/ppermute | solution.py:365
  69.0 1.5 %collective-permute-start.26 = (bf16[1248,128]{1,0:T(8,128)(2,1)S(1)}, bf16[1248,128]{1,0:T(8,128)(2,1)S(1)}, u32[]{:S(2)}, u32[]{:S(2)}) collective-permute-start(bf16[1248,128]{1,0:T(8,128)(2,1)S(1)} %get-tuple-element.69.own_ref), channel_id=1, source_target_pairs={{0,2},{2,0},{1,3},{3,1},{4,6},{6,4},{5,7},{7,5},{8,10},{10,8},{9,1... | collective-permute-start | bytes 958472 | tf_op jit(solution)/shard_map/ppermute | solution.py:370
  72.6 2.3 %collective-permute-start.25 = (bf16[224,128]{1,0:T(8,128)(2,1)S(1)}, bf16[224,128]{1,0:T(8,128)(2,1)S(1)}, u32[]{:S(2)}, u32[]{:S(2)}) collective-permute-start(bf16[224,128]{1,0:T(8,128)(2,1)S(1)} %get-tuple-element.70.refs_0_), channel_id=1, source_target_pairs={{0,12},{4,8},{8,4},{12,0},{1,13},{5,9},{9,5},{13,1},{2,14},{6,10},... | collective-permute-start | bytes 172040 | tf_op jit(solution)/shard_map/ppermute | solution.py:365
  75.6 1.8 %collective-permute-done.24.refs_2_ = bf16[224,128]{1,0:T(8,128)(2,1)S(1)} collective-permute-done((bf16[224,128]{1,0:T(8,128)(2,1)S(1)}, bf16[224,128]{1,0:T(8,128)(2,1)S(1)}, u32[]{:S(2)}, u32[]{:S(2)}) %collective-permute-start.24) | collective-permute-done | bytes 57376 | tf_op jit(solution)/shard_map/ppermute | solution.py:365
  77.4 1.2 %collective-permute-done.25.refs_3_ = bf16[224,128]{1,0:T(8,128)(2,1)S(1)} collective-permute-done((bf16[224,128]{1,0:T(8,128)(2,1)S(1)}, bf16[224,128]{1,0:T(8,128)(2,1)S(1)}, u32[]{:S(2)}, u32[]{:S(2)}) %collective-permute-start.25) | collective-permute-done | bytes 57376 | tf_op jit(solution)/shard_map/ppermute | solution.py:365
  78.7 1.3 %collective-permute-start.27 = (bf16[672,128]{1,0:T(8,128)(2,1)S(1)}, bf16[672,128]{1,0:T(8,128)(2,1)S(1)}, u32[]{:S(2)}, u32[]{:S(2)}) collective-permute-start(bf16[672,128]{1,0:T(8,128)(2,1)S(1)} %pad_maximum_fusion), channel_id=1, source_target_pairs={{0,2},{2,0},{1,3},{3,1},{4,6},{6,4},{5,7},{7,5},{8,10},{10,8},{9,1... | collective-permute-start | bytes 516104 | tf_op jit(solution)/shard_map/ppermute | solution.py:370
  80.0 1.6 %shard_map.125 = bf16[64,64,128]{2,1,0:T(8,128)(2,1)} custom-call(s32[65]{0:T(128)S(1)} %get-tuple-element.54.place_ref, bf16[1248,128]{1,0:T(8,128)(2,1)S(1)} %get-tuple-element.69.own_ref, bf16[1248,128]{1,0:T(8,128)(2,1)S(1)} %collective-permute-done.26.other_ref.refs_4_), custom_call_target="tpu_custom_call" | custom-call | tf_op jit(solution)/shard_map/pallas_call | solution.py:563
  81.6 2.5 %collective-permute-done.27.refs_5_ = bf16[672,128]{1,0:T(8,128)(2,1)S(1)} collective-permute-done((bf16[672,128]{1,0:T(8,128)(2,1)S(1)}, bf16[672,128]{1,0:T(8,128)(2,1)S(1)}, u32[]{:S(2)}, u32[]{:S(2)}) %collective-permute-start.27) | collective-permute-done | bytes 172064 | tf_op jit(solution)/shard_map/ppermute | solution.py:370
  (67 shorter events, 16.6 us)
Async XLA Ops:
  0.6 26.2 %copy-start = (bf16[27,128,128]{2,1,0:T(8,128)(2,1)S(1)}, bf16[27,128,128]{2,1,0:T(8,128)(2,1)}, u32[]{:S(2)}) copy-start(bf16[27,128,128]{2,1,0:T(8,128)(2,1)} %param.16) | copy-start | bytes 2654212
  0.6 7.0 %collective-permute-start = (s32[8,16]{1,0:T(8,128)}, s32[8,16]{1,0:T(8,128)S(1)}, u32[]{:S(2)}, u32[]{:S(2)}) collective-permute-start(s32[8,16]{1,0:T(8,128)} %bitcast.39), channel_id=1, source_target_pairs={{0,4},{4,0},{8,12},{12,8},{1,5},{5,1},{9,13},{13,9},{2,6},{6,2},{1... | collective-permute-start | bytes 1544 | tf_op jit(solution)/shard_map/ppermute | solution.py:365
  3.7 4.7 %collective-permute-start.1 = (s32[8,16]{1,0:T(8,128)}, s32[8,16]{1,0:T(8,128)S(1)}, u32[]{:S(2)}, u32[]{:S(2)}) collective-permute-start(s32[8,16]{1,0:T(8,128)} %bitcast.40), channel_id=1, source_target_pairs={{0,8},{4,12},{8,0},{12,4},{1,9},{5,13},{9,1},{13,5},{2,10},{6,14},... | collective-permute-start | bytes 1544 | tf_op jit(solution)/shard_map/ppermute | solution.py:365
  6.3 5.6 %collective-permute-start.2 = (s32[8,16]{1,0:T(8,128)}, s32[8,16]{1,0:T(8,128)S(1)}, u32[]{:S(2)}, u32[]{:S(2)}) collective-permute-start(s32[8,16]{1,0:T(8,128)} %bitcast.41), channel_id=1, source_target_pairs={{0,12},{4,8},{8,4},{12,0},{1,13},{5,9},{9,5},{13,1},{2,14},{6,10},... | collective-permute-start | bytes 1544 | tf_op jit(solution)/shard_map/ppermute | solution.py:365
  7.6 4.3 %copy-start.3 = (s32[1,8,16]{2,1,0:T(8,128)S(1)}, s32[1,8,16]{2,1,0:T(8,128)}, u32[]{:S(2)}) copy-start(s32[1,8,16]{2,1,0:T(8,128)} %param.11) | copy-start | bytes 1540
  12.0 3.8 %collective-permute-start.3 = (s32[4,8,16]{2,1,0:T(8,128)S(1)}, s32[4,8,16]{2,1,0:T(8,128)S(1)}, u32[]{:S(2)}, u32[]{:S(2)}) collective-permute-start(s32[4,8,16]{2,1,0:T(8,128)S(1)} %pad_add_fusion), channel_id=1, source_target_pairs={{0,2},{2,0},{1,3},{3,1},{4,6},{6,4},{5,7},{7,5},{8,10},{10,8},{9,1... | collective-permute-start | bytes 6152 | tf_op jit(solution)/shard_map/ppermute | solution.py:370
  17.0 3.4 %copy-start.5 = (s32[1,27,128]{2,0,1:T(1,128)S(1)}, s32[1,27,128]{2,0,1:T(1,128)}, u32[]{:S(2)}) copy-start(s32[1,27,128]{2,0,1:T(1,128)} %param.14) | copy-start | bytes 41476
  17.0 6.2 %collective-permute-start.6 = (bf16[8,64,128]{2,1,0:T(8,128)(2,1)S(1)}, bf16[8,64,128]{2,1,0:T(8,128)(2,1)S(1)}, u32[]{:S(2)}, u32[]{:S(2)}) collective-permute-start(bf16[8,64,128]{2,1,0:T(8,128)(2,1)S(1)} %shard_map.116), channel_id=1, source_target_pairs={{0,2},{2,0},{1,3},{3,1},{4,6},{6,4},{5,7},{7,5},{8,10},{10,8},{9,1... | collective-permute-start | bytes 393224 | tf_op jit(solution)/shard_map/ppermute | solution.py:370
  19.8 5.0 %collective-permute-start.4 = (bf16[8,64,128]{2,1,0:T(8,128)(2,1)S(1)}, bf16[8,64,128]{2,1,0:T(8,128)(2,1)S(1)}, u32[]{:S(2)}, u32[]{:S(2)}) collective-permute-start(bf16[8,64,128]{2,1,0:T(8,128)(2,1)S(1)} %shard_map.114), channel_id=1, source_target_pairs={{0,2},{2,0},{1,3},{3,1},{4,6},{6,4},{5,7},{7,5},{8,10},{10,8},{9,1... | collective-permute-start | bytes 393224 | tf_op jit(solution)/shard_map/ppermute | solution.py:370
  23.2 5.2 %collective-permute-start.7 = (bf16[4,64,128]{2,1,0:T(8,128)(2,1)S(1)}, bf16[4,64,128]{2,1,0:T(8,128)(2,1)S(1)}, u32[]{:S(2)}, u32[]{:S(2)}) collective-permute-start(bf16[4,64,128]{2,1,0:T(8,128)(2,1)S(1)} %get-tuple-element.44), channel_id=1, source_target_pairs={{0,8},{4,12},{8,0},{12,4},{1,9},{5,13},{9,1},{13,5},{2,10},{6,14},... | collective-permute-start | bytes 196616 | tf_op jit(solution)/shard_map/ppermute | solution.py:365
  23.3 6.3 %collective-permute-start.8 = (bf16[4,64,128]{2,1,0:T(8,128)(2,1)S(1)}, bf16[4,64,128]{2,1,0:T(8,128)(2,1)S(1)}, u32[]{:S(2)}, u32[]{:S(2)}) collective-permute-start(bf16[4,64,128]{2,1,0:T(8,128)(2,1)S(1)} %get-tuple-element.45), channel_id=1, source_target_pairs={{0,12},{4,8},{8,4},{12,0},{1,13},{5,9},{9,5},{13,1},{2,14},{6,10},... | collective-permute-start | bytes 196616 | tf_op jit(solution)/shard_map/ppermute | solution.py:365
  24.8 5.0 %collective-permute-start.5 = (bf16[4,64,128]{2,1,0:T(8,128)(2,1)S(1)}, bf16[4,64,128]{2,1,0:T(8,128)(2,1)S(1)}, u32[]{:S(2)}, u32[]{:S(2)}) collective-permute-start(bf16[4,64,128]{2,1,0:T(8,128)(2,1)S(1)} %get-tuple-element.42), channel_id=1, source_target_pairs={{0,4},{4,0},{8,12},{12,8},{1,5},{5,1},{9,13},{13,9},{2,6},{6,2},{1... | collective-permute-start | bytes 196616 | tf_op jit(solution)/shard_map/ppermute | solution.py:365
  30.5 5.4 %collective-permute-start.10 = (bf16[2,64,128]{2,1,0:T(8,128)(2,1)S(1)}, bf16[2,64,128]{2,1,0:T(8,128)(2,1)S(1)}, u32[]{:S(2)}, u32[]{:S(2)}) collective-permute-start(bf16[2,64,128]{2,1,0:T(8,128)(2,1)S(1)} %get-tuple-element.48), channel_id=1, source_target_pairs={{4,8},{8,4},{5,9},{9,5},{6,10},{10,6},{7,11},{11,7},{20,24},{24,20... | collective-permute-start | bytes 98312 | tf_op jit(solution)/shard_map/ppermute | solution.py:359
  31.2 4.7 %collective-permute-start.11 = (bf16[2,64,128]{2,1,0:T(8,128)(2,1)S(1)}, bf16[2,64,128]{2,1,0:T(8,128)(2,1)S(1)}, u32[]{:S(2)}, u32[]{:S(2)}) collective-permute-start(bf16[2,64,128]{2,1,0:T(8,128)(2,1)S(1)} %get-tuple-element.49), channel_id=1, source_target_pairs={{0,2},{2,0},{1,3},{3,1},{4,6},{6,4},{5,7},{7,5},{8,10},{10,8},{9,1... | collective-permute-start | bytes 98312 | tf_op jit(solution)/shard_map/ppermute | solution.py:359
  32.6 4.5 %collective-permute-start.9 = (bf16[2,64,128]{2,1,0:T(8,128)(2,1)S(1)}, bf16[2,64,128]{2,1,0:T(8,128)(2,1)S(1)}, u32[]{:S(2)}, u32[]{:S(2)}) collective-permute-start(bf16[2,64,128]{2,1,0:T(8,128)(2,1)S(1)} %get-tuple-element.47), channel_id=1, source_target_pairs={{0,4},{4,0},{8,12},{12,8},{1,5},{5,1},{9,13},{13,9},{2,6},{6,2},{1... | collective-permute-start | bytes 98312 | tf_op jit(solution)/shard_map/ppermute | solution.py:359
  37.2 3.5 %copy-start.4 = (bf16[1,4,64,128]{3,2,1,0:T(8,128)(2,1)S(1)}, bf16[1,4,64,128]{3,2,1,0:T(8,128)(2,1)}, u32[]{:S(2)}) copy-start(bf16[1,4,64,128]{3,2,1,0:T(8,128)(2,1)} %param.17) | copy-start | bytes 196612
  40.6 2.1 %collective-permute-start.12 = (f32[128,512]{1,0:T(8,128)S(1)}, f32[128,512]{1,0:T(8,128)S(1)}, u32[]{:S(2)}, u32[]{:S(2)}) collective-permute-start(f32[128,512]{1,0:T(8,128)S(1)} %get-tuple-element.50.refs_0_.part_ref), channel_id=1, source_target_pairs={{0,1},{1,0},{2,3},{3,2},{4,5},{5,4},{6,7},{7,6},{8,9},{9,8},{10,11... | collective-permute-start | bytes 786440 | tf_op jit(solution)/shard_map/ppermute | solution.py:501
  46.2 4.8 %collective-permute-start.13 = (bf16[2,64,128]{2,1,0:T(8,128)(2,1)S(1)}, bf16[2,64,128]{2,1,0:T(8,128)(2,1)S(1)}, u32[]{:S(2)}, u32[]{:S(2)}) collective-permute-start(bf16[2,64,128]{2,1,0:T(8,128)(2,1)S(1)} %get-tuple-element.57), channel_id=1, source_target_pairs={{0,4},{4,0},{8,12},{12,8},{1,5},{5,1},{9,13},{13,9},{2,6},{6,2},{1... | collective-permute-start | bytes 98312 | tf_op jit(solution)/shard_map/ppermute | solution.py:359
  48.3 2.7 %collective-permute-start.14 = (bf16[2,64,128]{2,1,0:T(8,128)(2,1)S(1)}, bf16[2,64,128]{2,1,0:T(8,128)(2,1)S(1)}, u32[]{:S(2)}, u32[]{:S(2)}) collective-permute-start(bf16[2,64,128]{2,1,0:T(8,128)(2,1)S(1)} %get-tuple-element.58), channel_id=1, source_target_pairs={{4,8},{8,4},{5,9},{9,5},{6,10},{10,6},{7,11},{11,7},{20,24},{24,20... | collective-permute-start | bytes 98312 | tf_op jit(solution)/shard_map/ppermute | solution.py:359
  48.9 4.0 %collective-permute-start.15 = (bf16[2,64,128]{2,1,0:T(8,128)(2,1)S(1)}, bf16[2,64,128]{2,1,0:T(8,128)(2,1)S(1)}, u32[]{:S(2)}, u32[]{:S(2)}) collective-permute-start(bf16[2,64,128]{2,1,0:T(8,128)(2,1)S(1)} %get-tuple-element.59), channel_id=1, source_target_pairs={{0,2},{2,0},{1,3},{3,1},{4,6},{6,4},{5,7},{7,5},{8,10},{10,8},{9,1... | collective-permute-start | bytes 98312 | tf_op jit(solution)/shard_map/ppermute | solution.py:359
  52.9 6.9 %collective-permute-start.19 = (bf16[896,128]{1,0:T(8,128)(2,1)S(1)}, bf16[896,128]{1,0:T(8,128)(2,1)S(1)}, u32[]{:S(2)}, u32[]{:S(2)}) collective-permute-start(bf16[896,128]{1,0:T(8,128)(2,1)S(1)} %get-tuple-element.64), channel_id=1, source_target_pairs={{0,2},{2,0},{1,3},{3,1},{4,6},{6,4},{5,7},{7,5},{8,10},{10,8},{9,1... | collective-permute-start | bytes 688136 | tf_op jit(solution)/shard_map/ppermute | solution.py:370
  54.1 8.8 %collective-permute-start.16 = (bf16[4,64,128]{2,1,0:T(8,128)(2,1)S(1)}, bf16[4,64,128]{2,1,0:T(8,128)(2,1)S(1)}, u32[]{:S(2)}, u32[]{:S(2)}) collective-permute-start(bf16[4,64,128]{2,1,0:T(8,128)(2,1)S(1)} %shard_map.122.refs_0_), channel_id=1, source_target_pairs={{0,4},{4,0},{8,12},{12,8},{1,5},{5,1},{9,13},{13,9},{2,6},{6,2},{1... | collective-permute-start | bytes 196616 | tf_op jit(solution)/shard_map/ppermute | solution.py:365
  57.4 7.8 %collective-permute-start.17 = (bf16[4,64,128]{2,1,0:T(8,128)(2,1)S(1)}, bf16[4,64,128]{2,1,0:T(8,128)(2,1)S(1)}, u32[]{:S(2)}, u32[]{:S(2)}) collective-permute-start(bf16[4,64,128]{2,1,0:T(8,128)(2,1)S(1)} %shard_map.122.refs_0_), channel_id=1, source_target_pairs={{0,8},{4,12},{8,0},{12,4},{1,9},{5,13},{9,1},{13,5},{2,10},{6,14},... | collective-permute-start | bytes 196616 | tf_op jit(solution)/shard_map/ppermute | solution.py:365
  57.6 7.6 %collective-permute-start.18 = (bf16[4,64,128]{2,1,0:T(8,128)(2,1)S(1)}, bf16[4,64,128]{2,1,0:T(8,128)(2,1)S(1)}, u32[]{:S(2)}, u32[]{:S(2)}) collective-permute-start(bf16[4,64,128]{2,1,0:T(8,128)(2,1)S(1)} %shard_map.122.refs_0_), channel_id=1, source_target_pairs={{0,12},{4,8},{8,4},{12,0},{1,13},{5,9},{9,5},{13,1},{2,14},{6,10},... | collective-permute-start | bytes 196616 | tf_op jit(solution)/shard_map/ppermute | solution.py:365
  59.9 5.8 %collective-permute-start.20 = (bf16[224,128]{1,0:T(8,128)(2,1)S(1)}, bf16[224,128]{1,0:T(8,128)(2,1)S(1)}, u32[]{:S(2)}, u32[]{:S(2)}) collective-permute-start(bf16[224,128]{1,0:T(8,128)(2,1)S(1)} %get-tuple-element.66), channel_id=1, source_target_pairs={{0,4},{4,0},{8,12},{12,8},{1,5},{5,1},{9,13},{13,9},{2,6},{6,2},{1... | collective-permute-start | bytes 172040 | tf_op jit(solution)/shard_map/ppermute | solution.py:365
  62.7 5.7 %collective-permute-start.21 = (bf16[224,128]{1,0:T(8,128)(2,1)S(1)}, bf16[224,128]{1,0:T(8,128)(2,1)S(1)}, u32[]{:S(2)}, u32[]{:S(2)}) collective-permute-start(bf16[224,128]{1,0:T(8,128)(2,1)S(1)} %get-tuple-element.67), channel_id=1, source_target_pairs={{0,8},{4,12},{8,0},{12,4},{1,9},{5,13},{9,1},{13,5},{2,10},{6,14},... | collective-permute-start | bytes 172040 | tf_op jit(solution)/shard_map/ppermute | solution.py:365
  62.9 6.1 %collective-permute-start.22 = (bf16[224,128]{1,0:T(8,128)(2,1)S(1)}, bf16[224,128]{1,0:T(8,128)(2,1)S(1)}, u32[]{:S(2)}, u32[]{:S(2)}) collective-permute-start(bf16[224,128]{1,0:T(8,128)(2,1)S(1)} %get-tuple-element.68), channel_id=1, source_target_pairs={{0,12},{4,8},{8,4},{12,0},{1,13},{5,9},{9,5},{13,1},{2,14},{6,10},... | collective-permute-start | bytes 172040 | tf_op jit(solution)/shard_map/ppermute | solution.py:365
  69.0 9.6 %collective-permute-start.26 = (bf16[1248,128]{1,0:T(8,128)(2,1)S(1)}, bf16[1248,128]{1,0:T(8,128)(2,1)S(1)}, u32[]{:S(2)}, u32[]{:S(2)}) collective-permute-start(bf16[1248,128]{1,0:T(8,128)(2,1)S(1)} %get-tuple-element.69.own_ref), channel_id=1, source_target_pairs={{0,2},{2,0},{1,3},{3,1},{4,6},{6,4},{5,7},{7,5},{8,10},{10,8},{9,1... | collective-permute-start | bytes 958472 | tf_op jit(solution)/shard_map/ppermute | solution.py:370
  70.5 5.0 %collective-permute-start.23 = (bf16[224,128]{1,0:T(8,128)(2,1)S(1)}, bf16[224,128]{1,0:T(8,128)(2,1)S(1)}, u32[]{:S(2)}, u32[]{:S(2)}) collective-permute-start(bf16[224,128]{1,0:T(8,128)(2,1)S(1)} %get-tuple-element.70.refs_0_), channel_id=1, source_target_pairs={{0,4},{4,0},{8,12},{12,8},{1,5},{5,1},{9,13},{13,9},{2,6},{6,2},{1... | collective-permute-start | bytes 172040 | tf_op jit(solution)/shard_map/ppermute | solution.py:365
  71.7 5.7 %collective-permute-start.24 = (bf16[224,128]{1,0:T(8,128)(2,1)S(1)}, bf16[224,128]{1,0:T(8,128)(2,1)S(1)}, u32[]{:S(2)}, u32[]{:S(2)}) collective-permute-start(bf16[224,128]{1,0:T(8,128)(2,1)S(1)} %get-tuple-element.70.refs_0_), channel_id=1, source_target_pairs={{0,8},{4,12},{8,0},{12,4},{1,9},{5,13},{9,1},{13,5},{2,10},{6,14},... | collective-permute-start | bytes 172040 | tf_op jit(solution)/shard_map/ppermute | solution.py:365
  72.6 6.0 %collective-permute-start.25 = (bf16[224,128]{1,0:T(8,128)(2,1)S(1)}, bf16[224,128]{1,0:T(8,128)(2,1)S(1)}, u32[]{:S(2)}, u32[]{:S(2)}) collective-permute-start(bf16[224,128]{1,0:T(8,128)(2,1)S(1)} %get-tuple-element.70.refs_0_), channel_id=1, source_target_pairs={{0,12},{4,8},{8,4},{12,0},{1,13},{5,9},{9,5},{13,1},{2,14},{6,10},... | collective-permute-start | bytes 172040 | tf_op jit(solution)/shard_map/ppermute | solution.py:365
  78.7 5.5 %collective-permute-start.27 = (bf16[672,128]{1,0:T(8,128)(2,1)S(1)}, bf16[672,128]{1,0:T(8,128)(2,1)S(1)}, u32[]{:S(2)}, u32[]{:S(2)}) collective-permute-start(bf16[672,128]{1,0:T(8,128)(2,1)S(1)} %pad_maximum_fusion), channel_id=1, source_target_pairs={{0,2},{2,0},{1,3},{3,1},{4,6},{6,4},{5,7},{7,5},{8,10},{10,8},{9,1... | collective-permute-start | bytes 516104 | tf_op jit(solution)/shard_map/ppermute | solution.py:370
  (5 other events, 7.4 us)

commit v3 on v2

--- a/solution.py
+++ b/solution.py
@@ -76,11 +76,8 @@
 
 
 def near_kernel(tile_rows, depths, tile_blocks, *refs):
-    send_ref, tables, far_ref = refs[0], refs[1 : 1 + tile_rows], refs[1 + tile_rows]
-    log_ref, (*outs, place_ref) = refs[2 + tile_rows], refs[3 + tile_rows :]
+    send_ref, tables, log_ref, outs = refs[0], refs[1:-3], refs[-3], refs[-2:]
     per = tile_rows // len(outs)
-    i, j = lax.axis_index("tile"), lax.axis_index("depth")
-    me = i * depths + j
 
     def emit(d, m, total):
         outs[d // per][(d % per) * tile_blocks + m] = total
@@ -95,13 +92,19 @@
         log_ref,
         emit,
     )
+
+
+def place_kernel(tile_rows, depths, tile_blocks, *refs):
+    send_ref, tables, far_ref, place_ref = refs[0], refs[1:-2], refs[-2], refs[-1]
+    i, j = lax.axis_index("tile"), lax.axis_index("depth")
+    me = i * depths + j
     for jx in range(depths):
         for d in range(tile_rows):
             p = (i ^ d) * depths + (j ^ jx)
             for c in range(send_ref.shape[1]):
                 block = send_ref[p, c]
                 target = far_ref[d, me, c] if jx else tables[d][me, c]
-                spot = jnp.where(block >= 0, block, log_ref.shape[0])
+                spot = jnp.where(block >= 0, block, place_ref.shape[0] - 1)
                 place_ref[spot] = (jx * tile_rows + d) * tile_blocks + target
 
 
@@ -152,43 +155,72 @@
     return jnp.where(fold == f, part, jnp.zeros_like(part))
 
 
-def forward_kernel(swap_count, chunk, *refs):
-    features_ref = refs[0]
-    received = refs[1 : 1 + swap_count]
-    source_ref, target_ref, weight_ref = refs[1 + swap_count : 4 + swap_count]
-    part_ref, columns_ref, values, places = refs[4 + swap_count :]
-    tile_blocks, half, width = features_ref.shape
-    offsets = weight_ref.shape[0]
-    channels = weight_ref.shape[1]
+def gather_folds(folded, rows_ref, first_fold, chunk, half, base_of, emit):
+    offsets, width = rows_ref.shape
     span = 2 * width
-    blocks = [features_ref[b] for b in range(tile_blocks)]
-    for ref in received:
-        blocks += [ref[b] for b in range(ref.shape[0])]
-    folds = len(blocks) // 2
-    folded = jnp.concatenate(
-        [jnp.concatenate([blocks[2 * f], blocks[2 * f + 1]], 1) for f in range(folds)], 0
-    )
     for first in range(0, offsets, chunk):
-        ks = range(first, first + chunk)
-        rows = [table_row(source_ref, k) for k in ks]
+        rows = [table_row(rows_ref, k) for k in range(first, first + chunk)]
         table = jnp.concatenate([one_hot(r & (span - 1), span) for r in rows], 1)
         gathered = jnp.dot(folded, table, preferred_element_type=F32).astype(BF16)
-        for n, k in enumerate(ks):
-            lanes = slice(n * width, (n + 1) * width)
-            fold = (rows[n] // span).astype(F32).astype(BF16)
-            picked = pick_fold(
-                fold, [gathered[f * half : (f + 1) * half, lanes] for f in range(folds)]
-            )
-            columns_ref[:, k * width : (k + 1) * width] = picked
-            product = jnp.dot(weight_ref[k], picked, preferred_element_type=F32)
-            product = product.astype(BF16)
-            target = table_row(target_ref, k)
-            fold = (target // span).astype(F32).astype(BF16)
-            places[:, k * width : (k + 1) * width] = one_hot(target & (span - 1), span)
-            for f in range(2):
-                values[f * channels : (f + 1) * channels, k * width : (k + 1) * width] = mask_fold(
-                    fold, f, product
-                )
+        for n, row in enumerate(rows):
+            fold = (row // span).astype(F32).astype(BF16)
+            picked = base_of(first + n)
+            for f in range(folded.shape[0] // half):
+                part = gathered[f * half : (f + 1) * half, n * width : (n + 1) * width]
+                picked = jnp.where(fold == first_fold + f, part, picked)
+            emit(first + n, picked)
+
+
+def fold_blocks(blocks):
+    return jnp.concatenate(
+        [jnp.concatenate(blocks[n : n + 2], 1) for n in range(0, len(blocks), 2)], 0
+    )
+
+
+def own_columns_kernel(chunk, features_ref, source_ref, out_ref):
+    count, half, width = features_ref.shape
+    zero = jnp.zeros((half, width), BF16)
+
+    def emit(k, picked):
+        out_ref[:, k * width : (k + 1) * width] = picked
+
+    folded = fold_blocks([features_ref[b] for b in range(count)])
+    gather_folds(folded, source_ref, 0, chunk, half, lambda k: zero, emit)
+
+
+def forward_kernel(own_folds, chunk, *refs):
+    own_ref, source_ref, target_ref, weight_ref = refs[:4]
+    received, (part_ref, columns_ref, values, places) = refs[4:-4], refs[-4:]
+    channels, half = weight_ref.shape[1:]
+    offsets, width = source_ref.shape
+    span = 2 * width
+
+    def lanes(k):
+        return slice(k * width, (k + 1) * width)
+
+    def emit(k, picked):
+        columns_ref[:, lanes(k)] = picked
+        product = jnp.dot(weight_ref[k], picked, preferred_element_type=F32).astype(BF16)
+        target = table_row(target_ref, k)
+        fold = (target // span).astype(F32).astype(BF16)
+        places[:, lanes(k)] = one_hot(target & (span - 1), span)
+        for f in range(2):
+            values[f * channels : (f + 1) * channels, lanes(k)] = mask_fold(fold, f, product)
+
+    blocks = [ref[b] for ref in received for b in range(ref.shape[0])]
+    if blocks:
+        gather_folds(
+            fold_blocks(blocks),
+            source_ref,
+            own_folds,
+            chunk,
+            half,
+            lambda k: own_ref[:, lanes(k)],
+            emit,
+        )
+    else:
+        for k in range(offsets):
+            emit(k, own_ref[:, lanes(k)])
     total = lax.dot_general(
         values[...], places[...], (((1,), (1,)), ((), ())), preferred_element_type=F32
     )
@@ -196,14 +228,16 @@
     part_ref[:, span:] = total[channels:]
 
 
-def input_grad_kernel(chunk, *refs):
-    part_ref, other_ref, cotangent_ref, source_ref, target_ref, weight_ref = refs[:6]
-    grad_columns_ref, own_ref = refs[6:8]
-    rims, (values, places) = refs[8:-2], refs[-2:]
+def weight_grad_kernel(chunk, *refs):
+    part_ref, other_ref, cotangent_ref, target_ref, columns_ref = refs[:5]
+    act_ref, grad_columns_ref = refs[5:7]
+    portions, held = refs[7:-1], refs[-1]
     tile_blocks, channels, width = cotangent_ref.shape
-    offsets, half, _ = weight_ref.shape
+    half = columns_ref.shape[0]
+    offsets = target_ref.shape[0]
     span = 2 * width
-    folds = values.shape[0] // half
+    portion = offsets // len(portions)
+    here = lax.axis_index("depth") if len(portions) > 1 else 0
     preact = part_ref[...] + other_ref[...]
     gate = 1.0 / (1.0 + jnp.exp(-preact))
     cotangent = jnp.concatenate([cotangent_ref[b] for b in range(tile_blocks)], 1).astype(F32)
@@ -220,12 +254,40 @@
             fold = (rows[n] // span).astype(F32).astype(BF16)
             picked = pick_fold(fold, [gathered[:channels, inside], gathered[channels:, inside]])
             grad_columns_ref[:, lanes] = picked
-            returned = jnp.dot(weight_ref[k], picked, preferred_element_type=F32).astype(BF16)
-            source = table_row(source_ref, k)
-            fold = (source // span).astype(F32).astype(BF16)
-            places[:, lanes] = one_hot(source & (span - 1), span)
-            for f in range(folds):
-                values[f * half : (f + 1) * half, lanes] = mask_fold(fold, f, returned)
+            term = lax.dot_general(
+                columns_ref[:, lanes],
+                picked,
+                (((1,), (1,)), ((), ())),
+                preferred_element_type=F32,
+            )
+            row = (k % portion) * half
+            held[(k // portion) ^ here, row : row + half, :] = term
+    for n, ref in enumerate(portions):
+        ref[...] = held[n].astype(ref.dtype)
+    start = pl.multiple_of(lax.axis_index("chan") * half, half)
+    own = part_ref[pl.ds(start, half), :] + other_ref[pl.ds(start, half), :]
+    own = own / (1.0 + jnp.exp(-own))
+    for b in range(tile_blocks):
+        act_ref[b] = own[:, b * width : (b + 1) * width].astype(BF16)
+
+
+def input_grad_kernel(grad_columns_ref, source_ref, weight_ref, own_ref, *refs):
+    rims, (values, places) = refs[:-2], refs[-2:]
+    tile_blocks = own_ref.shape[0]
+    offsets, half, _ = weight_ref.shape
+    width = source_ref.shape[1]
+    span = 2 * width
+    folds = values.shape[0] // half
+    for k in range(offsets):
+        lanes = slice(k * width, (k + 1) * width)
+        returned = jnp.dot(
+            weight_ref[k], grad_columns_ref[:, lanes], preferred_element_type=F32
+        ).astype(BF16)
+        source = table_row(source_ref, k)
+        fold = (source // span).astype(F32).astype(BF16)
+        places[:, lanes] = one_hot(source & (span - 1), span)
+        for f in range(folds):
+            values[f * half : (f + 1) * half, lanes] = mask_fold(fold, f, returned)
     total = lax.dot_general(
         values[...], places[...], (((1,), (1,)), ((), ())), preferred_element_type=F32
     )
@@ -242,89 +304,51 @@
             place += 1
 
 
-def weight_grad_kernel(part_ref, other_ref, columns_ref, grad_columns_ref, act_ref, *refs):
-    portions, held = refs[:-1], refs[-1]
-    half = columns_ref.shape[0]
-    tile_blocks, _, width = act_ref.shape
-    offsets = columns_ref.shape[1] // width
-    portion = offsets // len(portions)
-    here = lax.axis_index("depth") if len(portions) > 1 else 0
-    for k in range(offsets):
-        lanes = slice(k * width, (k + 1) * width)
-        term = lax.dot_general(
-            columns_ref[:, lanes],
-            grad_columns_ref[:, lanes],
-            (((1,), (1,)), ((), ())),
-            preferred_element_type=F32,
-        )
-        row = (k % portion) * half
-        held[(k // portion) ^ here, row : row + half, :] = term
-    for n, ref in enumerate(portions):
-        ref[...] = held[n].astype(ref.dtype)
-    start = pl.multiple_of(lax.axis_index("chan") * half, half)
-    own = part_ref[pl.ds(start, half), :] + other_ref[pl.ds(start, half), :]
-    own = own / (1.0 + jnp.exp(-own))
-    for b in range(tile_blocks):
-        act_ref[b] = own[:, b * width : (b + 1) * width].astype(BF16)
-
-
-def tile_grad_kernel(swaps, halo_ref, own_ref, *refs):
-    received, (out_ref, total) = refs[:-2], refs[-2:]
-    total[...] = own_ref[...]
+def add_rims(swaps, halo_ref, total, received):
     for (axis, parity, _), ref in zip(swaps, received):
         group = direction(axis, parity)
         for b in range(ref.shape[0]):
             where = halo_ref[group, b]
             total[where] = total[where] + ref[b].astype(F32)
+
+
+def tile_grad_kernel(swaps, halo_ref, own_ref, *refs):
+    received, (out_ref, total) = refs[:-2], refs[-2:]
+    total[...] = own_ref[...]
+    add_rims(swaps, halo_ref, total, received)
     out_ref[...] = total[...].astype(BF16)
 
 
-def row_sum_kernel(keep_ref, crossed_ref, *refs):
-    outs, total = refs[:-1], refs[-1]
-    total[...] = keep_ref[...] + crossed_ref[...].astype(F32)
+def collect_kernel(swaps, halo_ref, own_ref, keep_ref, crossed_ref, *refs):
+    received, refs = refs[: len(swaps)], refs[len(swaps) :]
+    (grad_ref, share_ref, *sends), (total, terms) = refs[:-2], refs[-2:]
+    blocks, half, _ = own_ref.shape
+    terms[...] = keep_ref[...] + crossed_ref[...].astype(F32)
+    total[...] = own_ref[...]
+    add_rims(swaps, halo_ref, total, received)
+    for b in range(blocks):
+        grad_ref[b * half : (b + 1) * half, :] = total[b].astype(BF16)
     i = lax.axis_index("tile")
-    rows = outs[0].shape[0]
-    for d, ref in enumerate(outs):
-        start = pl.multiple_of((i ^ d) * rows, rows)
-        ref[...] = total[pl.ds(start, rows), :].astype(ref.dtype)
-
-
-def column_kernel(tile_rows, *refs):
-    grads, terms, (bulk_ref, shard_ref) = refs[:tile_rows], refs[tile_rows:-2], refs[-2:]
-    row = 0
-    for ref in grads:
-        for b in range(ref.shape[0]):
-            bulk_ref[row : row + ref.shape[1], :] = ref[b]
-            row += ref.shape[1]
-    total = terms[0][...]
-    for ref in terms[1:]:
-        total = total + ref[...].astype(F32)
+    rows = share_ref.shape[0]
+    for d, ref in enumerate((share_ref, *sends)):
+        share = terms[pl.ds(pl.multiple_of((i ^ d) * rows, rows), rows), :]
+        if d:
+            ref[: blocks * half, :] = grad_ref[...]
+            ref[blocks * half :, :] = share.astype(BF16)
+        else:
+            ref[...] = share
+
+
+def column_kernel(grad_ref, share_ref, *refs):
+    received, (bulk_ref, shard_ref) = refs[:-2], refs[-2:]
+    rows = grad_ref.shape[0]
+    bulk_ref[:rows, :] = grad_ref[...]
+    total = share_ref[...]
+    for d, ref in enumerate(received, 1):
+        bulk_ref[d * rows : (d + 1) * rows, :] = ref[:rows, :]
+        total = total + ref[rows:, :].astype(F32)
     shard_ref[...] = total.astype(BF16)
-    bulk_ref[row:, :] = shard_ref[...]
-
-
-def row_sum_kernel(keep_ref, crossed_ref, *refs):
-    outs, total = refs[:-1], refs[-1]
-    total[...] = keep_ref[...] + crossed_ref[...].astype(F32)
-    i = lax.axis_index("tile")
-    rows = outs[0].shape[0]
-    for d, ref in enumerate(outs):
-        start = pl.multiple_of((i ^ d) * rows, rows)
-        ref[...] = total[pl.ds(start, rows), :].astype(ref.dtype)
-
-
-def column_kernel(tile_rows, *refs):
-    grads, terms, (bulk_ref, shard_ref) = refs[:tile_rows], refs[tile_rows:-2], refs[-2:]
-    row = 0
-    for ref in grads:
-        for b in range(ref.shape[0]):
-            bulk_ref[row : row + ref.shape[1], :] = ref[b]
-            row += ref.shape[1]
-    total = terms[0][...]
-    for ref in terms[1:]:
-        total = total + ref[...].astype(F32)
-    shard_ref[...] = total.astype(BF16)
-    bulk_ref[row:, :] = shard_ref[...]
+    bulk_ref[(len(received) + 1) * rows :, :] = shard_ref[...]
 
 
 def spread_kernel(place_ref, own_ref, other_ref, out_ref, held):
@@ -441,13 +465,20 @@
 
         far_high = far_sums(range(tile_rows // 2, tile_rows))
         far_low = far_sums(range(tile_rows // 2))
-        near_low, near_high, place = pl.pallas_call(
+        near_low, near_high = pl.pallas_call(
             functools.partial(near_kernel, tile_rows, depths, tile_blocks),
-            out_shape=(shape(held_blocks, F32),) * 2 + (shape((log_count + 1,), jnp.int32),),
-            in_specs=[SMEM] * (2 + tile_rows) + [VMEM],
-            out_specs=(VMEM,) * 2 + (SMEM,),
-            compiler_params=PARAMS,
-        )(send, *near, far, log_blocks)
+            out_shape=(shape(held_blocks, F32),) * 2,
+            in_specs=[SMEM] * (1 + tile_rows) + [VMEM],
+            out_specs=(VMEM,) * 2,
+            compiler_params=PARAMS,
+        )(send, *near, log_blocks)
+        place = pl.pallas_call(
+            functools.partial(place_kernel, tile_rows, depths, tile_blocks),
+            out_shape=shape((log_count + 1,), jnp.int32),
+            in_specs=[SMEM] * (2 + tile_rows),
+            out_specs=SMEM,
+            compiler_params=PARAMS,
+        )(send, *near, far)
         add = functools.partial(
             pl.pallas_call,
             add_kernel,
@@ -460,6 +491,7 @@
             near_low, far_low
         )
         incoming = to_rows([*low, *high], tile_rows)
+        incoming, place = lax.optimization_barrier((incoming, place))
     else:
         pick_table = (
             send.reshape(-1)[:, None] == jnp.arange(log_count, dtype=jnp.int32)[None, :]
@@ -487,8 +519,15 @@
     received = swap_all(swaps, sends)
 
     pairs_total = padded * pair_slots
+    own_columns = pl.pallas_call(
+        functools.partial(own_columns_kernel, chunk),
+        out_shape=shape((half, pairs_total), BF16),
+        in_specs=[VMEM] * 2,
+        out_specs=VMEM,
+        compiler_params=PARAMS,
+    )(features, source_rows)
     part, columns = pl.pallas_call(
-        functools.partial(forward_kernel, len(swaps), chunk),
+        functools.partial(forward_kernel, tile_blocks // 2, chunk),
         out_shape=(shape((channels, own_total), F32), shape((half, pairs_total), BF16)),
         in_specs=[VMEM] * (4 + len(swaps)),
         out_specs=(VMEM, VMEM),
@@ -497,66 +536,56 @@
             pltpu.VMEM((span, pairs_total), BF16),
         ],
         compiler_params=PARAMS,
-    )(features, *received, source_rows, target_rows, w_rows_t)
+    )(own_columns, source_rows, target_rows, w_rows_t, *received)
     other = lax.ppermute(part, "chan", [(0, 1), (1, 0)])
 
-    grad_columns, own_grad, *rims = pl.pallas_call(
-        functools.partial(input_grad_kernel, chunk),
-        out_shape=(
-            shape((channels, pairs_total), BF16),
-            shape((tile_blocks, half, width), F32),
-        )
-        + (rim_shape,) * len(swaps),
-        in_specs=[VMEM] * 6,
-        out_specs=(VMEM,) * (2 + len(swaps)),
+    portions = depths if merged else 1
+    portion = (padded // portions * half, channels)
+    activations, grad_columns, keep, *cross = pl.pallas_call(
+        functools.partial(weight_grad_kernel, chunk),
+        out_shape=(block_shape, shape((channels, pairs_total), BF16), shape(portion, F32))
+        + (shape(portion, BF16),) * (portions - 1),
+        in_specs=[VMEM] * 5,
+        out_specs=(VMEM,) * (2 + portions),
+        scratch_shapes=[pltpu.VMEM((portions, *portion), F32)],
+        compiler_params=PARAMS,
+    )(part, other, cotangent_full, target_rows, columns)
+    scale = float(tile_count * pair_slots) ** (-0.5)
+    own_grad, *rims = pl.pallas_call(
+        input_grad_kernel,
+        out_shape=(shape((tile_blocks, half, width), F32),) + (rim_shape,) * len(swaps),
+        in_specs=[VMEM] * 3,
+        out_specs=(VMEM,) * (1 + len(swaps)),
         scratch_shapes=[
             pltpu.VMEM((held_total // 2 * half, pairs_total), BF16),
             pltpu.VMEM((span, pairs_total), BF16),
         ],
         compiler_params=PARAMS,
-    )(part, other, cotangent_full, source_rows, target_rows, w_rows)
+    )(grad_columns, source_rows, w_rows)
     returned = swap_all(swaps, rims)
-    portions = depths if merged else 1
-    portion = (padded // portions * half, channels)
-    activations, keep, *cross = pl.pallas_call(
-        weight_grad_kernel,
-        out_shape=(block_shape, shape(portion, F32)) + (shape(portion, BF16),) * (portions - 1),
-        in_specs=[VMEM] * 4,
-        out_specs=(VMEM,) * (1 + portions),
-        scratch_shapes=[pltpu.VMEM((portions, *portion), F32)],
-        compiler_params=PARAMS,
-    )(part, other, columns, grad_columns)
-    scale = float(tile_count * pair_slots) ** (-0.5)
-    if merged:
-        cross, returned = lax.optimization_barrier((cross, returned))
-    tile_grad = pl.pallas_call(
-        functools.partial(tile_grad_kernel, swaps),
-        out_shape=block_shape,
-        in_specs=[SMEM] + [VMEM] * (1 + len(swaps)),
-        out_specs=VMEM,
-        scratch_shapes=[pltpu.VMEM((tile_blocks, half, width), F32)],
-        compiler_params=PARAMS,
-    )(halo, own_grad, *returned)
-
     if merged:
         rows = portion[0] // tile_rows
-        row_terms = pl.pallas_call(
-            row_sum_kernel,
-            out_shape=(shape((rows, channels), F32),)
-            + (shape((rows, channels), BF16),) * (tile_rows - 1),
-            in_specs=[VMEM] * 2,
-            out_specs=(VMEM,) * tile_rows,
-            scratch_shapes=[pltpu.VMEM(portion, F32)],
-            compiler_params=PARAMS,
-        )(keep, across(cross[0]))
-        column_rows = tile_rows * tile_blocks * half
+        own_rows = tile_blocks * half
+        column_rows = tile_rows * own_rows
+        grad, share, *sends = pl.pallas_call(
+            functools.partial(collect_kernel, swaps),
+            out_shape=(shape((own_rows, width), BF16), shape((rows, channels), F32))
+            + (shape((own_rows + rows, width), BF16),) * (tile_rows - 1),
+            in_specs=[SMEM] + [VMEM] * (3 + len(swaps)),
+            out_specs=(VMEM,) * (1 + tile_rows),
+            scratch_shapes=[
+                pltpu.VMEM((tile_blocks, half, width), F32),
+                pltpu.VMEM(portion, F32),
+            ],
+            compiler_params=PARAMS,
+        )(halo, own_grad, keep, across(cross[0]), *returned)
         bulk, shard = pl.pallas_call(
-            functools.partial(column_kernel, tile_rows),
+            column_kernel,
             out_shape=(shape((column_rows + rows, channels), BF16), shape((rows, channels), BF16)),
-            in_specs=[VMEM] * (2 * tile_rows),
+            in_specs=[VMEM] * (1 + tile_rows),
             out_specs=(VMEM,) * 2,
             compiler_params=PARAMS,
-        )(*to_rows([tile_grad] * tile_rows, tile_rows), *to_rows(row_terms, tile_rows))
+        )(grad, *to_rows([share, *sends], tile_rows))
         other_bulk = across(bulk)
         shards = to_rows([shard] * tile_rows, tile_rows)
         last, other_bulk = lax.optimization_barrier((jnp.concatenate(shards[1:]), other_bulk))
@@ -577,6 +606,14 @@
             compiler_params=PARAMS,
         )(*shards, other_bulk, across(last))
     else:
+        tile_grad = pl.pallas_call(
+            functools.partial(tile_grad_kernel, swaps),
+            out_shape=block_shape,
+            in_specs=[SMEM] + [VMEM] * (1 + len(swaps)),
+            out_specs=VMEM,
+            scratch_shapes=[pltpu.VMEM((tile_blocks, half, width), F32)],
+            compiler_params=PARAMS,
+        )(halo, own_grad, *returned)
         back_blocks = jnp.dot(
             place_table.T,
             tile_grad.reshape(tile_blocks, half * width),

time: 85.4 us -> 84.2 us (0.986)
  starting transfers between devices: 39.4 us -> 33.7 us
  waiting for transfers between devices: 22.6 us -> 26.6 us
    ppermute x15 -> x12, starting transfers between devices: 24 us -> 18.1 us  [to_rows(): lax.ppermute(arrays[d], 'tile', xor_pairs(tile_rows, d))]
    ppermute x15 -> x12, waiting for transfers between devices: 14.8 us -> 18 us  [to_rows(): lax.ppermute(arrays[d], 'tile', xor_pairs(tile_rows, d))]
    pallas_call x6 -> x7, Pallas kernels: 9.02 us -> 10.6 us  [the longest x1 3.02 us: local(): pl.pallas_call(functools.partial(forward_kernel, tile_blocks // 2, chunk)...]
    pallas_call x1, Pallas kernels: 2.63 us -> 1.52 us  [local(): pl.pallas_call(functools.partial(near_kernel, tile_rows, depths, tile_blo...]
  transfers between devices with their start and end apart: 28 -> 25, of which waited for: 16 -> 13; matrix products, arithmetic and copies ran while one was open for 1% -> 1% of each run, Pallas kernels for 9% -> 10%
where the time goes in v3:
time: 84.2 us; the launch traced here: 84 us
  starting transfers between devices  33.7 us (40%)
  waiting for transfers between devices  26.6 us (32%)
  Pallas kernels  18 us (21%)
  local copies, waits for them, and re-layouts  2.68 us (3%)
  blocking collectives  2.03 us (2%)
  between operations  0.9 us (1%)
    ppermute x12, starting transfers between devices, to_rows(): lax.ppermute(arrays[d], 'tile', xor_pairs(tile_rows, d))  18.1 us
    ppermute x12, waiting for transfers between devices, to_rows(): lax.ppermute(arrays[d], 'tile', xor_pairs(tile_rows, d))  18 us
    ppermute x6, starting transfers between devices, swap_all(): lax.ppermute(array, axis, pairs)  8.67 us
    ppermute x6, starting transfers between devices, across(): return lax.ppermute(array, 'depth', [(0, 1), (1, 0)])  6.87 us
    ppermute x6, waiting for transfers between devices, across(): return lax.ppermute(array, 'depth', [(0, 1), (1, 0)])  5.38 us
    ppermute x6, waiting for transfers between devices, swap_all(): lax.ppermute(array, axis, pairs)  3.24 us
    pallas_call x1, Pallas kernels, local(): pl.pallas_call(functools.partial(forward_kernel, tile_blocks // 2, chunk)...  3.02 us
    pallas_call x1, Pallas kernels, local(): pl.pallas_call(functools.partial(weight_grad_kernel, chunk), out_shape=(b...  2.83 us
  transfers between devices with their start and end apart: 25, of which 13 were waited for; matrix products, arithmetic and copies ran while one was open for 1% of the time, Pallas kernels for 10%

profile of v3, /device:TPU:0, one launch (start us, length us, event | category | flops | bytes accessed | tf_op | source)
XLA Modules:
  0.0 84.0 jit_solution(10322234948322306314)
XLA Ops:
  0.6 3.1 %collective-permute-start = (s32[8,16]{1,0:T(8,128)}, s32[8,16]{1,0:T(8,128)S(1)}, u32[]{:S(2)}, u32[]{:S(2)}) collective-permute-start(s32[8,16]{1,0:T(8,128)} %bitcast.40), channel_id=1, source_target_pairs={{0,4},{4,0},{8,12},{12,8},{1,5},{5,1},{9,13},{13,9},{2,6},{6,2},{1... | collective-permute-start | bytes 1544 | tf_op jit(solution)/shard_map/ppermute | solution.py:389
  3.7 2.6 %collective-permute-start.1 = (s32[8,16]{1,0:T(8,128)}, s32[8,16]{1,0:T(8,128)S(1)}, u32[]{:S(2)}, u32[]{:S(2)}) collective-permute-start(s32[8,16]{1,0:T(8,128)} %bitcast.41), channel_id=1, source_target_pairs={{0,8},{4,12},{8,0},{12,4},{1,9},{5,13},{9,1},{13,5},{2,10},{6,14},... | collective-permute-start | bytes 1544 | tf_op jit(solution)/shard_map/ppermute | solution.py:389
  6.3 1.2 %copy-done.1 = bf16[1,64,64,128]{3,2,1,0:T(8,128)(2,1)S(1)} copy-done((bf16[1,64,64,128]{3,2,1,0:T(8,128)(2,1)S(1)}, bf16[1,64,64,128]{3,2,1,0:T(8,128)(2,1)}, u32[]{:S(2)}) %copy-start.1) | copy-done | bytes 1048600
  8.5 3.5 %collective-permute-done.2.refs_4_ = s32[8,16]{1,0:T(8,128)S(1)} collective-permute-done((s32[8,16]{1,0:T(8,128)}, s32[8,16]{1,0:T(8,128)S(1)}, u32[]{:S(2)}, u32[]{:S(2)}) %collective-permute-start.2) | collective-permute-done | bytes 544 | tf_op jit(solution)/shard_map/ppermute | solution.py:389
  12.0 1.6 %collective-permute-start.3 = (s32[4,8,16]{2,1,0:T(8,128)S(1)}, s32[4,8,16]{2,1,0:T(8,128)S(1)}, u32[]{:S(2)}, u32[]{:S(2)}) collective-permute-start(s32[4,8,16]{2,1,0:T(8,128)S(1)} %pad_add_fusion), channel_id=1, source_target_pairs={{0,2},{2,0},{1,3},{3,1},{4,6},{6,4},{5,7},{7,5},{8,10},{10,8},{9,1... | collective-permute-start | bytes 6152 | tf_op jit(solution)/shard_map/ppermute | solution.py:394
  14.3 1.5 %collective-permute-done.3.far_ref.refs_5_ = s32[4,8,16]{2,1,0:T(8,128)S(1)} collective-permute-done((s32[4,8,16]{2,1,0:T(8,128)S(1)}, s32[4,8,16]{2,1,0:T(8,128)S(1)}, u32[]{:S(2)}, u32[]{:S(2)}) %collective-permute-start.3) | collective-permute-done | bytes 2080 | tf_op jit(solution)/shard_map/ppermute | solution.py:394
  15.8 1.2 %shard_map.116 = bf16[8,64,128]{2,1,0:T(8,128)(2,1)S(1)} custom-call(s32[8,16]{1,0:T(8,128)S(1)} %bitcast.36, s32[4,8,16]{2,1,0:T(8,128)S(1)} %collective-permute-done.3.far_ref.refs_5_, bf16[64,64,128]{2,1,0:T(8,128)(2,1)S(1)} %shard_map.112.refs_5_.log_ref), custom_call_target="tpu_custom_call" | custom-call | tf_op jit(solution)/shard_map/pallas_call | solution.py:457
  17.0 1.6 %collective-permute-start.6 = (bf16[8,64,128]{2,1,0:T(8,128)(2,1)S(1)}, bf16[8,64,128]{2,1,0:T(8,128)(2,1)S(1)}, u32[]{:S(2)}, u32[]{:S(2)}) collective-permute-start(bf16[8,64,128]{2,1,0:T(8,128)(2,1)S(1)} %shard_map.116), channel_id=1, source_target_pairs={{0,2},{2,0},{1,3},{3,1},{4,6},{6,4},{5,7},{7,5},{8,10},{10,8},{9,1... | collective-permute-start | bytes 393224 | tf_op jit(solution)/shard_map/ppermute | solution.py:394
  18.6 1.2 %shard_map.114 = bf16[8,64,128]{2,1,0:T(8,128)(2,1)S(1)} custom-call(s32[8,16]{1,0:T(8,128)S(1)} %bitcast.37, s32[4,8,16]{2,1,0:T(8,128)S(1)} %collective-permute-done.3.far_ref.refs_5_, bf16[64,64,128]{2,1,0:T(8,128)(2,1)S(1)} %shard_map.112.refs_5_.log_ref), custom_call_target="tpu_custom_call" | custom-call | tf_op jit(solution)/shard_map/pallas_call | solution.py:457
  20.5 1.5 %shard_map.113 = (f32[8,64,128]{2,1,0:T(8,128)S(1)}, f32[8,64,128]{2,1,0:T(8,128)S(1)}) custom-call(s32[8,16]{1,0:T(8,128)S(1)} %bitcast.38, s32[8,16]{1,0:T(8,128)S(1)} %bitcast.43, s32[8,16]{1,0:T(8,128)S(1)} %collective-permute-done.refs_2_, s32[8,16]{1,0:T(8,128)S(1)} %collective-permute-done.1.refs_3_, s32[8,16]{1,0:T(8,128)S(1)} %collective-permute-done.2.refs_4_, ...), custom_call_target="tpu_custom_call" | custom-call | tf_op jit(solution)/shard_map/pallas_call | solution.py:468
  22.2 1.2 %collective-permute-start.8 = (bf16[4,64,128]{2,1,0:T(8,128)(2,1)S(1)}, bf16[4,64,128]{2,1,0:T(8,128)(2,1)S(1)}, u32[]{:S(2)}, u32[]{:S(2)}) collective-permute-start(bf16[4,64,128]{2,1,0:T(8,128)(2,1)S(1)} %get-tuple-element.46), channel_id=1, source_target_pairs={{0,12},{4,8},{8,4},{12,0},{1,13},{5,9},{9,5},{13,1},{2,14},{6,10},... | collective-permute-start | bytes 196616 | tf_op jit(solution)/shard_map/ppermute | solution.py:389
  23.4 1.5 %collective-permute-done.4.far_ref = bf16[8,64,128]{2,1,0:T(8,128)(2,1)S(1)} collective-permute-done((bf16[8,64,128]{2,1,0:T(8,128)(2,1)S(1)}, bf16[8,64,128]{2,1,0:T(8,128)(2,1)S(1)}, u32[]{:S(2)}, u32[]{:S(2)}) %collective-permute-start.4) | collective-permute-done | bytes 131104 | tf_op jit(solution)/shard_map/ppermute | solution.py:394
  25.8 2.0 %shard_map.118.place_ref = s32[65]{0:T(128)S(1)} custom-call(s32[8,16]{1,0:T(8,128)S(1)} %bitcast.39, s32[8,16]{1,0:T(8,128)S(1)} %bitcast.44, s32[8,16]{1,0:T(8,128)S(1)} %collective-permute-done.refs_2_, s32[8,16]{1,0:T(8,128)S(1)} %collective-permute-done.1.refs_3_, s32[8,16]{1,0:T(8,128)S(1)} %collective-permute-done.2.refs_4_, ...), custom_call_target="tpu_custom_call" | custom-call | tf_op jit(solution)/shard_map/pallas_call | solution.py:475
  30.5 1.3 %collective-permute-start.11 = (bf16[2,64,128]{2,1,0:T(8,128)(2,1)S(1)}, bf16[2,64,128]{2,1,0:T(8,128)(2,1)S(1)}, u32[]{:S(2)}, u32[]{:S(2)}) collective-permute-start(bf16[2,64,128]{2,1,0:T(8,128)(2,1)S(1)} %get-tuple-element.54), channel_id=1, source_target_pairs={{0,2},{2,0},{1,3},{3,1},{4,6},{6,4},{5,7},{7,5},{8,10},{10,8},{9,1... | collective-permute-start | bytes 98312 | tf_op jit(solution)/shard_map/ppermute | solution.py:383
  31.8 2.4 %collective-permute-start.9 = (bf16[2,64,128]{2,1,0:T(8,128)(2,1)S(1)}, bf16[2,64,128]{2,1,0:T(8,128)(2,1)S(1)}, u32[]{:S(2)}, u32[]{:S(2)}) collective-permute-start(bf16[2,64,128]{2,1,0:T(8,128)(2,1)S(1)} %get-tuple-element.52), channel_id=1, source_target_pairs={{0,4},{4,0},{8,12},{12,8},{1,5},{5,1},{9,13},{13,9},{2,6},{6,2},{1... | collective-permute-start | bytes 98312 | tf_op jit(solution)/shard_map/ppermute | solution.py:383
  36.1 3.0 %shard_map.121 = (f32[128,512]{1,0:T(8,128)S(1)}, bf16[64,3584]{1,0:T(8,128)(2,1)S(1)}) custom-call(bf16[64,3584]{1,0:T(8,128)(2,1)S(1)} %shard_map.120.refs_0_, s32[28,128]{1,0:T(8,128)S(1)} %pad.11.source_ref.refs_1_, s32[28,128]{1,0:T(8,128)S(1)} %pad.12.refs_2_.refs_3_, bf16[28,128,64]{2,1,0:T(8,128)(2,1)S(1)} %copy.13.refs_3_, ...), custom_call_target="tpu_custom_call" | custom-call | tf_op jit(solution)/shard_map/pallas_call | solution.py:529
  39.2 2.0 %all-gather = bf16[1,4,128,128]{3,2,1,0:T(8,128)(2,1)S(1)} all-gather(bf16[1,4,64,128]{3,2,1,0:T(8,128)(2,1)S(1)} %copy-done.4), channel_id=2, replica_groups=mesh['groups'=2,'tile'=4,'depth'=2,'chan'=2] {'chan'}, dimensions={2}, use_global_device_ids=true | all-gather | bytes 196608 | tf_op jit(solution)/shard_map/all_gather | solution.py:439
  41.2 2.8 %shard_map.122 = (bf16[4,64,128]{2,1,0:T(8,128)(2,1)}, bf16[128,3584]{1,0:T(8,128)(2,1)S(1)}, f32[896,128]{1,0:T(8,128)S(1)}, bf16[896,128]{1,0:T(8,128)(2,1)S(1)}) custom-call(f32[128,512]{1,0:T(8,128)S(1)} %get-tuple-element.55.refs_0_, f32[128,512]{1,0:T(8,128)S(1)} %collective-permute-done.12.refs_1_, bf16[4,128,128]{2,1,0:T(8,128)(2,1)S(1)} %bitcast.35, ...), custom_call_target="tpu_custom_call" | custom-call | tf_op jit(solution)/shard_map/pallas_call | solution.py:544
  44.6 1.5 %shard_map.123 = (f32[4,64,128]{2,1,0:T(8,128)S(1)}, bf16[2,64,128]{2,1,0:T(8,128)(2,1)S(1)}, bf16[2,64,128]{2,1,0:T(8,128)(2,1)S(1)}, bf16[2,64,128]{2,1,0:T(8,128)(2,1)S(1)}) custom-call(bf16[128,3584]{1,0:T(8,128)(2,1)S(1)} %get-tuple-element.59.grad_columns_ref, s32[28,128]{1,0:T(8,128)S(1)} %pad.11.source_ref.refs_1_, ...), custom_call_target="tpu_custom_call" | custom-call | tf_op jit(solution)/shard_map/pallas_call | solution.py:554
  46.1 2.1 %collective-permute-start.14 = (bf16[2,64,128]{2,1,0:T(8,128)(2,1)S(1)}, bf16[2,64,128]{2,1,0:T(8,128)(2,1)S(1)}, u32[]{:S(2)}, u32[]{:S(2)}) collective-permute-start(bf16[2,64,128]{2,1,0:T(8,128)(2,1)S(1)} %get-tuple-element.63), channel_id=1, source_target_pairs={{0,4},{4,0},{8,12},{12,8},{1,5},{5,1},{9,13},{13,9},{2,6},{6,2},{1... | collective-permute-start | bytes 98312 | tf_op jit(solution)/shard_map/ppermute | solution.py:383
  48.9 1.5 %collective-permute-start.16 = (bf16[2,64,128]{2,1,0:T(8,128)(2,1)S(1)}, bf16[2,64,128]{2,1,0:T(8,128)(2,1)S(1)}, u32[]{:S(2)}, u32[]{:S(2)}) collective-permute-start(bf16[2,64,128]{2,1,0:T(8,128)(2,1)S(1)} %get-tuple-element.65), channel_id=1, source_target_pairs={{0,2},{2,0},{1,3},{3,1},{4,6},{6,4},{5,7},{7,5},{8,10},{10,8},{9,1... | collective-permute-start | bytes 98312 | tf_op jit(solution)/shard_map/ppermute | solution.py:383
  50.4 2.4 %collective-permute-done.16.refs_2_ = bf16[2,64,128]{2,1,0:T(8,128)(2,1)S(1)} collective-permute-done((bf16[2,64,128]{2,1,0:T(8,128)(2,1)S(1)}, bf16[2,64,128]{2,1,0:T(8,128)(2,1)S(1)}, u32[]{:S(2)}, u32[]{:S(2)}) %collective-permute-start.16) | collective-permute-done | bytes 32800 | tf_op jit(solution)/shard_map/ppermute | solution.py:383
  53.6 3.2 %collective-permute-start.17 = (bf16[480,128]{1,0:T(8,128)(2,1)S(1)}, bf16[480,128]{1,0:T(8,128)(2,1)S(1)}, u32[]{:S(2)}, u32[]{:S(2)}) collective-permute-start(bf16[480,128]{1,0:T(8,128)(2,1)S(1)} %get-tuple-element.68), channel_id=1, source_target_pairs={{0,4},{4,0},{8,12},{12,8},{1,5},{5,1},{9,13},{13,9},{2,6},{6,2},{1... | collective-permute-start | bytes 368648 | tf_op jit(solution)/shard_map/ppermute | solution.py:389
  57.0 2.2 %collective-permute-start.19 = (bf16[480,128]{1,0:T(8,128)(2,1)S(1)}, bf16[480,128]{1,0:T(8,128)(2,1)S(1)}, u32[]{:S(2)}, u32[]{:S(2)}) collective-permute-start(bf16[480,128]{1,0:T(8,128)(2,1)S(1)} %get-tuple-element.70), channel_id=1, source_target_pairs={{0,12},{4,8},{8,4},{12,0},{1,13},{5,9},{9,5},{13,1},{2,14},{6,10},... | collective-permute-start | bytes 368648 | tf_op jit(solution)/shard_map/ppermute | solution.py:389
  59.3 1.7 %collective-permute-done.17.refs_0_ = bf16[480,128]{1,0:T(8,128)(2,1)S(1)} collective-permute-done((bf16[480,128]{1,0:T(8,128)(2,1)S(1)}, bf16[480,128]{1,0:T(8,128)(2,1)S(1)}, u32[]{:S(2)}, u32[]{:S(2)}) %collective-permute-start.17) | collective-permute-done | bytes 122912 | tf_op jit(solution)/shard_map/ppermute | solution.py:389
  61.0 6.9 %collective-permute-done.18.refs_1_ = bf16[480,128]{1,0:T(8,128)(2,1)S(1)} collective-permute-done((bf16[480,128]{1,0:T(8,128)(2,1)S(1)}, bf16[480,128]{1,0:T(8,128)(2,1)S(1)}, u32[]{:S(2)}, u32[]{:S(2)}) %collective-permute-start.18) | collective-permute-done | bytes 122912 | tf_op jit(solution)/shard_map/ppermute | solution.py:389
  69.1 2.2 %collective-permute-start.20 = (bf16[224,128]{1,0:T(8,128)(2,1)S(1)}, bf16[224,128]{1,0:T(8,128)(2,1)S(1)}, u32[]{:S(2)}, u32[]{:S(2)}) collective-permute-start(bf16[224,128]{1,0:T(8,128)(2,1)S(1)} %get-tuple-element.72.refs_0_), channel_id=1, source_target_pairs={{0,4},{4,0},{8,12},{12,8},{1,5},{5,1},{9,13},{13,9},{2,6},{6,2},{1... | collective-permute-start | bytes 172040 | tf_op jit(solution)/shard_map/ppermute | solution.py:389
  71.4 2.3 %collective-permute-start.22 = (bf16[224,128]{1,0:T(8,128)(2,1)S(1)}, bf16[224,128]{1,0:T(8,128)(2,1)S(1)}, u32[]{:S(2)}, u32[]{:S(2)}) collective-permute-start(bf16[224,128]{1,0:T(8,128)(2,1)S(1)} %get-tuple-element.72.refs_0_), channel_id=1, source_target_pairs={{0,12},{4,8},{8,4},{12,0},{1,13},{5,9},{9,5},{13,1},{2,14},{6,10},... | collective-permute-start | bytes 172040 | tf_op jit(solution)/shard_map/ppermute | solution.py:389
  73.7 3.1 %collective-permute-done.21.refs_2_ = bf16[224,128]{1,0:T(8,128)(2,1)S(1)} collective-permute-done((bf16[224,128]{1,0:T(8,128)(2,1)S(1)}, bf16[224,128]{1,0:T(8,128)(2,1)S(1)}, u32[]{:S(2)}, u32[]{:S(2)}) %collective-permute-start.21) | collective-permute-done | bytes 57376 | tf_op jit(solution)/shard_map/ppermute | solution.py:389
  77.5 1.4 %collective-permute-start.24 = (bf16[672,128]{1,0:T(8,128)(2,1)S(1)}, bf16[672,128]{1,0:T(8,128)(2,1)S(1)}, u32[]{:S(2)}, u32[]{:S(2)}) collective-permute-start(bf16[672,128]{1,0:T(8,128)(2,1)S(1)} %pad_maximum_fusion), channel_id=1, source_target_pairs={{0,2},{2,0},{1,3},{3,1},{4,6},{6,4},{5,7},{7,5},{8,10},{10,8},{9,1... | collective-permute-start | bytes 516104 | tf_op jit(solution)/shard_map/ppermute | solution.py:394
  78.9 1.6 %shard_map.126 = bf16[64,64,128]{2,1,0:T(8,128)(2,1)} custom-call(s32[65]{0:T(128)S(1)} %shard_map.118.place_ref, bf16[1248,128]{1,0:T(8,128)(2,1)S(1)} %get-tuple-element.71.own_ref, bf16[1248,128]{1,0:T(8,128)(2,1)S(1)} %collective-permute-done.23.other_ref.refs_4_), custom_call_target="tpu_custom_call" | custom-call | tf_op jit(solution)/shard_map/pallas_call | solution.py:592
  80.5 2.4 %collective-permute-done.24.refs_5_ = bf16[672,128]{1,0:T(8,128)(2,1)S(1)} collective-permute-done((bf16[672,128]{1,0:T(8,128)(2,1)S(1)}, bf16[672,128]{1,0:T(8,128)(2,1)S(1)}, u32[]{:S(2)}, u32[]{:S(2)}) %collective-permute-start.24) | collective-permute-done | bytes 172064 | tf_op jit(solution)/shard_map/ppermute | solution.py:394
  (62 shorter events, 13.0 us)
Async XLA Ops:
  0.6 25.1 %copy-start = (bf16[27,128,128]{2,1,0:T(8,128)(2,1)S(1)}, bf16[27,128,128]{2,1,0:T(8,128)(2,1)}, u32[]{:S(2)}) copy-start(bf16[27,128,128]{2,1,0:T(8,128)(2,1)} %param.16) | copy-start | bytes 2654212
  0.6 7.0 %collective-permute-start = (s32[8,16]{1,0:T(8,128)}, s32[8,16]{1,0:T(8,128)S(1)}, u32[]{:S(2)}, u32[]{:S(2)}) collective-permute-start(s32[8,16]{1,0:T(8,128)} %bitcast.40), channel_id=1, source_target_pairs={{0,4},{4,0},{8,12},{12,8},{1,5},{5,1},{9,13},{13,9},{2,6},{6,2},{1... | collective-permute-start | bytes 1544 | tf_op jit(solution)/shard_map/ppermute | solution.py:389
  3.7 4.7 %collective-permute-start.1 = (s32[8,16]{1,0:T(8,128)}, s32[8,16]{1,0:T(8,128)S(1)}, u32[]{:S(2)}, u32[]{:S(2)}) collective-permute-start(s32[8,16]{1,0:T(8,128)} %bitcast.41), channel_id=1, source_target_pairs={{0,8},{4,12},{8,0},{12,4},{1,9},{5,13},{9,1},{13,5},{2,10},{6,14},... | collective-permute-start | bytes 1544 | tf_op jit(solution)/shard_map/ppermute | solution.py:389
  6.3 5.6 %collective-permute-start.2 = (s32[8,16]{1,0:T(8,128)}, s32[8,16]{1,0:T(8,128)S(1)}, u32[]{:S(2)}, u32[]{:S(2)}) collective-permute-start(s32[8,16]{1,0:T(8,128)} %bitcast.42), channel_id=1, source_target_pairs={{0,12},{4,8},{8,4},{12,0},{1,13},{5,9},{9,5},{13,1},{2,14},{6,10},... | collective-permute-start | bytes 1544 | tf_op jit(solution)/shard_map/ppermute | solution.py:389
  6.3 1.2 %copy-start.1 = (bf16[1,64,64,128]{3,2,1,0:T(8,128)(2,1)S(1)}, bf16[1,64,64,128]{3,2,1,0:T(8,128)(2,1)}, u32[]{:S(2)}) copy-start(bf16[1,64,64,128]{3,2,1,0:T(8,128)(2,1)} %param.9) | copy-start | bytes 3145732
  7.6 4.3 %copy-start.3 = (s32[1,8,16]{2,1,0:T(8,128)S(1)}, s32[1,8,16]{2,1,0:T(8,128)}, u32[]{:S(2)}) copy-start(s32[1,8,16]{2,1,0:T(8,128)} %param.11) | copy-start | bytes 1540
  12.0 3.8 %collective-permute-start.3 = (s32[4,8,16]{2,1,0:T(8,128)S(1)}, s32[4,8,16]{2,1,0:T(8,128)S(1)}, u32[]{:S(2)}, u32[]{:S(2)}) collective-permute-start(s32[4,8,16]{2,1,0:T(8,128)S(1)} %pad_add_fusion), channel_id=1, source_target_pairs={{0,2},{2,0},{1,3},{3,1},{4,6},{6,4},{5,7},{7,5},{8,10},{10,8},{9,1... | collective-permute-start | bytes 6152 | tf_op jit(solution)/shard_map/ppermute | solution.py:394
  14.3 1.5 %copy-start.2 = (s32[1,8,16]{2,1,0:T(8,128)S(1)}, s32[1,8,16]{2,1,0:T(8,128)}, u32[]{:S(2)}) copy-start(s32[1,8,16]{2,1,0:T(8,128)} %param.10) | copy-start | bytes 1540
  17.0 3.4 %copy-start.5 = (s32[1,27,128]{2,0,1:T(1,128)S(1)}, s32[1,27,128]{2,0,1:T(1,128)}, u32[]{:S(2)}) copy-start(s32[1,27,128]{2,0,1:T(1,128)} %param.14) | copy-start | bytes 41476
  17.0 3.4 %copy-start.6 = (s32[1,27,128]{2,0,1:T(1,128)S(1)}, s32[1,27,128]{2,0,1:T(1,128)}, u32[]{:S(2)}) copy-start(s32[1,27,128]{2,0,1:T(1,128)} %param.13) | copy-start | bytes 41476
  17.0 5.0 %collective-permute-start.6 = (bf16[8,64,128]{2,1,0:T(8,128)(2,1)S(1)}, bf16[8,64,128]{2,1,0:T(8,128)(2,1)S(1)}, u32[]{:S(2)}, u32[]{:S(2)}) collective-permute-start(bf16[8,64,128]{2,1,0:T(8,128)(2,1)S(1)} %shard_map.116), channel_id=1, source_target_pairs={{0,2},{2,0},{1,3},{3,1},{4,6},{6,4},{5,7},{7,5},{8,10},{10,8},{9,1... | collective-permute-start | bytes 393224 | tf_op jit(solution)/shard_map/ppermute | solution.py:394
  19.8 5.0 %collective-permute-start.4 = (bf16[8,64,128]{2,1,0:T(8,128)(2,1)S(1)}, bf16[8,64,128]{2,1,0:T(8,128)(2,1)S(1)}, u32[]{:S(2)}, u32[]{:S(2)}) collective-permute-start(bf16[8,64,128]{2,1,0:T(8,128)(2,1)S(1)} %shard_map.114), channel_id=1, source_target_pairs={{0,2},{2,0},{1,3},{3,1},{4,6},{6,4},{5,7},{7,5},{8,10},{10,8},{9,1... | collective-permute-start | bytes 393224 | tf_op jit(solution)/shard_map/ppermute | solution.py:394
  22.1 5.8 %collective-permute-start.7 = (bf16[4,64,128]{2,1,0:T(8,128)(2,1)S(1)}, bf16[4,64,128]{2,1,0:T(8,128)(2,1)S(1)}, u32[]{:S(2)}, u32[]{:S(2)}) collective-permute-start(bf16[4,64,128]{2,1,0:T(8,128)(2,1)S(1)} %get-tuple-element.45), channel_id=1, source_target_pairs={{0,8},{4,12},{8,0},{12,4},{1,9},{5,13},{9,1},{13,5},{2,10},{6,14},... | collective-permute-start | bytes 196616 | tf_op jit(solution)/shard_map/ppermute | solution.py:389
  22.2 6.2 %collective-permute-start.8 = (bf16[4,64,128]{2,1,0:T(8,128)(2,1)S(1)}, bf16[4,64,128]{2,1,0:T(8,128)(2,1)S(1)}, u32[]{:S(2)}, u32[]{:S(2)}) collective-permute-start(bf16[4,64,128]{2,1,0:T(8,128)(2,1)S(1)} %get-tuple-element.46), channel_id=1, source_target_pairs={{0,12},{4,8},{8,4},{12,0},{1,13},{5,9},{9,5},{13,1},{2,14},{6,10},... | collective-permute-start | bytes 196616 | tf_op jit(solution)/shard_map/ppermute | solution.py:389
  24.9 4.3 %collective-permute-start.5 = (bf16[4,64,128]{2,1,0:T(8,128)(2,1)S(1)}, bf16[4,64,128]{2,1,0:T(8,128)(2,1)S(1)}, u32[]{:S(2)}, u32[]{:S(2)}) collective-permute-start(bf16[4,64,128]{2,1,0:T(8,128)(2,1)S(1)} %get-tuple-element.43), channel_id=1, source_target_pairs={{0,4},{4,0},{8,12},{12,8},{1,5},{5,1},{9,13},{13,9},{2,6},{6,2},{1... | collective-permute-start | bytes 196616 | tf_op jit(solution)/shard_map/ppermute | solution.py:389
  29.8 5.5 %collective-permute-start.10 = (bf16[2,64,128]{2,1,0:T(8,128)(2,1)S(1)}, bf16[2,64,128]{2,1,0:T(8,128)(2,1)S(1)}, u32[]{:S(2)}, u32[]{:S(2)}) collective-permute-start(bf16[2,64,128]{2,1,0:T(8,128)(2,1)S(1)} %get-tuple-element.53), channel_id=1, source_target_pairs={{4,8},{8,4},{5,9},{9,5},{6,10},{10,6},{7,11},{11,7},{20,24},{24,20... | collective-permute-start | bytes 98312 | tf_op jit(solution)/shard_map/ppermute | solution.py:383
  30.5 4.8 %collective-permute-start.11 = (bf16[2,64,128]{2,1,0:T(8,128)(2,1)S(1)}, bf16[2,64,128]{2,1,0:T(8,128)(2,1)S(1)}, u32[]{:S(2)}, u32[]{:S(2)}) collective-permute-start(bf16[2,64,128]{2,1,0:T(8,128)(2,1)S(1)} %get-tuple-element.54), channel_id=1, source_target_pairs={{0,2},{2,0},{1,3},{3,1},{4,6},{6,4},{5,7},{7,5},{8,10},{10,8},{9,1... | collective-permute-start | bytes 98312 | tf_op jit(solution)/shard_map/ppermute | solution.py:383
  31.8 4.3 %collective-permute-start.9 = (bf16[2,64,128]{2,1,0:T(8,128)(2,1)S(1)}, bf16[2,64,128]{2,1,0:T(8,128)(2,1)S(1)}, u32[]{:S(2)}, u32[]{:S(2)}) collective-permute-start(bf16[2,64,128]{2,1,0:T(8,128)(2,1)S(1)} %get-tuple-element.52), channel_id=1, source_target_pairs={{0,4},{4,0},{8,12},{12,8},{1,5},{5,1},{9,13},{13,9},{2,6},{6,2},{1... | collective-permute-start | bytes 98312 | tf_op jit(solution)/shard_map/ppermute | solution.py:383
  35.2 3.9 %copy-start.4 = (bf16[1,4,64,128]{3,2,1,0:T(8,128)(2,1)S(1)}, bf16[1,4,64,128]{3,2,1,0:T(8,128)(2,1)}, u32[]{:S(2)}) copy-start(bf16[1,4,64,128]{3,2,1,0:T(8,128)(2,1)} %param.17) | copy-start | bytes 196612
  39.1 2.1 %collective-permute-start.12 = (f32[128,512]{1,0:T(8,128)S(1)}, f32[128,512]{1,0:T(8,128)S(1)}, u32[]{:S(2)}, u32[]{:S(2)}) collective-permute-start(f32[128,512]{1,0:T(8,128)S(1)} %get-tuple-element.55.refs_0_), channel_id=1, source_target_pairs={{0,1},{1,0},{2,3},{3,2},{4,5},{5,4},{6,7},{7,6},{8,9},{9,8},{10,11... | collective-permute-start | bytes 786440 | tf_op jit(solution)/shard_map/ppermute | solution.py:540
  44.0 8.8 %collective-permute-start.13 = (bf16[896,128]{1,0:T(8,128)(2,1)S(1)}, bf16[896,128]{1,0:T(8,128)(2,1)S(1)}, u32[]{:S(2)}, u32[]{:S(2)}) collective-permute-start(bf16[896,128]{1,0:T(8,128)(2,1)S(1)} %get-tuple-element.62), channel_id=1, source_target_pairs={{0,2},{2,0},{1,3},{3,1},{4,6},{6,4},{5,7},{7,5},{8,10},{10,8},{9,1... | collective-permute-start | bytes 688136 | tf_op jit(solution)/shard_map/ppermute | solution.py:394
  46.1 4.3 %collective-permute-start.14 = (bf16[2,64,128]{2,1,0:T(8,128)(2,1)S(1)}, bf16[2,64,128]{2,1,0:T(8,128)(2,1)S(1)}, u32[]{:S(2)}, u32[]{:S(2)}) collective-permute-start(bf16[2,64,128]{2,1,0:T(8,128)(2,1)S(1)} %get-tuple-element.63), channel_id=1, source_target_pairs={{0,4},{4,0},{8,12},{12,8},{1,5},{5,1},{9,13},{13,9},{2,6},{6,2},{1... | collective-permute-start | bytes 98312 | tf_op jit(solution)/shard_map/ppermute | solution.py:383
  48.2 2.2 %collective-permute-start.15 = (bf16[2,64,128]{2,1,0:T(8,128)(2,1)S(1)}, bf16[2,64,128]{2,1,0:T(8,128)(2,1)S(1)}, u32[]{:S(2)}, u32[]{:S(2)}) collective-permute-start(bf16[2,64,128]{2,1,0:T(8,128)(2,1)S(1)} %get-tuple-element.64), channel_id=1, source_target_pairs={{4,8},{8,4},{5,9},{9,5},{6,10},{10,6},{7,11},{11,7},{20,24},{24,20... | collective-permute-start | bytes 98312 | tf_op jit(solution)/shard_map/ppermute | solution.py:383
  48.9 4.0 %collective-permute-start.16 = (bf16[2,64,128]{2,1,0:T(8,128)(2,1)S(1)}, bf16[2,64,128]{2,1,0:T(8,128)(2,1)S(1)}, u32[]{:S(2)}, u32[]{:S(2)}) collective-permute-start(bf16[2,64,128]{2,1,0:T(8,128)(2,1)S(1)} %get-tuple-element.65), channel_id=1, source_target_pairs={{0,2},{2,0},{1,3},{3,1},{4,6},{6,4},{5,7},{7,5},{8,10},{10,8},{9,1... | collective-permute-start | bytes 98312 | tf_op jit(solution)/shard_map/ppermute | solution.py:383
  53.6 7.4 %collective-permute-start.17 = (bf16[480,128]{1,0:T(8,128)(2,1)S(1)}, bf16[480,128]{1,0:T(8,128)(2,1)S(1)}, u32[]{:S(2)}, u32[]{:S(2)}) collective-permute-start(bf16[480,128]{1,0:T(8,128)(2,1)S(1)} %get-tuple-element.68), channel_id=1, source_target_pairs={{0,4},{4,0},{8,12},{12,8},{1,5},{5,1},{9,13},{13,9},{2,6},{6,2},{1... | collective-permute-start | bytes 368648 | tf_op jit(solution)/shard_map/ppermute | solution.py:389
  56.8 11.1 %collective-permute-start.18 = (bf16[480,128]{1,0:T(8,128)(2,1)S(1)}, bf16[480,128]{1,0:T(8,128)(2,1)S(1)}, u32[]{:S(2)}, u32[]{:S(2)}) collective-permute-start(bf16[480,128]{1,0:T(8,128)(2,1)S(1)} %get-tuple-element.69), channel_id=1, source_target_pairs={{0,8},{4,12},{8,0},{12,4},{1,9},{5,13},{9,1},{13,5},{2,10},{6,14},... | collective-permute-start | bytes 368648 | tf_op jit(solution)/shard_map/ppermute | solution.py:389
  57.0 10.9 %collective-permute-start.19 = (bf16[480,128]{1,0:T(8,128)(2,1)S(1)}, bf16[480,128]{1,0:T(8,128)(2,1)S(1)}, u32[]{:S(2)}, u32[]{:S(2)}) collective-permute-start(bf16[480,128]{1,0:T(8,128)(2,1)S(1)} %get-tuple-element.70), channel_id=1, source_target_pairs={{0,12},{4,8},{8,4},{12,0},{1,13},{5,9},{9,5},{13,1},{2,14},{6,10},... | collective-permute-start | bytes 368648 | tf_op jit(solution)/shard_map/ppermute | solution.py:389
  68.0 9.5 %collective-permute-start.23 = (bf16[1248,128]{1,0:T(8,128)(2,1)S(1)}, bf16[1248,128]{1,0:T(8,128)(2,1)S(1)}, u32[]{:S(2)}, u32[]{:S(2)}) collective-permute-start(bf16[1248,128]{1,0:T(8,128)(2,1)S(1)} %get-tuple-element.71.own_ref), channel_id=1, source_target_pairs={{0,2},{2,0},{1,3},{3,1},{4,6},{6,4},{5,7},{7,5},{8,10},{10,8},{9,1... | collective-permute-start | bytes 958472 | tf_op jit(solution)/shard_map/ppermute | solution.py:394
  69.1 4.6 %collective-permute-start.20 = (bf16[224,128]{1,0:T(8,128)(2,1)S(1)}, bf16[224,128]{1,0:T(8,128)(2,1)S(1)}, u32[]{:S(2)}, u32[]{:S(2)}) collective-permute-start(bf16[224,128]{1,0:T(8,128)(2,1)S(1)} %get-tuple-element.72.refs_0_), channel_id=1, source_target_pairs={{0,4},{4,0},{8,12},{12,8},{1,5},{5,1},{9,13},{13,9},{2,6},{6,2},{1... | collective-permute-start | bytes 172040 | tf_op jit(solution)/shard_map/ppermute | solution.py:389
  71.3 5.5 %collective-permute-start.21 = (bf16[224,128]{1,0:T(8,128)(2,1)S(1)}, bf16[224,128]{1,0:T(8,128)(2,1)S(1)}, u32[]{:S(2)}, u32[]{:S(2)}) collective-permute-start(bf16[224,128]{1,0:T(8,128)(2,1)S(1)} %get-tuple-element.72.refs_0_), channel_id=1, source_target_pairs={{0,8},{4,12},{8,0},{12,4},{1,9},{5,13},{9,1},{13,5},{2,10},{6,14},... | collective-permute-start | bytes 172040 | tf_op jit(solution)/shard_map/ppermute | solution.py:389
  71.4 6.1 %collective-permute-start.22 = (bf16[224,128]{1,0:T(8,128)(2,1)S(1)}, bf16[224,128]{1,0:T(8,128)(2,1)S(1)}, u32[]{:S(2)}, u32[]{:S(2)}) collective-permute-start(bf16[224,128]{1,0:T(8,128)(2,1)S(1)} %get-tuple-element.72.refs_0_), channel_id=1, source_target_pairs={{0,12},{4,8},{8,4},{12,0},{1,13},{5,9},{9,5},{13,1},{2,14},{6,10},... | collective-permute-start | bytes 172040 | tf_op jit(solution)/shard_map/ppermute | solution.py:389
  77.5 5.5 %collective-permute-start.24 = (bf16[672,128]{1,0:T(8,128)(2,1)S(1)}, bf16[672,128]{1,0:T(8,128)(2,1)S(1)}, u32[]{:S(2)}, u32[]{:S(2)}) collective-permute-start(bf16[672,128]{1,0:T(8,128)(2,1)S(1)} %pad_maximum_fusion), channel_id=1, source_target_pairs={{0,2},{2,0},{1,3},{3,1},{4,6},{6,4},{5,7},{7,5},{8,10},{10,8},{9,1... | collective-permute-start | bytes 516104 | tf_op jit(solution)/shard_map/ppermute | solution.py:394
  (2 other events, 1.3 us)

commit v4 on v3

--- a/solution.py
+++ b/solution.py
@@ -339,30 +339,34 @@
             ref[...] = share
 
 
-def column_kernel(grad_ref, share_ref, *refs):
+def column_kernel(early, share_ref, *refs):
     received, (bulk_ref, shard_ref) = refs[:-2], refs[-2:]
-    rows = grad_ref.shape[0]
-    bulk_ref[:rows, :] = grad_ref[...]
+    rows = received[0].shape[0] - share_ref.shape[0]
     total = share_ref[...]
-    for d, ref in enumerate(received, 1):
-        bulk_ref[d * rows : (d + 1) * rows, :] = ref[:rows, :]
+    for d, ref in enumerate(received):
         total = total + ref[rows:, :].astype(F32)
+        if d >= early:
+            bulk_ref[(d - early) * rows : (d - early + 1) * rows, :] = ref[:rows, :]
     shard_ref[...] = total.astype(BF16)
-    bulk_ref[(len(received) + 1) * rows :, :] = shard_ref[...]
-
-
-def spread_kernel(place_ref, own_ref, other_ref, out_ref, held):
-    rows = held.shape[0] // 2
+    bulk_ref[(len(received) - early) * rows :, :] = shard_ref[...]
+
+
+def spread_kernel(place_ref, *refs):
+    parts, (out_ref, held) = refs[:-2], refs[-2:]
     height = out_ref.shape[1]
-    held[:rows, :] = own_ref[:rows, :]
-    held[rows:, :] = other_ref[:rows, :]
+    rows = parts[0].shape[0]
+    first = 0
+    for n, ref in enumerate(parts):
+        count = rows if n % 3 < 2 else held.shape[0] // 2 - 2 * rows
+        held[first : first + count, :] = ref[:count, :]
+        first += count
     for b in range(out_ref.shape[0]):
-        first = pl.multiple_of(place_ref[b] * height, height)
-        out_ref[b] = held[pl.ds(first, height), :]
+        start = pl.multiple_of(place_ref[b] * height, height)
+        out_ref[b] = held[pl.ds(start, height), :]
 
 
 def weight_kernel(scale, tile_rows, *refs):
-    near, (bulk_ref, far_ref, out_ref, held) = refs[:tile_rows], refs[tile_rows:]
+    near, (bulk_ref, *far), (out_ref, held) = refs[:tile_rows], refs[tile_rows:-2], refs[-2:]
     i, j = lax.axis_index("tile"), lax.axis_index("depth")
     rows = near[0].shape[0]
     for jx in range(2):
@@ -372,7 +376,7 @@
             elif d == 0:
                 shard = bulk_ref[bulk_ref.shape[0] - rows :, :]
             else:
-                shard = far_ref[(d - 1) * rows : d * rows, :]
+                shard = far[d - 1][...]
             start = pl.multiple_of(((j ^ jx) * tile_rows + (i ^ d)) * rows, rows)
             held[pl.ds(start, rows), :] = shard.astype(F32) * scale
     out_ref[...] = held[: out_ref.shape[0], :]
@@ -579,32 +583,39 @@
             ],
             compiler_params=PARAMS,
         )(halo, own_grad, keep, across(cross[0]), *returned)
+        received = to_rows([share, *sends], tile_rows)
+        early = [across(grad), across(received[1])]
+        received, early = lax.optimization_barrier((received, early))
         bulk, shard = pl.pallas_call(
-            column_kernel,
-            out_shape=(shape((column_rows + rows, channels), BF16), shape((rows, channels), BF16)),
-            in_specs=[VMEM] * (1 + tile_rows),
+            functools.partial(column_kernel, 1),
+            out_shape=(
+                shape((column_rows - 2 * own_rows + rows, channels), BF16),
+                shape((rows, channels), BF16),
+            ),
+            in_specs=[VMEM] * tile_rows,
             out_specs=(VMEM,) * 2,
             compiler_params=PARAMS,
-        )(grad, *to_rows([share, *sends], tile_rows))
+        )(*received)
         other_bulk = across(bulk)
         shards = to_rows([shard] * tile_rows, tile_rows)
-        last, other_bulk = lax.optimization_barrier((jnp.concatenate(shards[1:]), other_bulk))
         grad_log = pl.pallas_call(
             spread_kernel,
             out_shape=shape((log_count, half, width), BF16),
-            in_specs=[SMEM] + [VMEM] * 2,
+            in_specs=[SMEM] + [VMEM] * 6,
             out_specs=VMEM,
             scratch_shapes=[pltpu.VMEM((2 * column_rows, width), BF16)],
             compiler_params=PARAMS,
-        )(place, bulk, other_bulk)
+        )(place, grad, received[1], bulk, *early, other_bulk)
+        far_shards = [across(part) for part in shards[1:]]
+        far_shards, grad_log = lax.optimization_barrier((far_shards, grad_log))
         grad_weight = pl.pallas_call(
             functools.partial(weight_kernel, scale, tile_rows),
             out_shape=shape((offsets * half, channels), F32),
-            in_specs=[VMEM] * (tile_rows + 2),
+            in_specs=[VMEM] * (2 * tile_rows),
             out_specs=VMEM,
             scratch_shapes=[pltpu.VMEM((padded * half, channels), F32)],
             compiler_params=PARAMS,
-        )(*shards, other_bulk, across(last))
+        )(*shards, other_bulk, *far_shards)
     else:
         tile_grad = pl.pallas_call(
             functools.partial(tile_grad_kernel, swaps),

time: 84.2 us -> 83.5 us (level)
  waiting for transfers between devices: 26.6 us -> 22.2 us
  starting transfers between devices: 33.7 us -> 37.5 us
    ppermute x12, waiting for transfers between devices: 18 us -> 10.7 us  [to_rows(): lax.ppermute(arrays[d], 'tile', xor_pairs(tile_rows, d))]
    ppermute x6 -> x10, starting transfers between devices: 6.87 us -> 10.6 us  [across(): return lax.ppermute(array, 'depth', [(0, 1), (1, 0)])]
    ppermute x6 -> x10, waiting for transfers between devices: 5.38 us -> 8.31 us  [across(): return lax.ppermute(array, 'depth', [(0, 1), (1, 0)])]
  transfers between devices with their start and end apart: 25 -> 29, of which waited for: 13 -> 14; matrix products, arithmetic and copies ran while one was open for 1% -> 1% of each run, Pallas kernels for 10% -> 10%
where the time goes in v4:
time: 83.5 us; the launch traced here: 83.3 us
  starting transfers between devices  37.5 us (45%)
  waiting for transfers between devices  22.2 us (27%)
  Pallas kernels  17.9 us (21%)
  local copies, waits for them, and re-layouts  2.68 us (3%)
  blocking collectives  2.03 us (2%)
  between operations  0.9 us (1%)
    ppermute x12, starting transfers between devices, to_rows(): lax.ppermute(arrays[d], 'tile', xor_pairs(tile_rows, d))  18.1 us
    ppermute x12, waiting for transfers between devices, to_rows(): lax.ppermute(arrays[d], 'tile', xor_pairs(tile_rows, d))  10.7 us
    ppermute x10, starting transfers between devices, across(): return lax.ppermute(array, 'depth', [(0, 1), (1, 0)])  10.6 us
    ppermute x6, starting transfers between devices, swap_all(): lax.ppermute(array, axis, pairs)  8.67 us
    ppermute x10, waiting for transfers between devices, across(): return lax.ppermute(array, 'depth', [(0, 1), (1, 0)])  8.31 us
    ppermute x6, waiting for transfers between devices, swap_all(): lax.ppermute(array, axis, pairs)  3.24 us
    pallas_call x1, Pallas kernels, local(): pl.pallas_call(functools.partial(forward_kernel, tile_blocks // 2, chunk)...  3.02 us
    pallas_call x1, Pallas kernels, local(): pl.pallas_call(functools.partial(weight_grad_kernel, chunk), out_shape=(b...  2.83 us
  transfers between devices with their start and end apart: 29, of which 14 were waited for; matrix products, arithmetic and copies ran while one was open for 1% of the time, Pallas kernels for 10%

profile of v4, /device:TPU:0, one launch (start us, length us, event | category | flops | bytes accessed | tf_op | source)
XLA Modules:
  0.0 83.3 jit_solution(10451255264926624447)
XLA Ops:
  0.6 3.1 %collective-permute-start = (s32[8,16]{1,0:T(8,128)}, s32[8,16]{1,0:T(8,128)S(1)}, u32[]{:S(2)}, u32[]{:S(2)}) collective-permute-start(s32[8,16]{1,0:T(8,128)} %bitcast.40), channel_id=1, source_target_pairs={{0,4},{4,0},{8,12},{12,8},{1,5},{5,1},{9,13},{13,9},{2,6},{6,2},{1... | collective-permute-start | bytes 1544 | tf_op jit(solution)/shard_map/ppermute | solution.py:393
  3.7 2.6 %collective-permute-start.1 = (s32[8,16]{1,0:T(8,128)}, s32[8,16]{1,0:T(8,128)S(1)}, u32[]{:S(2)}, u32[]{:S(2)}) collective-permute-start(s32[8,16]{1,0:T(8,128)} %bitcast.41), channel_id=1, source_target_pairs={{0,8},{4,12},{8,0},{12,4},{1,9},{5,13},{9,1},{13,5},{2,10},{6,14},... | collective-permute-start | bytes 1544 | tf_op jit(solution)/shard_map/ppermute | solution.py:393
  6.3 1.2 %copy-done.1 = bf16[1,64,64,128]{3,2,1,0:T(8,128)(2,1)S(1)} copy-done((bf16[1,64,64,128]{3,2,1,0:T(8,128)(2,1)S(1)}, bf16[1,64,64,128]{3,2,1,0:T(8,128)(2,1)}, u32[]{:S(2)}) %copy-start.1) | copy-done | bytes 1048600
  8.5 3.5 %collective-permute-done.2.refs_4_ = s32[8,16]{1,0:T(8,128)S(1)} collective-permute-done((s32[8,16]{1,0:T(8,128)}, s32[8,16]{1,0:T(8,128)S(1)}, u32[]{:S(2)}, u32[]{:S(2)}) %collective-permute-start.2) | collective-permute-done | bytes 544 | tf_op jit(solution)/shard_map/ppermute | solution.py:393
  12.0 1.6 %collective-permute-start.3 = (s32[4,8,16]{2,1,0:T(8,128)S(1)}, s32[4,8,16]{2,1,0:T(8,128)S(1)}, u32[]{:S(2)}, u32[]{:S(2)}) collective-permute-start(s32[4,8,16]{2,1,0:T(8,128)S(1)} %pad_add_fusion), channel_id=1, source_target_pairs={{0,2},{2,0},{1,3},{3,1},{4,6},{6,4},{5,7},{7,5},{8,10},{10,8},{9,1... | collective-permute-start | bytes 6152 | tf_op jit(solution)/shard_map/ppermute | solution.py:398
  14.3 1.5 %collective-permute-done.3.far_ref.refs_5_ = s32[4,8,16]{2,1,0:T(8,128)S(1)} collective-permute-done((s32[4,8,16]{2,1,0:T(8,128)S(1)}, s32[4,8,16]{2,1,0:T(8,128)S(1)}, u32[]{:S(2)}, u32[]{:S(2)}) %collective-permute-start.3) | collective-permute-done | bytes 2080 | tf_op jit(solution)/shard_map/ppermute | solution.py:398
  15.8 1.2 %shard_map.116 = bf16[8,64,128]{2,1,0:T(8,128)(2,1)S(1)} custom-call(s32[8,16]{1,0:T(8,128)S(1)} %bitcast.36, s32[4,8,16]{2,1,0:T(8,128)S(1)} %collective-permute-done.3.far_ref.refs_5_, bf16[64,64,128]{2,1,0:T(8,128)(2,1)S(1)} %shard_map.112.refs_5_.log_ref), custom_call_target="tpu_custom_call" | custom-call | tf_op jit(solution)/shard_map/pallas_call | solution.py:461
  17.0 1.6 %collective-permute-start.6 = (bf16[8,64,128]{2,1,0:T(8,128)(2,1)S(1)}, bf16[8,64,128]{2,1,0:T(8,128)(2,1)S(1)}, u32[]{:S(2)}, u32[]{:S(2)}) collective-permute-start(bf16[8,64,128]{2,1,0:T(8,128)(2,1)S(1)} %shard_map.116), channel_id=1, source_target_pairs={{0,2},{2,0},{1,3},{3,1},{4,6},{6,4},{5,7},{7,5},{8,10},{10,8},{9,1... | collective-permute-start | bytes 393224 | tf_op jit(solution)/shard_map/ppermute | solution.py:398
  18.6 1.2 %shard_map.114 = bf16[8,64,128]{2,1,0:T(8,128)(2,1)S(1)} custom-call(s32[8,16]{1,0:T(8,128)S(1)} %bitcast.37, s32[4,8,16]{2,1,0:T(8,128)S(1)} %collective-permute-done.3.far_ref.refs_5_, bf16[64,64,128]{2,1,0:T(8,128)(2,1)S(1)} %shard_map.112.refs_5_.log_ref), custom_call_target="tpu_custom_call" | custom-call | tf_op jit(solution)/shard_map/pallas_call | solution.py:461
  20.5 1.5 %shard_map.113 = (f32[8,64,128]{2,1,0:T(8,128)S(1)}, f32[8,64,128]{2,1,0:T(8,128)S(1)}) custom-call(s32[8,16]{1,0:T(8,128)S(1)} %bitcast.38, s32[8,16]{1,0:T(8,128)S(1)} %bitcast.43, s32[8,16]{1,0:T(8,128)S(1)} %collective-permute-done.refs_2_, s32[8,16]{1,0:T(8,128)S(1)} %collective-permute-done.1.refs_3_, s32[8,16]{1,0:T(8,128)S(1)} %collective-permute-done.2.refs_4_, ...), custom_call_target="tpu_custom_call" | custom-call | tf_op jit(solution)/shard_map/pallas_call | solution.py:472
  23.4 1.5 %collective-permute-done.4.far_ref = bf16[8,64,128]{2,1,0:T(8,128)(2,1)S(1)} collective-permute-done((bf16[8,64,128]{2,1,0:T(8,128)(2,1)S(1)}, bf16[8,64,128]{2,1,0:T(8,128)(2,1)S(1)}, u32[]{:S(2)}, u32[]{:S(2)}) %collective-permute-start.4) | collective-permute-done | bytes 131104 | tf_op jit(solution)/shard_map/ppermute | solution.py:398
  25.8 2.0 %shard_map.118.place_ref = s32[65]{0:T(128)S(1)} custom-call(s32[8,16]{1,0:T(8,128)S(1)} %bitcast.39, s32[8,16]{1,0:T(8,128)S(1)} %bitcast.44, s32[8,16]{1,0:T(8,128)S(1)} %collective-permute-done.refs_2_, s32[8,16]{1,0:T(8,128)S(1)} %collective-permute-done.1.refs_3_, s32[8,16]{1,0:T(8,128)S(1)} %collective-permute-done.2.refs_4_, ...), custom_call_target="tpu_custom_call" | custom-call | tf_op jit(solution)/shard_map/pallas_call | solution.py:479
  30.5 1.3 %collective-permute-start.11 = (bf16[2,64,128]{2,1,0:T(8,128)(2,1)S(1)}, bf16[2,64,128]{2,1,0:T(8,128)(2,1)S(1)}, u32[]{:S(2)}, u32[]{:S(2)}) collective-permute-start(bf16[2,64,128]{2,1,0:T(8,128)(2,1)S(1)} %get-tuple-element.62), channel_id=1, source_target_pairs={{0,2},{2,0},{1,3},{3,1},{4,6},{6,4},{5,7},{7,5},{8,10},{10,8},{9,1... | collective-permute-start | bytes 98312 | tf_op jit(solution)/shard_map/ppermute | solution.py:387
  31.8 2.4 %collective-permute-start.9 = (bf16[2,64,128]{2,1,0:T(8,128)(2,1)S(1)}, bf16[2,64,128]{2,1,0:T(8,128)(2,1)S(1)}, u32[]{:S(2)}, u32[]{:S(2)}) collective-permute-start(bf16[2,64,128]{2,1,0:T(8,128)(2,1)S(1)} %get-tuple-element.60), channel_id=1, source_target_pairs={{0,4},{4,0},{8,12},{12,8},{1,5},{5,1},{9,13},{13,9},{2,6},{6,2},{1... | collective-permute-start | bytes 98312 | tf_op jit(solution)/shard_map/ppermute | solution.py:387
  36.1 3.0 %shard_map.121 = (f32[128,512]{1,0:T(8,128)S(1)}, bf16[64,3584]{1,0:T(8,128)(2,1)S(1)}) custom-call(bf16[64,3584]{1,0:T(8,128)(2,1)S(1)} %shard_map.120.refs_0_, s32[28,128]{1,0:T(8,128)S(1)} %pad.11.source_ref.refs_1_, s32[28,128]{1,0:T(8,128)S(1)} %pad.12.refs_2_.refs_3_, bf16[28,128,64]{2,1,0:T(8,128)(2,1)S(1)} %copy.13.refs_3_, ...), custom_call_target="tpu_custom_call" | custom-call | tf_op jit(solution)/shard_map/pallas_call | solution.py:533
  39.2 2.0 %all-gather = bf16[1,4,128,128]{3,2,1,0:T(8,128)(2,1)S(1)} all-gather(bf16[1,4,64,128]{3,2,1,0:T(8,128)(2,1)S(1)} %copy-done.4), channel_id=2, replica_groups=mesh['groups'=2,'tile'=4,'depth'=2,'chan'=2] {'chan'}, dimensions={2}, use_global_device_ids=true | all-gather | bytes 196608 | tf_op jit(solution)/shard_map/all_gather | solution.py:443
  41.2 2.8 %shard_map.122 = (bf16[4,64,128]{2,1,0:T(8,128)(2,1)}, bf16[128,3584]{1,0:T(8,128)(2,1)S(1)}, f32[896,128]{1,0:T(8,128)S(1)}, bf16[896,128]{1,0:T(8,128)(2,1)S(1)}) custom-call(f32[128,512]{1,0:T(8,128)S(1)} %get-tuple-element.63.refs_0_, f32[128,512]{1,0:T(8,128)S(1)} %collective-permute-done.12.refs_1_, bf16[4,128,128]{2,1,0:T(8,128)(2,1)S(1)} %bitcast.35, ...), custom_call_target="tpu_custom_call" | custom-call | tf_op jit(solution)/shard_map/pallas_call | solution.py:548
  44.6 1.5 %shard_map.123 = (f32[4,64,128]{2,1,0:T(8,128)S(1)}, bf16[2,64,128]{2,1,0:T(8,128)(2,1)S(1)}, bf16[2,64,128]{2,1,0:T(8,128)(2,1)S(1)}, bf16[2,64,128]{2,1,0:T(8,128)(2,1)S(1)}) custom-call(bf16[128,3584]{1,0:T(8,128)(2,1)S(1)} %get-tuple-element.66.grad_columns_ref, s32[28,128]{1,0:T(8,128)S(1)} %pad.11.source_ref.refs_1_, ...), custom_call_target="tpu_custom_call" | custom-call | tf_op jit(solution)/shard_map/pallas_call | solution.py:558
  46.1 2.1 %collective-permute-start.14 = (bf16[2,64,128]{2,1,0:T(8,128)(2,1)S(1)}, bf16[2,64,128]{2,1,0:T(8,128)(2,1)S(1)}, u32[]{:S(2)}, u32[]{:S(2)}) collective-permute-start(bf16[2,64,128]{2,1,0:T(8,128)(2,1)S(1)} %get-tuple-element.70), channel_id=1, source_target_pairs={{0,4},{4,0},{8,12},{12,8},{1,5},{5,1},{9,13},{13,9},{2,6},{6,2},{1... | collective-permute-start | bytes 98312 | tf_op jit(solution)/shard_map/ppermute | solution.py:387
  48.9 1.5 %collective-permute-start.16 = (bf16[2,64,128]{2,1,0:T(8,128)(2,1)S(1)}, bf16[2,64,128]{2,1,0:T(8,128)(2,1)S(1)}, u32[]{:S(2)}, u32[]{:S(2)}) collective-permute-start(bf16[2,64,128]{2,1,0:T(8,128)(2,1)S(1)} %get-tuple-element.72), channel_id=1, source_target_pairs={{0,2},{2,0},{1,3},{3,1},{4,6},{6,4},{5,7},{7,5},{8,10},{10,8},{9,1... | collective-permute-start | bytes 98312 | tf_op jit(solution)/shard_map/ppermute | solution.py:387
  50.4 2.4 %collective-permute-done.16.refs_2_ = bf16[2,64,128]{2,1,0:T(8,128)(2,1)S(1)} collective-permute-done((bf16[2,64,128]{2,1,0:T(8,128)(2,1)S(1)}, bf16[2,64,128]{2,1,0:T(8,128)(2,1)S(1)}, u32[]{:S(2)}, u32[]{:S(2)}) %collective-permute-start.16) | collective-permute-done | bytes 32800 | tf_op jit(solution)/shard_map/ppermute | solution.py:387
  53.6 3.3 %collective-permute-start.17 = (bf16[480,128]{1,0:T(8,128)(2,1)S(1)}, bf16[480,128]{1,0:T(8,128)(2,1)S(1)}, u32[]{:S(2)}, u32[]{:S(2)}) collective-permute-start(bf16[480,128]{1,0:T(8,128)(2,1)S(1)} %get-tuple-element.74), channel_id=1, source_target_pairs={{0,4},{4,0},{8,12},{12,8},{1,5},{5,1},{9,13},{13,9},{2,6},{6,2},{1... | collective-permute-start | bytes 368648 | tf_op jit(solution)/shard_map/ppermute | solution.py:393
  57.0 2.3 %collective-permute-start.19 = (bf16[480,128]{1,0:T(8,128)(2,1)S(1)}, bf16[480,128]{1,0:T(8,128)(2,1)S(1)}, u32[]{:S(2)}, u32[]{:S(2)}) collective-permute-start(bf16[480,128]{1,0:T(8,128)(2,1)S(1)} %get-tuple-element.76), channel_id=1, source_target_pairs={{0,12},{4,8},{8,4},{12,0},{1,13},{5,9},{9,5},{13,1},{2,14},{6,10},... | collective-permute-start | bytes 368648 | tf_op jit(solution)/shard_map/ppermute | solution.py:393
  59.3 1.7 %collective-permute-done.17.refs_0_.refs_1_ = bf16[480,128]{1,0:T(8,128)(2,1)S(1)} collective-permute-done((bf16[480,128]{1,0:T(8,128)(2,1)S(1)}, bf16[480,128]{1,0:T(8,128)(2,1)S(1)}, u32[]{:S(2)}, u32[]{:S(2)}) %collective-permute-start.17) | collective-permute-done | bytes 122912 | tf_op jit(solution)/shard_map/ppermute | solution.py:393
  63.0 3.6 %collective-permute-done.20.refs_3_ = bf16[256,128]{1,0:T(8,128)(2,1)S(1)} collective-permute-done((bf16[256,128]{1,0:T(8,128)(2,1)S(1)}, bf16[256,128]{1,0:T(8,128)(2,1)S(1)}, u32[]{:S(2)}, u32[]{:S(2)}) %collective-permute-start.20) | collective-permute-done | bytes 65568 | tf_op jit(solution)/shard_map/ppermute | solution.py:398
  66.6 1.3 %collective-permute-done.18.refs_1_ = bf16[480,128]{1,0:T(8,128)(2,1)S(1)} collective-permute-done((bf16[480,128]{1,0:T(8,128)(2,1)S(1)}, bf16[480,128]{1,0:T(8,128)(2,1)S(1)}, u32[]{:S(2)}, u32[]{:S(2)}) %collective-permute-start.18) | collective-permute-done | bytes 122912 | tf_op jit(solution)/shard_map/ppermute | solution.py:393
  69.1 2.2 %collective-permute-start.22 = (bf16[224,128]{1,0:T(8,128)(2,1)S(1)}, bf16[224,128]{1,0:T(8,128)(2,1)S(1)}, u32[]{:S(2)}, u32[]{:S(2)}) collective-permute-start(bf16[224,128]{1,0:T(8,128)(2,1)S(1)} %get-tuple-element.82.refs_0_), channel_id=1, source_target_pairs={{0,4},{4,0},{8,12},{12,8},{1,5},{5,1},{9,13},{13,9},{2,6},{6,2},{1... | collective-permute-start | bytes 172040 | tf_op jit(solution)/shard_map/ppermute | solution.py:393
  71.4 2.3 %collective-permute-start.26 = (bf16[224,128]{1,0:T(8,128)(2,1)S(1)}, bf16[224,128]{1,0:T(8,128)(2,1)S(1)}, u32[]{:S(2)}, u32[]{:S(2)}) collective-permute-start(bf16[224,128]{1,0:T(8,128)(2,1)S(1)} %get-tuple-element.82.refs_0_), channel_id=1, source_target_pairs={{0,12},{4,8},{8,4},{12,0},{1,13},{5,9},{9,5},{13,1},{2,14},{6,10},... | collective-permute-start | bytes 172040 | tf_op jit(solution)/shard_map/ppermute | solution.py:393
  74.8 2.0 %collective-permute-done.24.refs_2_ = bf16[224,128]{1,0:T(8,128)(2,1)S(1)} collective-permute-done((bf16[224,128]{1,0:T(8,128)(2,1)S(1)}, bf16[224,128]{1,0:T(8,128)(2,1)S(1)}, u32[]{:S(2)}, u32[]{:S(2)}) %collective-permute-start.24) | collective-permute-done | bytes 57376 | tf_op jit(solution)/shard_map/ppermute | solution.py:393
  76.8 1.3 %collective-permute-start.25 = (bf16[224,128]{1,0:T(8,128)(2,1)S(1)}, bf16[224,128]{1,0:T(8,128)(2,1)S(1)}, u32[]{:S(2)}, u32[]{:S(2)}) collective-permute-start(bf16[224,128]{1,0:T(8,128)(2,1)S(1)} %collective-permute-done.24.refs_2_), channel_id=1, source_target_pairs={{0,2},{2,0},{1,3},{3,1},{4,6},{6,4},{5,7},{7,5},{8,10},{10,8},{9,1... | collective-permute-start | bytes 172040 | tf_op jit(solution)/shard_map/ppermute | solution.py:398
  78.8 1.6 %shard_map.126 = bf16[64,64,128]{2,1,0:T(8,128)(2,1)} custom-call(s32[65]{0:T(128)S(1)} %shard_map.118.place_ref, bf16[256,128]{1,0:T(8,128)(2,1)S(1)} %get-tuple-element.77.refs_0_, bf16[480,128]{1,0:T(8,128)(2,1)S(1)} %collective-permute-done.17.refs_0_.refs_1_, bf16[736,128]{1,0:T(8,128)(2,1)S(1)} %get-tuple-element.84.refs_2_, ...), custom_call_target="tpu_custom_call" | custom-call | tf_op jit(solution)/shard_map/pallas_call | solution.py:601
  81.0 1.3 %collective-permute-done.27.refs_7_ = bf16[224,128]{1,0:T(8,128)(2,1)S(1)} collective-permute-done((bf16[224,128]{1,0:T(8,128)(2,1)S(1)}, bf16[224,128]{1,0:T(8,128)(2,1)S(1)}, u32[]{:S(2)}, u32[]{:S(2)}) %collective-permute-start.27) | collective-permute-done | bytes 57376 | tf_op jit(solution)/shard_map/ppermute | solution.py:398
  (69 shorter events, 18.0 us)
Async XLA Ops:
  0.6 25.1 %copy-start = (bf16[27,128,128]{2,1,0:T(8,128)(2,1)S(1)}, bf16[27,128,128]{2,1,0:T(8,128)(2,1)}, u32[]{:S(2)}) copy-start(bf16[27,128,128]{2,1,0:T(8,128)(2,1)} %param.16) | copy-start | bytes 2654212
  0.6 7.0 %collective-permute-start = (s32[8,16]{1,0:T(8,128)}, s32[8,16]{1,0:T(8,128)S(1)}, u32[]{:S(2)}, u32[]{:S(2)}) collective-permute-start(s32[8,16]{1,0:T(8,128)} %bitcast.40), channel_id=1, source_target_pairs={{0,4},{4,0},{8,12},{12,8},{1,5},{5,1},{9,13},{13,9},{2,6},{6,2},{1... | collective-permute-start | bytes 1544 | tf_op jit(solution)/shard_map/ppermute | solution.py:393
  3.7 4.7 %collective-permute-start.1 = (s32[8,16]{1,0:T(8,128)}, s32[8,16]{1,0:T(8,128)S(1)}, u32[]{:S(2)}, u32[]{:S(2)}) collective-permute-start(s32[8,16]{1,0:T(8,128)} %bitcast.41), channel_id=1, source_target_pairs={{0,8},{4,12},{8,0},{12,4},{1,9},{5,13},{9,1},{13,5},{2,10},{6,14},... | collective-permute-start | bytes 1544 | tf_op jit(solution)/shard_map/ppermute | solution.py:393
  6.3 5.6 %collective-permute-start.2 = (s32[8,16]{1,0:T(8,128)}, s32[8,16]{1,0:T(8,128)S(1)}, u32[]{:S(2)}, u32[]{:S(2)}) collective-permute-start(s32[8,16]{1,0:T(8,128)} %bitcast.42), channel_id=1, source_target_pairs={{0,12},{4,8},{8,4},{12,0},{1,13},{5,9},{9,5},{13,1},{2,14},{6,10},... | collective-permute-start | bytes 1544 | tf_op jit(solution)/shard_map/ppermute | solution.py:393
  7.6 4.3 %copy-start.3 = (s32[1,8,16]{2,1,0:T(8,128)S(1)}, s32[1,8,16]{2,1,0:T(8,128)}, u32[]{:S(2)}) copy-start(s32[1,8,16]{2,1,0:T(8,128)} %param.11) | copy-start | bytes 1540
  12.0 3.8 %collective-permute-start.3 = (s32[4,8,16]{2,1,0:T(8,128)S(1)}, s32[4,8,16]{2,1,0:T(8,128)S(1)}, u32[]{:S(2)}, u32[]{:S(2)}) collective-permute-start(s32[4,8,16]{2,1,0:T(8,128)S(1)} %pad_add_fusion), channel_id=1, source_target_pairs={{0,2},{2,0},{1,3},{3,1},{4,6},{6,4},{5,7},{7,5},{8,10},{10,8},{9,1... | collective-permute-start | bytes 6152 | tf_op jit(solution)/shard_map/ppermute | solution.py:398
  17.0 5.0 %collective-permute-start.6 = (bf16[8,64,128]{2,1,0:T(8,128)(2,1)S(1)}, bf16[8,64,128]{2,1,0:T(8,128)(2,1)S(1)}, u32[]{:S(2)}, u32[]{:S(2)}) collective-permute-start(bf16[8,64,128]{2,1,0:T(8,128)(2,1)S(1)} %shard_map.116), channel_id=1, source_target_pairs={{0,2},{2,0},{1,3},{3,1},{4,6},{6,4},{5,7},{7,5},{8,10},{10,8},{9,1... | collective-permute-start | bytes 393224 | tf_op jit(solution)/shard_map/ppermute | solution.py:398
  19.8 5.0 %collective-permute-start.4 = (bf16[8,64,128]{2,1,0:T(8,128)(2,1)S(1)}, bf16[8,64,128]{2,1,0:T(8,128)(2,1)S(1)}, u32[]{:S(2)}, u32[]{:S(2)}) collective-permute-start(bf16[8,64,128]{2,1,0:T(8,128)(2,1)S(1)} %shard_map.114), channel_id=1, source_target_pairs={{0,2},{2,0},{1,3},{3,1},{4,6},{6,4},{5,7},{7,5},{8,10},{10,8},{9,1... | collective-permute-start | bytes 393224 | tf_op jit(solution)/shard_map/ppermute | solution.py:398
  22.1 5.8 %collective-permute-start.7 = (bf16[4,64,128]{2,1,0:T(8,128)(2,1)S(1)}, bf16[4,64,128]{2,1,0:T(8,128)(2,1)S(1)}, u32[]{:S(2)}, u32[]{:S(2)}) collective-permute-start(bf16[4,64,128]{2,1,0:T(8,128)(2,1)S(1)} %get-tuple-element.53), channel_id=1, source_target_pairs={{0,8},{4,12},{8,0},{12,4},{1,9},{5,13},{9,1},{13,5},{2,10},{6,14},... | collective-permute-start | bytes 196616 | tf_op jit(solution)/shard_map/ppermute | solution.py:393
  22.2 6.2 %collective-permute-start.8 = (bf16[4,64,128]{2,1,0:T(8,128)(2,1)S(1)}, bf16[4,64,128]{2,1,0:T(8,128)(2,1)S(1)}, u32[]{:S(2)}, u32[]{:S(2)}) collective-permute-start(bf16[4,64,128]{2,1,0:T(8,128)(2,1)S(1)} %get-tuple-element.54), channel_id=1, source_target_pairs={{0,12},{4,8},{8,4},{12,0},{1,13},{5,9},{9,5},{13,1},{2,14},{6,10},... | collective-permute-start | bytes 196616 | tf_op jit(solution)/shard_map/ppermute | solution.py:393
  24.9 4.3 %collective-permute-start.5 = (bf16[4,64,128]{2,1,0:T(8,128)(2,1)S(1)}, bf16[4,64,128]{2,1,0:T(8,128)(2,1)S(1)}, u32[]{:S(2)}, u32[]{:S(2)}) collective-permute-start(bf16[4,64,128]{2,1,0:T(8,128)(2,1)S(1)} %get-tuple-element.51), channel_id=1, source_target_pairs={{0,4},{4,0},{8,12},{12,8},{1,5},{5,1},{9,13},{13,9},{2,6},{6,2},{1... | collective-permute-start | bytes 196616 | tf_op jit(solution)/shard_map/ppermute | solution.py:393
  29.8 5.5 %collective-permute-start.10 = (bf16[2,64,128]{2,1,0:T(8,128)(2,1)S(1)}, bf16[2,64,128]{2,1,0:T(8,128)(2,1)S(1)}, u32[]{:S(2)}, u32[]{:S(2)}) collective-permute-start(bf16[2,64,128]{2,1,0:T(8,128)(2,1)S(1)} %get-tuple-element.61), channel_id=1, source_target_pairs={{4,8},{8,4},{5,9},{9,5},{6,10},{10,6},{7,11},{11,7},{20,24},{24,20... | collective-permute-start | bytes 98312 | tf_op jit(solution)/shard_map/ppermute | solution.py:387
  30.5 4.8 %collective-permute-start.11 = (bf16[2,64,128]{2,1,0:T(8,128)(2,1)S(1)}, bf16[2,64,128]{2,1,0:T(8,128)(2,1)S(1)}, u32[]{:S(2)}, u32[]{:S(2)}) collective-permute-start(bf16[2,64,128]{2,1,0:T(8,128)(2,1)S(1)} %get-tuple-element.62), channel_id=1, source_target_pairs={{0,2},{2,0},{1,3},{3,1},{4,6},{6,4},{5,7},{7,5},{8,10},{10,8},{9,1... | collective-permute-start | bytes 98312 | tf_op jit(solution)/shard_map/ppermute | solution.py:387
  31.8 4.3 %collective-permute-start.9 = (bf16[2,64,128]{2,1,0:T(8,128)(2,1)S(1)}, bf16[2,64,128]{2,1,0:T(8,128)(2,1)S(1)}, u32[]{:S(2)}, u32[]{:S(2)}) collective-permute-start(bf16[2,64,128]{2,1,0:T(8,128)(2,1)S(1)} %get-tuple-element.60), channel_id=1, source_target_pairs={{0,4},{4,0},{8,12},{12,8},{1,5},{5,1},{9,13},{13,9},{2,6},{6,2},{1... | collective-permute-start | bytes 98312 | tf_op jit(solution)/shard_map/ppermute | solution.py:387
  35.2 3.9 %copy-start.4 = (bf16[1,4,64,128]{3,2,1,0:T(8,128)(2,1)S(1)}, bf16[1,4,64,128]{3,2,1,0:T(8,128)(2,1)}, u32[]{:S(2)}) copy-start(bf16[1,4,64,128]{3,2,1,0:T(8,128)(2,1)} %param.17) | copy-start | bytes 196612
  39.1 2.1 %collective-permute-start.12 = (f32[128,512]{1,0:T(8,128)S(1)}, f32[128,512]{1,0:T(8,128)S(1)}, u32[]{:S(2)}, u32[]{:S(2)}) collective-permute-start(f32[128,512]{1,0:T(8,128)S(1)} %get-tuple-element.63.refs_0_), channel_id=1, source_target_pairs={{0,1},{1,0},{2,3},{3,2},{4,5},{5,4},{6,7},{7,6},{8,9},{9,8},{10,11... | collective-permute-start | bytes 786440 | tf_op jit(solution)/shard_map/ppermute | solution.py:544
  44.0 8.8 %collective-permute-start.13 = (bf16[896,128]{1,0:T(8,128)(2,1)S(1)}, bf16[896,128]{1,0:T(8,128)(2,1)S(1)}, u32[]{:S(2)}, u32[]{:S(2)}) collective-permute-start(bf16[896,128]{1,0:T(8,128)(2,1)S(1)} %get-tuple-element.69), channel_id=1, source_target_pairs={{0,2},{2,0},{1,3},{3,1},{4,6},{6,4},{5,7},{7,5},{8,10},{10,8},{9,1... | collective-permute-start | bytes 688136 | tf_op jit(solution)/shard_map/ppermute | solution.py:398
  46.1 4.3 %collective-permute-start.14 = (bf16[2,64,128]{2,1,0:T(8,128)(2,1)S(1)}, bf16[2,64,128]{2,1,0:T(8,128)(2,1)S(1)}, u32[]{:S(2)}, u32[]{:S(2)}) collective-permute-start(bf16[2,64,128]{2,1,0:T(8,128)(2,1)S(1)} %get-tuple-element.70), channel_id=1, source_target_pairs={{0,4},{4,0},{8,12},{12,8},{1,5},{5,1},{9,13},{13,9},{2,6},{6,2},{1... | collective-permute-start | bytes 98312 | tf_op jit(solution)/shard_map/ppermute | solution.py:387
  48.2 2.2 %collective-permute-start.15 = (bf16[2,64,128]{2,1,0:T(8,128)(2,1)S(1)}, bf16[2,64,128]{2,1,0:T(8,128)(2,1)S(1)}, u32[]{:S(2)}, u32[]{:S(2)}) collective-permute-start(bf16[2,64,128]{2,1,0:T(8,128)(2,1)S(1)} %get-tuple-element.71), channel_id=1, source_target_pairs={{4,8},{8,4},{5,9},{9,5},{6,10},{10,6},{7,11},{11,7},{20,24},{24,20... | collective-permute-start | bytes 98312 | tf_op jit(solution)/shard_map/ppermute | solution.py:387
  48.9 4.0 %collective-permute-start.16 = (bf16[2,64,128]{2,1,0:T(8,128)(2,1)S(1)}, bf16[2,64,128]{2,1,0:T(8,128)(2,1)S(1)}, u32[]{:S(2)}, u32[]{:S(2)}) collective-permute-start(bf16[2,64,128]{2,1,0:T(8,128)(2,1)S(1)} %get-tuple-element.72), channel_id=1, source_target_pairs={{0,2},{2,0},{1,3},{3,1},{4,6},{6,4},{5,7},{7,5},{8,10},{10,8},{9,1... | collective-permute-start | bytes 98312 | tf_op jit(solution)/shard_map/ppermute | solution.py:387
  53.6 7.4 %collective-permute-start.17 = (bf16[480,128]{1,0:T(8,128)(2,1)S(1)}, bf16[480,128]{1,0:T(8,128)(2,1)S(1)}, u32[]{:S(2)}, u32[]{:S(2)}) collective-permute-start(bf16[480,128]{1,0:T(8,128)(2,1)S(1)} %get-tuple-element.74), channel_id=1, source_target_pairs={{0,4},{4,0},{8,12},{12,8},{1,5},{5,1},{9,13},{13,9},{2,6},{6,2},{1... | collective-permute-start | bytes 368648 | tf_op jit(solution)/shard_map/ppermute | solution.py:393
  56.8 11.1 %collective-permute-start.18 = (bf16[480,128]{1,0:T(8,128)(2,1)S(1)}, bf16[480,128]{1,0:T(8,128)(2,1)S(1)}, u32[]{:S(2)}, u32[]{:S(2)}) collective-permute-start(bf16[480,128]{1,0:T(8,128)(2,1)S(1)} %get-tuple-element.75), channel_id=1, source_target_pairs={{0,8},{4,12},{8,0},{12,4},{1,9},{5,13},{9,1},{13,5},{2,10},{6,14},... | collective-permute-start | bytes 368648 | tf_op jit(solution)/shard_map/ppermute | solution.py:393
  57.0 10.9 %collective-permute-start.19 = (bf16[480,128]{1,0:T(8,128)(2,1)S(1)}, bf16[480,128]{1,0:T(8,128)(2,1)S(1)}, u32[]{:S(2)}, u32[]{:S(2)}) collective-permute-start(bf16[480,128]{1,0:T(8,128)(2,1)S(1)} %get-tuple-element.76), channel_id=1, source_target_pairs={{0,12},{4,8},{8,4},{12,0},{1,13},{5,9},{9,5},{13,1},{2,14},{6,10},... | collective-permute-start | bytes 368648 | tf_op jit(solution)/shard_map/ppermute | solution.py:393
  61.0 6.9 %collective-permute-start.21 = (bf16[480,128]{1,0:T(8,128)(2,1)S(1)}, bf16[480,128]{1,0:T(8,128)(2,1)S(1)}, u32[]{:S(2)}, u32[]{:S(2)}) collective-permute-start(bf16[480,128]{1,0:T(8,128)(2,1)S(1)} %collective-permute-done.17.refs_0_.refs_1_), channel_id=1, source_target_pairs={{0,2},{2,0},{1,3},{3,1},{4,6},{6,4},{5,7},{7,5},{8,10},{10,8},{9,1... | collective-permute-start | bytes 368648 | tf_op jit(solution)/shard_map/ppermute | solution.py:398
  62.1 4.5 %collective-permute-start.20 = (bf16[256,128]{1,0:T(8,128)(2,1)S(1)}, bf16[256,128]{1,0:T(8,128)(2,1)S(1)}, u32[]{:S(2)}, u32[]{:S(2)}) collective-permute-start(bf16[256,128]{1,0:T(8,128)(2,1)S(1)} %get-tuple-element.77.refs_0_), channel_id=1, source_target_pairs={{0,2},{2,0},{1,3},{3,1},{4,6},{6,4},{5,7},{7,5},{8,10},{10,8},{9,1... | collective-permute-start | bytes 196616 | tf_op jit(solution)/shard_map/ppermute | solution.py:398
  68.0 10.9 %collective-permute-start.28 = (bf16[736,128]{1,0:T(8,128)(2,1)S(1)}, bf16[736,128]{1,0:T(8,128)(2,1)S(1)}, u32[]{:S(2)}, u32[]{:S(2)}) collective-permute-start(bf16[736,128]{1,0:T(8,128)(2,1)S(1)} %get-tuple-element.84.refs_2_), channel_id=1, source_target_pairs={{0,2},{2,0},{1,3},{3,1},{4,6},{6,4},{5,7},{7,5},{8,10},{10,8},{9,1... | collective-permute-start | bytes 565256 | tf_op jit(solution)/shard_map/ppermute | solution.py:398
  69.1 4.6 %collective-permute-start.22 = (bf16[224,128]{1,0:T(8,128)(2,1)S(1)}, bf16[224,128]{1,0:T(8,128)(2,1)S(1)}, u32[]{:S(2)}, u32[]{:S(2)}) collective-permute-start(bf16[224,128]{1,0:T(8,128)(2,1)S(1)} %get-tuple-element.82.refs_0_), channel_id=1, source_target_pairs={{0,4},{4,0},{8,12},{12,8},{1,5},{5,1},{9,13},{13,9},{2,6},{6,2},{1... | collective-permute-start | bytes 172040 | tf_op jit(solution)/shard_map/ppermute | solution.py:393
  71.3 5.5 %collective-permute-start.24 = (bf16[224,128]{1,0:T(8,128)(2,1)S(1)}, bf16[224,128]{1,0:T(8,128)(2,1)S(1)}, u32[]{:S(2)}, u32[]{:S(2)}) collective-permute-start(bf16[224,128]{1,0:T(8,128)(2,1)S(1)} %get-tuple-element.82.refs_0_), channel_id=1, source_target_pairs={{0,8},{4,12},{8,0},{12,4},{1,9},{5,13},{9,1},{13,5},{2,10},{6,14},... | collective-permute-start | bytes 172040 | tf_op jit(solution)/shard_map/ppermute | solution.py:393
  71.4 6.7 %collective-permute-start.26 = (bf16[224,128]{1,0:T(8,128)(2,1)S(1)}, bf16[224,128]{1,0:T(8,128)(2,1)S(1)}, u32[]{:S(2)}, u32[]{:S(2)}) collective-permute-start(bf16[224,128]{1,0:T(8,128)(2,1)S(1)} %get-tuple-element.82.refs_0_), channel_id=1, source_target_pairs={{0,12},{4,8},{8,4},{12,0},{1,13},{5,9},{9,5},{13,1},{2,14},{6,10},... | collective-permute-start | bytes 172040 | tf_op jit(solution)/shard_map/ppermute | solution.py:393
  73.7 6.8 %collective-permute-start.23 = (bf16[224,128]{1,0:T(8,128)(2,1)S(1)}, bf16[224,128]{1,0:T(8,128)(2,1)S(1)}, u32[]{:S(2)}, u32[]{:S(2)}) collective-permute-start(bf16[224,128]{1,0:T(8,128)(2,1)S(1)} %collective-permute-done.22.refs_1_), channel_id=1, source_target_pairs={{0,2},{2,0},{1,3},{3,1},{4,6},{6,4},{5,7},{7,5},{8,10},{10,8},{9,1... | collective-permute-start | bytes 172040 | tf_op jit(solution)/shard_map/ppermute | solution.py:398
  76.8 4.2 %collective-permute-start.25 = (bf16[224,128]{1,0:T(8,128)(2,1)S(1)}, bf16[224,128]{1,0:T(8,128)(2,1)S(1)}, u32[]{:S(2)}, u32[]{:S(2)}) collective-permute-start(bf16[224,128]{1,0:T(8,128)(2,1)S(1)} %collective-permute-done.24.refs_2_), channel_id=1, source_target_pairs={{0,2},{2,0},{1,3},{3,1},{4,6},{6,4},{5,7},{7,5},{8,10},{10,8},{9,1... | collective-permute-start | bytes 172040 | tf_op jit(solution)/shard_map/ppermute | solution.py:398
  78.1 4.2 %collective-permute-start.27 = (bf16[224,128]{1,0:T(8,128)(2,1)S(1)}, bf16[224,128]{1,0:T(8,128)(2,1)S(1)}, u32[]{:S(2)}, u32[]{:S(2)}) collective-permute-start(bf16[224,128]{1,0:T(8,128)(2,1)S(1)} %collective-permute-done.26.refs_3_), channel_id=1, source_target_pairs={{0,2},{2,0},{1,3},{3,1},{4,6},{6,4},{5,7},{7,5},{8,10},{10,8},{9,1... | collective-permute-start | bytes 172040 | tf_op jit(solution)/shard_map/ppermute | solution.py:398
  (6 other events, 10.9 us)

commit v5 on v4

--- a/solution.py
+++ b/solution.py
@@ -417,7 +417,7 @@
     pair_slots = in_rows.shape[2]
     own_total = tile_blocks * width
     span = 2 * width
-    chunk = 4
+    chunk = 28
     padded = -(-offsets // chunk) * chunk
     swaps = exchanges(tile_rows, depths)
     merged = (tile_rows, depths) == (4, 2) and capacity >= tile_blocks
@@ -546,7 +546,7 @@
     portions = depths if merged else 1
     portion = (padded // portions * half, channels)
     activations, grad_columns, keep, *cross = pl.pallas_call(
-        functools.partial(weight_grad_kernel, chunk),
+        functools.partial(weight_grad_kernel, chunk // 2),
         out_shape=(block_shape, shape((channels, pairs_total), BF16), shape(portion, F32))
         + (shape(portion, BF16),) * (portions - 1),
         in_specs=[VMEM] * 5,

time: 83.5 us -> 81.4 us (0.975)
  Pallas kernels: 17.9 us -> 15.7 us
    pallas_call x1, Pallas kernels: 3.02 us -> 1.7 us  [local(): pl.pallas_call(functools.partial(forward_kernel, tile_blocks // 2, chunk)...]
    pallas_call x1, Pallas kernels: 2.83 us -> 1.96 us  [local(): pl.pallas_call(functools.partial(weight_grad_kernel, chunk // 2), out_sha...]
where the time goes in v5:
time: 81.4 us; the launch traced here: 81.1 us
  starting transfers between devices  37.4 us (46%)
  waiting for transfers between devices  22.3 us (27%)
  Pallas kernels  15.7 us (19%)
  local copies, waits for them, and re-layouts  2.68 us (3%)
  blocking collectives  2.03 us (2%)
  between operations  0.9 us (1%)
    ppermute x12, starting transfers between devices, to_rows(): lax.ppermute(arrays[d], 'tile', xor_pairs(tile_rows, d))  18.1 us
    ppermute x12, waiting for transfers between devices, to_rows(): lax.ppermute(arrays[d], 'tile', xor_pairs(tile_rows, d))  10.7 us
    ppermute x10, starting transfers between devices, across(): return lax.ppermute(array, 'depth', [(0, 1), (1, 0)])  10.6 us
    ppermute x6, starting transfers between devices, swap_all(): lax.ppermute(array, axis, pairs)  8.65 us
    ppermute x10, waiting for transfers between devices, across(): return lax.ppermute(array, 'depth', [(0, 1), (1, 0)])  8.33 us
    ppermute x6, waiting for transfers between devices, swap_all(): lax.ppermute(array, axis, pairs)  3.24 us
    pallas_call x2, Pallas kernels, far_sums(): pl.pallas_call(functools.partial(far_kernel, rows_away, depths, tile_bloc...  2.42 us
    pallas_call x1, Pallas kernels, local(): pl.pallas_call(functools.partial(place_kernel, tile_rows, depths, tile_bl...  2.04 us
  transfers between devices with their start and end apart: 29, of which 14 were waited for; matrix products, arithmetic and copies ran while one was open for 1% of the time, Pallas kernels for 10%

profile of v5, /device:TPU:0, one launch (start us, length us, event | category | flops | bytes accessed | tf_op | source)
XLA Modules:
  0.0 81.1 jit_solution(10022149497317695264)
XLA Ops:
  0.6 3.1 %collective-permute-start = (s32[8,16]{1,0:T(8,128)}, s32[8,16]{1,0:T(8,128)S(1)}, u32[]{:S(2)}, u32[]{:S(2)}) collective-permute-start(s32[8,16]{1,0:T(8,128)} %bitcast.40), channel_id=1, source_target_pairs={{0,4},{4,0},{8,12},{12,8},{1,5},{5,1},{9,13},{13,9},{2,6},{6,2},{1... | collective-permute-start | bytes 1544 | tf_op jit(solution)/shard_map/ppermute | solution.py:393
  3.7 2.6 %collective-permute-start.1 = (s32[8,16]{1,0:T(8,128)}, s32[8,16]{1,0:T(8,128)S(1)}, u32[]{:S(2)}, u32[]{:S(2)}) collective-permute-start(s32[8,16]{1,0:T(8,128)} %bitcast.41), channel_id=1, source_target_pairs={{0,8},{4,12},{8,0},{12,4},{1,9},{5,13},{9,1},{13,5},{2,10},{6,14},... | collective-permute-start | bytes 1544 | tf_op jit(solution)/shard_map/ppermute | solution.py:393
  6.3 1.2 %copy-done.1 = bf16[1,64,64,128]{3,2,1,0:T(8,128)(2,1)S(1)} copy-done((bf16[1,64,64,128]{3,2,1,0:T(8,128)(2,1)S(1)}, bf16[1,64,64,128]{3,2,1,0:T(8,128)(2,1)}, u32[]{:S(2)}) %copy-start.1) | copy-done | bytes 1048600
  8.5 3.5 %collective-permute-done.2.refs_4_ = s32[8,16]{1,0:T(8,128)S(1)} collective-permute-done((s32[8,16]{1,0:T(8,128)}, s32[8,16]{1,0:T(8,128)S(1)}, u32[]{:S(2)}, u32[]{:S(2)}) %collective-permute-start.2) | collective-permute-done | bytes 544 | tf_op jit(solution)/shard_map/ppermute | solution.py:393
  12.0 1.6 %collective-permute-start.3 = (s32[4,8,16]{2,1,0:T(8,128)S(1)}, s32[4,8,16]{2,1,0:T(8,128)S(1)}, u32[]{:S(2)}, u32[]{:S(2)}) collective-permute-start(s32[4,8,16]{2,1,0:T(8,128)S(1)} %pad_add_fusion), channel_id=1, source_target_pairs={{0,2},{2,0},{1,3},{3,1},{4,6},{6,4},{5,7},{7,5},{8,10},{10,8},{9,1... | collective-permute-start | bytes 6152 | tf_op jit(solution)/shard_map/ppermute | solution.py:398
  14.3 1.5 %collective-permute-done.3.far_ref.refs_5_ = s32[4,8,16]{2,1,0:T(8,128)S(1)} collective-permute-done((s32[4,8,16]{2,1,0:T(8,128)S(1)}, s32[4,8,16]{2,1,0:T(8,128)S(1)}, u32[]{:S(2)}, u32[]{:S(2)}) %collective-permute-start.3) | collective-permute-done | bytes 2080 | tf_op jit(solution)/shard_map/ppermute | solution.py:398
  15.8 1.2 %shard_map.116 = bf16[8,64,128]{2,1,0:T(8,128)(2,1)S(1)} custom-call(s32[8,16]{1,0:T(8,128)S(1)} %bitcast.36, s32[4,8,16]{2,1,0:T(8,128)S(1)} %collective-permute-done.3.far_ref.refs_5_, bf16[64,64,128]{2,1,0:T(8,128)(2,1)S(1)} %shard_map.112.refs_5_.log_ref), custom_call_target="tpu_custom_call" | custom-call | tf_op jit(solution)/shard_map/pallas_call | solution.py:461
  17.0 1.6 %collective-permute-start.6 = (bf16[8,64,128]{2,1,0:T(8,128)(2,1)S(1)}, bf16[8,64,128]{2,1,0:T(8,128)(2,1)S(1)}, u32[]{:S(2)}, u32[]{:S(2)}) collective-permute-start(bf16[8,64,128]{2,1,0:T(8,128)(2,1)S(1)} %shard_map.116), channel_id=1, source_target_pairs={{0,2},{2,0},{1,3},{3,1},{4,6},{6,4},{5,7},{7,5},{8,10},{10,8},{9,1... | collective-permute-start | bytes 393224 | tf_op jit(solution)/shard_map/ppermute | solution.py:398
  18.6 1.2 %shard_map.114 = bf16[8,64,128]{2,1,0:T(8,128)(2,1)S(1)} custom-call(s32[8,16]{1,0:T(8,128)S(1)} %bitcast.37, s32[4,8,16]{2,1,0:T(8,128)S(1)} %collective-permute-done.3.far_ref.refs_5_, bf16[64,64,128]{2,1,0:T(8,128)(2,1)S(1)} %shard_map.112.refs_5_.log_ref), custom_call_target="tpu_custom_call" | custom-call | tf_op jit(solution)/shard_map/pallas_call | solution.py:461
  20.5 1.5 %shard_map.113 = (f32[8,64,128]{2,1,0:T(8,128)S(1)}, f32[8,64,128]{2,1,0:T(8,128)S(1)}) custom-call(s32[8,16]{1,0:T(8,128)S(1)} %bitcast.38, s32[8,16]{1,0:T(8,128)S(1)} %bitcast.43, s32[8,16]{1,0:T(8,128)S(1)} %collective-permute-done.refs_2_, s32[8,16]{1,0:T(8,128)S(1)} %collective-permute-done.1.refs_3_, s32[8,16]{1,0:T(8,128)S(1)} %collective-permute-done.2.refs_4_, ...), custom_call_target="tpu_custom_call" | custom-call | tf_op jit(solution)/shard_map/pallas_call | solution.py:472
  23.4 1.5 %collective-permute-done.4.far_ref = bf16[8,64,128]{2,1,0:T(8,128)(2,1)S(1)} collective-permute-done((bf16[8,64,128]{2,1,0:T(8,128)(2,1)S(1)}, bf16[8,64,128]{2,1,0:T(8,128)(2,1)S(1)}, u32[]{:S(2)}, u32[]{:S(2)}) %collective-permute-start.4) | collective-permute-done | bytes 131104 | tf_op jit(solution)/shard_map/ppermute | solution.py:398
  25.8 2.0 %shard_map.118.place_ref = s32[65]{0:T(128)S(1)} custom-call(s32[8,16]{1,0:T(8,128)S(1)} %bitcast.39, s32[8,16]{1,0:T(8,128)S(1)} %bitcast.44, s32[8,16]{1,0:T(8,128)S(1)} %collective-permute-done.refs_2_, s32[8,16]{1,0:T(8,128)S(1)} %collective-permute-done.1.refs_3_, s32[8,16]{1,0:T(8,128)S(1)} %collective-permute-done.2.refs_4_, ...), custom_call_target="tpu_custom_call" | custom-call | tf_op jit(solution)/shard_map/pallas_call | solution.py:479
  30.5 1.3 %collective-permute-start.11 = (bf16[2,64,128]{2,1,0:T(8,128)(2,1)S(1)}, bf16[2,64,128]{2,1,0:T(8,128)(2,1)S(1)}, u32[]{:S(2)}, u32[]{:S(2)}) collective-permute-start(bf16[2,64,128]{2,1,0:T(8,128)(2,1)S(1)} %get-tuple-element.62), channel_id=1, source_target_pairs={{0,2},{2,0},{1,3},{3,1},{4,6},{6,4},{5,7},{7,5},{8,10},{10,8},{9,1... | collective-permute-start | bytes 98312 | tf_op jit(solution)/shard_map/ppermute | solution.py:387
  31.8 2.4 %collective-permute-start.9 = (bf16[2,64,128]{2,1,0:T(8,128)(2,1)S(1)}, bf16[2,64,128]{2,1,0:T(8,128)(2,1)S(1)}, u32[]{:S(2)}, u32[]{:S(2)}) collective-permute-start(bf16[2,64,128]{2,1,0:T(8,128)(2,1)S(1)} %get-tuple-element.60), channel_id=1, source_target_pairs={{0,4},{4,0},{8,12},{12,8},{1,5},{5,1},{9,13},{13,9},{2,6},{6,2},{1... | collective-permute-start | bytes 98312 | tf_op jit(solution)/shard_map/ppermute | solution.py:387
  36.1 1.7 %shard_map.121 = (f32[128,512]{1,0:T(8,128)S(1)}, bf16[64,3584]{1,0:T(8,128)(2,1)S(1)}) custom-call(bf16[64,3584]{1,0:T(8,128)(2,1)S(1)} %shard_map.120.refs_0_, s32[28,128]{1,0:T(8,128)S(1)} %pad.11.source_ref.refs_1_, s32[28,128]{1,0:T(8,128)S(1)} %pad.12.refs_2_.refs_3_, bf16[28,128,64]{2,1,0:T(8,128)(2,1)S(1)} %copy.13.refs_3_, ...), custom_call_target="tpu_custom_call" | custom-call | tf_op jit(solution)/shard_map/pallas_call | solution.py:533
  37.9 2.0 %all-gather = bf16[1,4,128,128]{3,2,1,0:T(8,128)(2,1)S(1)} all-gather(bf16[1,4,64,128]{3,2,1,0:T(8,128)(2,1)S(1)} %copy-done.4), channel_id=2, replica_groups=mesh['groups'=2,'tile'=4,'depth'=2,'chan'=2] {'chan'}, dimensions={2}, use_global_device_ids=true | all-gather | bytes 196608 | tf_op jit(solution)/shard_map/all_gather | solution.py:443
  39.9 2.0 %shard_map.122 = (bf16[4,64,128]{2,1,0:T(8,128)(2,1)}, bf16[128,3584]{1,0:T(8,128)(2,1)S(1)}, f32[896,128]{1,0:T(8,128)S(1)}, bf16[896,128]{1,0:T(8,128)(2,1)S(1)}) custom-call(f32[128,512]{1,0:T(8,128)S(1)} %get-tuple-element.63.refs_0_, f32[128,512]{1,0:T(8,128)S(1)} %collective-permute-done.12.refs_1_, bf16[4,128,128]{2,1,0:T(8,128)(2,1)S(1)} %bitcast.35, ...), custom_call_target="tpu_custom_call" | custom-call | tf_op jit(solution)/shard_map/pallas_call | solution.py:548
  42.4 1.5 %shard_map.123 = (f32[4,64,128]{2,1,0:T(8,128)S(1)}, bf16[2,64,128]{2,1,0:T(8,128)(2,1)S(1)}, bf16[2,64,128]{2,1,0:T(8,128)(2,1)S(1)}, bf16[2,64,128]{2,1,0:T(8,128)(2,1)S(1)}) custom-call(bf16[128,3584]{1,0:T(8,128)(2,1)S(1)} %get-tuple-element.66.grad_columns_ref, s32[28,128]{1,0:T(8,128)S(1)} %pad.11.source_ref.refs_1_, ...), custom_call_target="tpu_custom_call" | custom-call | tf_op jit(solution)/shard_map/pallas_call | solution.py:558
  43.9 2.1 %collective-permute-start.14 = (bf16[2,64,128]{2,1,0:T(8,128)(2,1)S(1)}, bf16[2,64,128]{2,1,0:T(8,128)(2,1)S(1)}, u32[]{:S(2)}, u32[]{:S(2)}) collective-permute-start(bf16[2,64,128]{2,1,0:T(8,128)(2,1)S(1)} %get-tuple-element.70), channel_id=1, source_target_pairs={{0,4},{4,0},{8,12},{12,8},{1,5},{5,1},{9,13},{13,9},{2,6},{6,2},{1... | collective-permute-start | bytes 98312 | tf_op jit(solution)/shard_map/ppermute | solution.py:387
  46.7 1.5 %collective-permute-start.16 = (bf16[2,64,128]{2,1,0:T(8,128)(2,1)S(1)}, bf16[2,64,128]{2,1,0:T(8,128)(2,1)S(1)}, u32[]{:S(2)}, u32[]{:S(2)}) collective-permute-start(bf16[2,64,128]{2,1,0:T(8,128)(2,1)S(1)} %get-tuple-element.72), channel_id=1, source_target_pairs={{0,2},{2,0},{1,3},{3,1},{4,6},{6,4},{5,7},{7,5},{8,10},{10,8},{9,1... | collective-permute-start | bytes 98312 | tf_op jit(solution)/shard_map/ppermute | solution.py:387
  48.2 2.4 %collective-permute-done.16.refs_2_ = bf16[2,64,128]{2,1,0:T(8,128)(2,1)S(1)} collective-permute-done((bf16[2,64,128]{2,1,0:T(8,128)(2,1)S(1)}, bf16[2,64,128]{2,1,0:T(8,128)(2,1)S(1)}, u32[]{:S(2)}, u32[]{:S(2)}) %collective-permute-start.16) | collective-permute-done | bytes 32800 | tf_op jit(solution)/shard_map/ppermute | solution.py:387
  51.4 3.2 %collective-permute-start.17 = (bf16[480,128]{1,0:T(8,128)(2,1)S(1)}, bf16[480,128]{1,0:T(8,128)(2,1)S(1)}, u32[]{:S(2)}, u32[]{:S(2)}) collective-permute-start(bf16[480,128]{1,0:T(8,128)(2,1)S(1)} %get-tuple-element.74), channel_id=1, source_target_pairs={{0,4},{4,0},{8,12},{12,8},{1,5},{5,1},{9,13},{13,9},{2,6},{6,2},{1... | collective-permute-start | bytes 368648 | tf_op jit(solution)/shard_map/ppermute | solution.py:393
  54.8 2.2 %collective-permute-start.19 = (bf16[480,128]{1,0:T(8,128)(2,1)S(1)}, bf16[480,128]{1,0:T(8,128)(2,1)S(1)}, u32[]{:S(2)}, u32[]{:S(2)}) collective-permute-start(bf16[480,128]{1,0:T(8,128)(2,1)S(1)} %get-tuple-element.76), channel_id=1, source_target_pairs={{0,12},{4,8},{8,4},{12,0},{1,13},{5,9},{9,5},{13,1},{2,14},{6,10},... | collective-permute-start | bytes 368648 | tf_op jit(solution)/shard_map/ppermute | solution.py:393
  57.1 1.7 %collective-permute-done.17.refs_0_.refs_1_ = bf16[480,128]{1,0:T(8,128)(2,1)S(1)} collective-permute-done((bf16[480,128]{1,0:T(8,128)(2,1)S(1)}, bf16[480,128]{1,0:T(8,128)(2,1)S(1)}, u32[]{:S(2)}, u32[]{:S(2)}) %collective-permute-start.17) | collective-permute-done | bytes 122912 | tf_op jit(solution)/shard_map/ppermute | solution.py:393
  60.8 3.6 %collective-permute-done.20.refs_3_ = bf16[256,128]{1,0:T(8,128)(2,1)S(1)} collective-permute-done((bf16[256,128]{1,0:T(8,128)(2,1)S(1)}, bf16[256,128]{1,0:T(8,128)(2,1)S(1)}, u32[]{:S(2)}, u32[]{:S(2)}) %collective-permute-start.20) | collective-permute-done | bytes 65568 | tf_op jit(solution)/shard_map/ppermute | solution.py:398
  64.4 1.3 %collective-permute-done.18.refs_1_ = bf16[480,128]{1,0:T(8,128)(2,1)S(1)} collective-permute-done((bf16[480,128]{1,0:T(8,128)(2,1)S(1)}, bf16[480,128]{1,0:T(8,128)(2,1)S(1)}, u32[]{:S(2)}, u32[]{:S(2)}) %collective-permute-start.18) | collective-permute-done | bytes 122912 | tf_op jit(solution)/shard_map/ppermute | solution.py:393
  66.9 2.2 %collective-permute-start.22 = (bf16[224,128]{1,0:T(8,128)(2,1)S(1)}, bf16[224,128]{1,0:T(8,128)(2,1)S(1)}, u32[]{:S(2)}, u32[]{:S(2)}) collective-permute-start(bf16[224,128]{1,0:T(8,128)(2,1)S(1)} %get-tuple-element.82.refs_0_), channel_id=1, source_target_pairs={{0,4},{4,0},{8,12},{12,8},{1,5},{5,1},{9,13},{13,9},{2,6},{6,2},{1... | collective-permute-start | bytes 172040 | tf_op jit(solution)/shard_map/ppermute | solution.py:393
  69.2 2.3 %collective-permute-start.26 = (bf16[224,128]{1,0:T(8,128)(2,1)S(1)}, bf16[224,128]{1,0:T(8,128)(2,1)S(1)}, u32[]{:S(2)}, u32[]{:S(2)}) collective-permute-start(bf16[224,128]{1,0:T(8,128)(2,1)S(1)} %get-tuple-element.82.refs_0_), channel_id=1, source_target_pairs={{0,12},{4,8},{8,4},{12,0},{1,13},{5,9},{9,5},{13,1},{2,14},{6,10},... | collective-permute-start | bytes 172040 | tf_op jit(solution)/shard_map/ppermute | solution.py:393
  72.6 2.0 %collective-permute-done.24.refs_2_ = bf16[224,128]{1,0:T(8,128)(2,1)S(1)} collective-permute-done((bf16[224,128]{1,0:T(8,128)(2,1)S(1)}, bf16[224,128]{1,0:T(8,128)(2,1)S(1)}, u32[]{:S(2)}, u32[]{:S(2)}) %collective-permute-start.24) | collective-permute-done | bytes 57376 | tf_op jit(solution)/shard_map/ppermute | solution.py:393
  74.6 1.3 %collective-permute-start.25 = (bf16[224,128]{1,0:T(8,128)(2,1)S(1)}, bf16[224,128]{1,0:T(8,128)(2,1)S(1)}, u32[]{:S(2)}, u32[]{:S(2)}) collective-permute-start(bf16[224,128]{1,0:T(8,128)(2,1)S(1)} %collective-permute-done.24.refs_2_), channel_id=1, source_target_pairs={{0,2},{2,0},{1,3},{3,1},{4,6},{6,4},{5,7},{7,5},{8,10},{10,8},{9,1... | collective-permute-start | bytes 172040 | tf_op jit(solution)/shard_map/ppermute | solution.py:398
  76.6 1.6 %shard_map.126 = bf16[64,64,128]{2,1,0:T(8,128)(2,1)} custom-call(s32[65]{0:T(128)S(1)} %shard_map.118.place_ref, bf16[256,128]{1,0:T(8,128)(2,1)S(1)} %get-tuple-element.77.refs_0_, bf16[480,128]{1,0:T(8,128)(2,1)S(1)} %collective-permute-done.17.refs_0_.refs_1_, bf16[736,128]{1,0:T(8,128)(2,1)S(1)} %get-tuple-element.84.refs_2_, ...), custom_call_target="tpu_custom_call" | custom-call | tf_op jit(solution)/shard_map/pallas_call | solution.py:601
  78.8 1.3 %collective-permute-done.27.refs_7_ = bf16[224,128]{1,0:T(8,128)(2,1)S(1)} collective-permute-done((bf16[224,128]{1,0:T(8,128)(2,1)S(1)}, bf16[224,128]{1,0:T(8,128)(2,1)S(1)}, u32[]{:S(2)}, u32[]{:S(2)}) %collective-permute-start.27) | collective-permute-done | bytes 57376 | tf_op jit(solution)/shard_map/ppermute | solution.py:398
  (69 shorter events, 18.0 us)
Async XLA Ops:
  0.6 25.1 %copy-start = (bf16[27,128,128]{2,1,0:T(8,128)(2,1)S(1)}, bf16[27,128,128]{2,1,0:T(8,128)(2,1)}, u32[]{:S(2)}) copy-start(bf16[27,128,128]{2,1,0:T(8,128)(2,1)} %param.16) | copy-start | bytes 2654212
  0.6 7.0 %collective-permute-start = (s32[8,16]{1,0:T(8,128)}, s32[8,16]{1,0:T(8,128)S(1)}, u32[]{:S(2)}, u32[]{:S(2)}) collective-permute-start(s32[8,16]{1,0:T(8,128)} %bitcast.40), channel_id=1, source_target_pairs={{0,4},{4,0},{8,12},{12,8},{1,5},{5,1},{9,13},{13,9},{2,6},{6,2},{1... | collective-permute-start | bytes 1544 | tf_op jit(solution)/shard_map/ppermute | solution.py:393
  3.7 4.7 %collective-permute-start.1 = (s32[8,16]{1,0:T(8,128)}, s32[8,16]{1,0:T(8,128)S(1)}, u32[]{:S(2)}, u32[]{:S(2)}) collective-permute-start(s32[8,16]{1,0:T(8,128)} %bitcast.41), channel_id=1, source_target_pairs={{0,8},{4,12},{8,0},{12,4},{1,9},{5,13},{9,1},{13,5},{2,10},{6,14},... | collective-permute-start | bytes 1544 | tf_op jit(solution)/shard_map/ppermute | solution.py:393
  6.3 5.6 %collective-permute-start.2 = (s32[8,16]{1,0:T(8,128)}, s32[8,16]{1,0:T(8,128)S(1)}, u32[]{:S(2)}, u32[]{:S(2)}) collective-permute-start(s32[8,16]{1,0:T(8,128)} %bitcast.42), channel_id=1, source_target_pairs={{0,12},{4,8},{8,4},{12,0},{1,13},{5,9},{9,5},{13,1},{2,14},{6,10},... | collective-permute-start | bytes 1544 | tf_op jit(solution)/shard_map/ppermute | solution.py:393
  7.6 4.3 %copy-start.3 = (s32[1,8,16]{2,1,0:T(8,128)S(1)}, s32[1,8,16]{2,1,0:T(8,128)}, u32[]{:S(2)}) copy-start(s32[1,8,16]{2,1,0:T(8,128)} %param.11) | copy-start | bytes 1540
  12.0 3.8 %collective-permute-start.3 = (s32[4,8,16]{2,1,0:T(8,128)S(1)}, s32[4,8,16]{2,1,0:T(8,128)S(1)}, u32[]{:S(2)}, u32[]{:S(2)}) collective-permute-start(s32[4,8,16]{2,1,0:T(8,128)S(1)} %pad_add_fusion), channel_id=1, source_target_pairs={{0,2},{2,0},{1,3},{3,1},{4,6},{6,4},{5,7},{7,5},{8,10},{10,8},{9,1... | collective-permute-start | bytes 6152 | tf_op jit(solution)/shard_map/ppermute | solution.py:398
  17.0 3.4 %copy-start.5 = (s32[1,27,128]{2,0,1:T(1,128)S(1)}, s32[1,27,128]{2,0,1:T(1,128)}, u32[]{:S(2)}) copy-start(s32[1,27,128]{2,0,1:T(1,128)} %param.14) | copy-start | bytes 41476
  17.0 5.0 %collective-permute-start.6 = (bf16[8,64,128]{2,1,0:T(8,128)(2,1)S(1)}, bf16[8,64,128]{2,1,0:T(8,128)(2,1)S(1)}, u32[]{:S(2)}, u32[]{:S(2)}) collective-permute-start(bf16[8,64,128]{2,1,0:T(8,128)(2,1)S(1)} %shard_map.116), channel_id=1, source_target_pairs={{0,2},{2,0},{1,3},{3,1},{4,6},{6,4},{5,7},{7,5},{8,10},{10,8},{9,1... | collective-permute-start | bytes 393224 | tf_op jit(solution)/shard_map/ppermute | solution.py:398
  19.8 5.0 %collective-permute-start.4 = (bf16[8,64,128]{2,1,0:T(8,128)(2,1)S(1)}, bf16[8,64,128]{2,1,0:T(8,128)(2,1)S(1)}, u32[]{:S(2)}, u32[]{:S(2)}) collective-permute-start(bf16[8,64,128]{2,1,0:T(8,128)(2,1)S(1)} %shard_map.114), channel_id=1, source_target_pairs={{0,2},{2,0},{1,3},{3,1},{4,6},{6,4},{5,7},{7,5},{8,10},{10,8},{9,1... | collective-permute-start | bytes 393224 | tf_op jit(solution)/shard_map/ppermute | solution.py:398
  22.1 5.8 %collective-permute-start.7 = (bf16[4,64,128]{2,1,0:T(8,128)(2,1)S(1)}, bf16[4,64,128]{2,1,0:T(8,128)(2,1)S(1)}, u32[]{:S(2)}, u32[]{:S(2)}) collective-permute-start(bf16[4,64,128]{2,1,0:T(8,128)(2,1)S(1)} %get-tuple-element.53), channel_id=1, source_target_pairs={{0,8},{4,12},{8,0},{12,4},{1,9},{5,13},{9,1},{13,5},{2,10},{6,14},... | collective-permute-start | bytes 196616 | tf_op jit(solution)/shard_map/ppermute | solution.py:393
  22.2 6.2 %collective-permute-start.8 = (bf16[4,64,128]{2,1,0:T(8,128)(2,1)S(1)}, bf16[4,64,128]{2,1,0:T(8,128)(2,1)S(1)}, u32[]{:S(2)}, u32[]{:S(2)}) collective-permute-start(bf16[4,64,128]{2,1,0:T(8,128)(2,1)S(1)} %get-tuple-element.54), channel_id=1, source_target_pairs={{0,12},{4,8},{8,4},{12,0},{1,13},{5,9},{9,5},{13,1},{2,14},{6,10},... | collective-permute-start | bytes 196616 | tf_op jit(solution)/shard_map/ppermute | solution.py:393
  24.9 4.3 %collective-permute-start.5 = (bf16[4,64,128]{2,1,0:T(8,128)(2,1)S(1)}, bf16[4,64,128]{2,1,0:T(8,128)(2,1)S(1)}, u32[]{:S(2)}, u32[]{:S(2)}) collective-permute-start(bf16[4,64,128]{2,1,0:T(8,128)(2,1)S(1)} %get-tuple-element.51), channel_id=1, source_target_pairs={{0,4},{4,0},{8,12},{12,8},{1,5},{5,1},{9,13},{13,9},{2,6},{6,2},{1... | collective-permute-start | bytes 196616 | tf_op jit(solution)/shard_map/ppermute | solution.py:393
  29.8 5.5 %collective-permute-start.10 = (bf16[2,64,128]{2,1,0:T(8,128)(2,1)S(1)}, bf16[2,64,128]{2,1,0:T(8,128)(2,1)S(1)}, u32[]{:S(2)}, u32[]{:S(2)}) collective-permute-start(bf16[2,64,128]{2,1,0:T(8,128)(2,1)S(1)} %get-tuple-element.61), channel_id=1, source_target_pairs={{4,8},{8,4},{5,9},{9,5},{6,10},{10,6},{7,11},{11,7},{20,24},{24,20... | collective-permute-start | bytes 98312 | tf_op jit(solution)/shard_map/ppermute | solution.py:387
  30.5 4.8 %collective-permute-start.11 = (bf16[2,64,128]{2,1,0:T(8,128)(2,1)S(1)}, bf16[2,64,128]{2,1,0:T(8,128)(2,1)S(1)}, u32[]{:S(2)}, u32[]{:S(2)}) collective-permute-start(bf16[2,64,128]{2,1,0:T(8,128)(2,1)S(1)} %get-tuple-element.62), channel_id=1, source_target_pairs={{0,2},{2,0},{1,3},{3,1},{4,6},{6,4},{5,7},{7,5},{8,10},{10,8},{9,1... | collective-permute-start | bytes 98312 | tf_op jit(solution)/shard_map/ppermute | solution.py:387
  31.8 4.3 %collective-permute-start.9 = (bf16[2,64,128]{2,1,0:T(8,128)(2,1)S(1)}, bf16[2,64,128]{2,1,0:T(8,128)(2,1)S(1)}, u32[]{:S(2)}, u32[]{:S(2)}) collective-permute-start(bf16[2,64,128]{2,1,0:T(8,128)(2,1)S(1)} %get-tuple-element.60), channel_id=1, source_target_pairs={{0,4},{4,0},{8,12},{12,8},{1,5},{5,1},{9,13},{13,9},{2,6},{6,2},{1... | collective-permute-start | bytes 98312 | tf_op jit(solution)/shard_map/ppermute | solution.py:387
  37.8 2.1 %collective-permute-start.12 = (f32[128,512]{1,0:T(8,128)S(1)}, f32[128,512]{1,0:T(8,128)S(1)}, u32[]{:S(2)}, u32[]{:S(2)}) collective-permute-start(f32[128,512]{1,0:T(8,128)S(1)} %get-tuple-element.63.refs_0_), channel_id=1, source_target_pairs={{0,1},{1,0},{2,3},{3,2},{4,5},{5,4},{6,7},{7,6},{8,9},{9,8},{10,11... | collective-permute-start | bytes 786440 | tf_op jit(solution)/shard_map/ppermute | solution.py:544
  41.9 8.8 %collective-permute-start.13 = (bf16[896,128]{1,0:T(8,128)(2,1)S(1)}, bf16[896,128]{1,0:T(8,128)(2,1)S(1)}, u32[]{:S(2)}, u32[]{:S(2)}) collective-permute-start(bf16[896,128]{1,0:T(8,128)(2,1)S(1)} %get-tuple-element.69), channel_id=1, source_target_pairs={{0,2},{2,0},{1,3},{3,1},{4,6},{6,4},{5,7},{7,5},{8,10},{10,8},{9,1... | collective-permute-start | bytes 688136 | tf_op jit(solution)/shard_map/ppermute | solution.py:398
  43.9 4.3 %collective-permute-start.14 = (bf16[2,64,128]{2,1,0:T(8,128)(2,1)S(1)}, bf16[2,64,128]{2,1,0:T(8,128)(2,1)S(1)}, u32[]{:S(2)}, u32[]{:S(2)}) collective-permute-start(bf16[2,64,128]{2,1,0:T(8,128)(2,1)S(1)} %get-tuple-element.70), channel_id=1, source_target_pairs={{0,4},{4,0},{8,12},{12,8},{1,5},{5,1},{9,13},{13,9},{2,6},{6,2},{1... | collective-permute-start | bytes 98312 | tf_op jit(solution)/shard_map/ppermute | solution.py:387
  46.0 2.2 %collective-permute-start.15 = (bf16[2,64,128]{2,1,0:T(8,128)(2,1)S(1)}, bf16[2,64,128]{2,1,0:T(8,128)(2,1)S(1)}, u32[]{:S(2)}, u32[]{:S(2)}) collective-permute-start(bf16[2,64,128]{2,1,0:T(8,128)(2,1)S(1)} %get-tuple-element.71), channel_id=1, source_target_pairs={{4,8},{8,4},{5,9},{9,5},{6,10},{10,6},{7,11},{11,7},{20,24},{24,20... | collective-permute-start | bytes 98312 | tf_op jit(solution)/shard_map/ppermute | solution.py:387
  46.7 4.0 %collective-permute-start.16 = (bf16[2,64,128]{2,1,0:T(8,128)(2,1)S(1)}, bf16[2,64,128]{2,1,0:T(8,128)(2,1)S(1)}, u32[]{:S(2)}, u32[]{:S(2)}) collective-permute-start(bf16[2,64,128]{2,1,0:T(8,128)(2,1)S(1)} %get-tuple-element.72), channel_id=1, source_target_pairs={{0,2},{2,0},{1,3},{3,1},{4,6},{6,4},{5,7},{7,5},{8,10},{10,8},{9,1... | collective-permute-start | bytes 98312 | tf_op jit(solution)/shard_map/ppermute | solution.py:387
  51.4 7.4 %collective-permute-start.17 = (bf16[480,128]{1,0:T(8,128)(2,1)S(1)}, bf16[480,128]{1,0:T(8,128)(2,1)S(1)}, u32[]{:S(2)}, u32[]{:S(2)}) collective-permute-start(bf16[480,128]{1,0:T(8,128)(2,1)S(1)} %get-tuple-element.74), channel_id=1, source_target_pairs={{0,4},{4,0},{8,12},{12,8},{1,5},{5,1},{9,13},{13,9},{2,6},{6,2},{1... | collective-permute-start | bytes 368648 | tf_op jit(solution)/shard_map/ppermute | solution.py:393
  54.6 11.1 %collective-permute-start.18 = (bf16[480,128]{1,0:T(8,128)(2,1)S(1)}, bf16[480,128]{1,0:T(8,128)(2,1)S(1)}, u32[]{:S(2)}, u32[]{:S(2)}) collective-permute-start(bf16[480,128]{1,0:T(8,128)(2,1)S(1)} %get-tuple-element.75), channel_id=1, source_target_pairs={{0,8},{4,12},{8,0},{12,4},{1,9},{5,13},{9,1},{13,5},{2,10},{6,14},... | collective-permute-start | bytes 368648 | tf_op jit(solution)/shard_map/ppermute | solution.py:393
  54.8 10.9 %collective-permute-start.19 = (bf16[480,128]{1,0:T(8,128)(2,1)S(1)}, bf16[480,128]{1,0:T(8,128)(2,1)S(1)}, u32[]{:S(2)}, u32[]{:S(2)}) collective-permute-start(bf16[480,128]{1,0:T(8,128)(2,1)S(1)} %get-tuple-element.76), channel_id=1, source_target_pairs={{0,12},{4,8},{8,4},{12,0},{1,13},{5,9},{9,5},{13,1},{2,14},{6,10},... | collective-permute-start | bytes 368648 | tf_op jit(solution)/shard_map/ppermute | solution.py:393
  58.8 6.9 %collective-permute-start.21 = (bf16[480,128]{1,0:T(8,128)(2,1)S(1)}, bf16[480,128]{1,0:T(8,128)(2,1)S(1)}, u32[]{:S(2)}, u32[]{:S(2)}) collective-permute-start(bf16[480,128]{1,0:T(8,128)(2,1)S(1)} %collective-permute-done.17.refs_0_.refs_1_), channel_id=1, source_target_pairs={{0,2},{2,0},{1,3},{3,1},{4,6},{6,4},{5,7},{7,5},{8,10},{10,8},{9,1... | collective-permute-start | bytes 368648 | tf_op jit(solution)/shard_map/ppermute | solution.py:398
  59.9 4.5 %collective-permute-start.20 = (bf16[256,128]{1,0:T(8,128)(2,1)S(1)}, bf16[256,128]{1,0:T(8,128)(2,1)S(1)}, u32[]{:S(2)}, u32[]{:S(2)}) collective-permute-start(bf16[256,128]{1,0:T(8,128)(2,1)S(1)} %get-tuple-element.77.refs_0_), channel_id=1, source_target_pairs={{0,2},{2,0},{1,3},{3,1},{4,6},{6,4},{5,7},{7,5},{8,10},{10,8},{9,1... | collective-permute-start | bytes 196616 | tf_op jit(solution)/shard_map/ppermute | solution.py:398
  65.8 10.9 %collective-permute-start.28 = (bf16[736,128]{1,0:T(8,128)(2,1)S(1)}, bf16[736,128]{1,0:T(8,128)(2,1)S(1)}, u32[]{:S(2)}, u32[]{:S(2)}) collective-permute-start(bf16[736,128]{1,0:T(8,128)(2,1)S(1)} %get-tuple-element.84.refs_2_), channel_id=1, source_target_pairs={{0,2},{2,0},{1,3},{3,1},{4,6},{6,4},{5,7},{7,5},{8,10},{10,8},{9,1... | collective-permute-start | bytes 565256 | tf_op jit(solution)/shard_map/ppermute | solution.py:398
  66.9 4.6 %collective-permute-start.22 = (bf16[224,128]{1,0:T(8,128)(2,1)S(1)}, bf16[224,128]{1,0:T(8,128)(2,1)S(1)}, u32[]{:S(2)}, u32[]{:S(2)}) collective-permute-start(bf16[224,128]{1,0:T(8,128)(2,1)S(1)} %get-tuple-element.82.refs_0_), channel_id=1, source_target_pairs={{0,4},{4,0},{8,12},{12,8},{1,5},{5,1},{9,13},{13,9},{2,6},{6,2},{1... | collective-permute-start | bytes 172040 | tf_op jit(solution)/shard_map/ppermute | solution.py:393
  69.1 5.5 %collective-permute-start.24 = (bf16[224,128]{1,0:T(8,128)(2,1)S(1)}, bf16[224,128]{1,0:T(8,128)(2,1)S(1)}, u32[]{:S(2)}, u32[]{:S(2)}) collective-permute-start(bf16[224,128]{1,0:T(8,128)(2,1)S(1)} %get-tuple-element.82.refs_0_), channel_id=1, source_target_pairs={{0,8},{4,12},{8,0},{12,4},{1,9},{5,13},{9,1},{13,5},{2,10},{6,14},... | collective-permute-start | bytes 172040 | tf_op jit(solution)/shard_map/ppermute | solution.py:393
  69.2 6.7 %collective-permute-start.26 = (bf16[224,128]{1,0:T(8,128)(2,1)S(1)}, bf16[224,128]{1,0:T(8,128)(2,1)S(1)}, u32[]{:S(2)}, u32[]{:S(2)}) collective-permute-start(bf16[224,128]{1,0:T(8,128)(2,1)S(1)} %get-tuple-element.82.refs_0_), channel_id=1, source_target_pairs={{0,12},{4,8},{8,4},{12,0},{1,13},{5,9},{9,5},{13,1},{2,14},{6,10},... | collective-permute-start | bytes 172040 | tf_op jit(solution)/shard_map/ppermute | solution.py:393
  71.5 6.7 %collective-permute-start.23 = (bf16[224,128]{1,0:T(8,128)(2,1)S(1)}, bf16[224,128]{1,0:T(8,128)(2,1)S(1)}, u32[]{:S(2)}, u32[]{:S(2)}) collective-permute-start(bf16[224,128]{1,0:T(8,128)(2,1)S(1)} %collective-permute-done.22.refs_1_), channel_id=1, source_target_pairs={{0,2},{2,0},{1,3},{3,1},{4,6},{6,4},{5,7},{7,5},{8,10},{10,8},{9,1... | collective-permute-start | bytes 172040 | tf_op jit(solution)/shard_map/ppermute | solution.py:398
  74.6 4.2 %collective-permute-start.25 = (bf16[224,128]{1,0:T(8,128)(2,1)S(1)}, bf16[224,128]{1,0:T(8,128)(2,1)S(1)}, u32[]{:S(2)}, u32[]{:S(2)}) collective-permute-start(bf16[224,128]{1,0:T(8,128)(2,1)S(1)} %collective-permute-done.24.refs_2_), channel_id=1, source_target_pairs={{0,2},{2,0},{1,3},{3,1},{4,6},{6,4},{5,7},{7,5},{8,10},{10,8},{9,1... | collective-permute-start | bytes 172040 | tf_op jit(solution)/shard_map/ppermute | solution.py:398
  75.9 4.2 %collective-permute-start.27 = (bf16[224,128]{1,0:T(8,128)(2,1)S(1)}, bf16[224,128]{1,0:T(8,128)(2,1)S(1)}, u32[]{:S(2)}, u32[]{:S(2)}) collective-permute-start(bf16[224,128]{1,0:T(8,128)(2,1)S(1)} %collective-permute-done.26.refs_3_), channel_id=1, source_target_pairs={{0,2},{2,0},{1,3},{3,1},{4,6},{6,4},{5,7},{7,5},{8,10},{10,8},{9,1... | collective-permute-start | bytes 172040 | tf_op jit(solution)/shard_map/ppermute | solution.py:398
  (6 other events, 10.1 us)

commit v6 on v5

--- a/solution.py
+++ b/solution.py
@@ -200,7 +200,10 @@
 
     def emit(k, picked):
         columns_ref[:, lanes(k)] = picked
-        product = jnp.dot(weight_ref[k], picked, preferred_element_type=F32).astype(BF16)
+
+    def multiply(k):
+        product = jnp.dot(weight_ref[k], columns_ref[:, lanes(k)], preferred_element_type=F32)
+        product = product.astype(BF16)
         target = table_row(target_ref, k)
         fold = (target // span).astype(F32).astype(BF16)
         places[:, lanes(k)] = one_hot(target & (span - 1), span)
@@ -221,6 +224,8 @@
     else:
         for k in range(offsets):
             emit(k, own_ref[:, lanes(k)])
+    for k in range(offsets):
+        multiply(k)
     total = lax.dot_general(
         values[...], places[...], (((1,), (1,)), ((), ())), preferred_element_type=F32
     )
@@ -254,14 +259,15 @@
             fold = (rows[n] // span).astype(F32).astype(BF16)
             picked = pick_fold(fold, [gathered[:channels, inside], gathered[channels:, inside]])
             grad_columns_ref[:, lanes] = picked
-            term = lax.dot_general(
-                columns_ref[:, lanes],
-                picked,
-                (((1,), (1,)), ((), ())),
-                preferred_element_type=F32,
-            )
-            row = (k % portion) * half
-            held[(k // portion) ^ here, row : row + half, :] = term
+    for k in range(offsets):
+        lanes = slice(k * width, (k + 1) * width)
+        row = (k % portion) * half
+        held[(k // portion) ^ here, row : row + half, :] = lax.dot_general(
+            columns_ref[:, lanes],
+            grad_columns_ref[:, lanes],
+            (((1,), (1,)), ((), ())),
+            preferred_element_type=F32,
+        )
     for n, ref in enumerate(portions):
         ref[...] = held[n].astype(ref.dtype)
     start = pl.multiple_of(lax.axis_index("chan") * half, half)

time: 81.4 us -> 81.4 us (level)
  no operation moved by 1% of the time
where the time goes in v6:
time: 81.4 us; the launch traced here: 81.1 us
  starting transfers between devices  37.4 us (46%)
  waiting for transfers between devices  22.3 us (27%)
  Pallas kernels  15.7 us (19%)
  local copies, waits for them, and re-layouts  2.68 us (3%)
  blocking collectives  2.03 us (2%)
  between operations  0.9 us (1%)
    ppermute x12, starting transfers between devices, to_rows(): lax.ppermute(arrays[d], 'tile', xor_pairs(tile_rows, d))  18.1 us
    ppermute x12, waiting for transfers between devices, to_rows(): lax.ppermute(arrays[d], 'tile', xor_pairs(tile_rows, d))  10.7 us
    ppermute x10, starting transfers between devices, across(): return lax.ppermute(array, 'depth', [(0, 1), (1, 0)])  10.6 us
    ppermute x6, starting transfers between devices, swap_all(): lax.ppermute(array, axis, pairs)  8.66 us
    ppermute x10, waiting for transfers between devices, across(): return lax.ppermute(array, 'depth', [(0, 1), (1, 0)])  8.34 us
    ppermute x6, waiting for transfers between devices, swap_all(): lax.ppermute(array, axis, pairs)  3.25 us
    pallas_call x2, Pallas kernels, far_sums(): pl.pallas_call(functools.partial(far_kernel, rows_away, depths, tile_bloc...  2.42 us
    pallas_call x1, Pallas kernels, local(): pl.pallas_call(functools.partial(place_kernel, tile_rows, depths, tile_bl...  2.04 us
  transfers between devices with their start and end apart: 29, of which 14 were waited for; matrix products, arithmetic and copies ran while one was open for 1% of the time, Pallas kernels for 10%

profile of v6, /device:TPU:0, one launch (start us, length us, event | category | flops | bytes accessed | tf_op | source)
XLA Modules:
  0.0 81.1 jit_solution(12242203240939165016)
XLA Ops:
  0.6 3.1 %collective-permute-start = (s32[8,16]{1,0:T(8,128)}, s32[8,16]{1,0:T(8,128)S(1)}, u32[]{:S(2)}, u32[]{:S(2)}) collective-permute-start(s32[8,16]{1,0:T(8,128)} %bitcast.40), channel_id=1, source_target_pairs={{0,4},{4,0},{8,12},{12,8},{1,5},{5,1},{9,13},{13,9},{2,6},{6,2},{1... | collective-permute-start | bytes 1544 | tf_op jit(solution)/shard_map/ppermute | solution.py:399
  3.7 2.6 %collective-permute-start.1 = (s32[8,16]{1,0:T(8,128)}, s32[8,16]{1,0:T(8,128)S(1)}, u32[]{:S(2)}, u32[]{:S(2)}) collective-permute-start(s32[8,16]{1,0:T(8,128)} %bitcast.41), channel_id=1, source_target_pairs={{0,8},{4,12},{8,0},{12,4},{1,9},{5,13},{9,1},{13,5},{2,10},{6,14},... | collective-permute-start | bytes 1544 | tf_op jit(solution)/shard_map/ppermute | solution.py:399
  6.3 1.2 %copy-done.1 = bf16[1,64,64,128]{3,2,1,0:T(8,128)(2,1)S(1)} copy-done((bf16[1,64,64,128]{3,2,1,0:T(8,128)(2,1)S(1)}, bf16[1,64,64,128]{3,2,1,0:T(8,128)(2,1)}, u32[]{:S(2)}) %copy-start.1) | copy-done | bytes 1048600
  8.5 3.5 %collective-permute-done.2.refs_4_ = s32[8,16]{1,0:T(8,128)S(1)} collective-permute-done((s32[8,16]{1,0:T(8,128)}, s32[8,16]{1,0:T(8,128)S(1)}, u32[]{:S(2)}, u32[]{:S(2)}) %collective-permute-start.2) | collective-permute-done | bytes 544 | tf_op jit(solution)/shard_map/ppermute | solution.py:399
  12.0 1.6 %collective-permute-start.3 = (s32[4,8,16]{2,1,0:T(8,128)S(1)}, s32[4,8,16]{2,1,0:T(8,128)S(1)}, u32[]{:S(2)}, u32[]{:S(2)}) collective-permute-start(s32[4,8,16]{2,1,0:T(8,128)S(1)} %pad_add_fusion), channel_id=1, source_target_pairs={{0,2},{2,0},{1,3},{3,1},{4,6},{6,4},{5,7},{7,5},{8,10},{10,8},{9,1... | collective-permute-start | bytes 6152 | tf_op jit(solution)/shard_map/ppermute | solution.py:404
  14.3 1.5 %collective-permute-done.3.far_ref.refs_5_ = s32[4,8,16]{2,1,0:T(8,128)S(1)} collective-permute-done((s32[4,8,16]{2,1,0:T(8,128)S(1)}, s32[4,8,16]{2,1,0:T(8,128)S(1)}, u32[]{:S(2)}, u32[]{:S(2)}) %collective-permute-start.3) | collective-permute-done | bytes 2080 | tf_op jit(solution)/shard_map/ppermute | solution.py:404
  15.8 1.2 %shard_map.116 = bf16[8,64,128]{2,1,0:T(8,128)(2,1)S(1)} custom-call(s32[8,16]{1,0:T(8,128)S(1)} %bitcast.36, s32[4,8,16]{2,1,0:T(8,128)S(1)} %collective-permute-done.3.far_ref.refs_5_, bf16[64,64,128]{2,1,0:T(8,128)(2,1)S(1)} %shard_map.112.refs_5_.log_ref), custom_call_target="tpu_custom_call" | custom-call | tf_op jit(solution)/shard_map/pallas_call | solution.py:467
  17.0 1.6 %collective-permute-start.6 = (bf16[8,64,128]{2,1,0:T(8,128)(2,1)S(1)}, bf16[8,64,128]{2,1,0:T(8,128)(2,1)S(1)}, u32[]{:S(2)}, u32[]{:S(2)}) collective-permute-start(bf16[8,64,128]{2,1,0:T(8,128)(2,1)S(1)} %shard_map.116), channel_id=1, source_target_pairs={{0,2},{2,0},{1,3},{3,1},{4,6},{6,4},{5,7},{7,5},{8,10},{10,8},{9,1... | collective-permute-start | bytes 393224 | tf_op jit(solution)/shard_map/ppermute | solution.py:404
  18.6 1.2 %shard_map.114 = bf16[8,64,128]{2,1,0:T(8,128)(2,1)S(1)} custom-call(s32[8,16]{1,0:T(8,128)S(1)} %bitcast.37, s32[4,8,16]{2,1,0:T(8,128)S(1)} %collective-permute-done.3.far_ref.refs_5_, bf16[64,64,128]{2,1,0:T(8,128)(2,1)S(1)} %shard_map.112.refs_5_.log_ref), custom_call_target="tpu_custom_call" | custom-call | tf_op jit(solution)/shard_map/pallas_call | solution.py:467
  20.5 1.5 %shard_map.113 = (f32[8,64,128]{2,1,0:T(8,128)S(1)}, f32[8,64,128]{2,1,0:T(8,128)S(1)}) custom-call(s32[8,16]{1,0:T(8,128)S(1)} %bitcast.38, s32[8,16]{1,0:T(8,128)S(1)} %bitcast.43, s32[8,16]{1,0:T(8,128)S(1)} %collective-permute-done.refs_2_, s32[8,16]{1,0:T(8,128)S(1)} %collective-permute-done.1.refs_3_, s32[8,16]{1,0:T(8,128)S(1)} %collective-permute-done.2.refs_4_, ...), custom_call_target="tpu_custom_call" | custom-call | tf_op jit(solution)/shard_map/pallas_call | solution.py:478
  23.4 1.5 %collective-permute-done.4.far_ref = bf16[8,64,128]{2,1,0:T(8,128)(2,1)S(1)} collective-permute-done((bf16[8,64,128]{2,1,0:T(8,128)(2,1)S(1)}, bf16[8,64,128]{2,1,0:T(8,128)(2,1)S(1)}, u32[]{:S(2)}, u32[]{:S(2)}) %collective-permute-start.4) | collective-permute-done | bytes 131104 | tf_op jit(solution)/shard_map/ppermute | solution.py:404
  25.8 2.0 %shard_map.118.place_ref = s32[65]{0:T(128)S(1)} custom-call(s32[8,16]{1,0:T(8,128)S(1)} %bitcast.39, s32[8,16]{1,0:T(8,128)S(1)} %bitcast.44, s32[8,16]{1,0:T(8,128)S(1)} %collective-permute-done.refs_2_, s32[8,16]{1,0:T(8,128)S(1)} %collective-permute-done.1.refs_3_, s32[8,16]{1,0:T(8,128)S(1)} %collective-permute-done.2.refs_4_, ...), custom_call_target="tpu_custom_call" | custom-call | tf_op jit(solution)/shard_map/pallas_call | solution.py:485
  30.5 1.3 %collective-permute-start.11 = (bf16[2,64,128]{2,1,0:T(8,128)(2,1)S(1)}, bf16[2,64,128]{2,1,0:T(8,128)(2,1)S(1)}, u32[]{:S(2)}, u32[]{:S(2)}) collective-permute-start(bf16[2,64,128]{2,1,0:T(8,128)(2,1)S(1)} %get-tuple-element.62), channel_id=1, source_target_pairs={{0,2},{2,0},{1,3},{3,1},{4,6},{6,4},{5,7},{7,5},{8,10},{10,8},{9,1... | collective-permute-start | bytes 98312 | tf_op jit(solution)/shard_map/ppermute | solution.py:393
  31.8 2.4 %collective-permute-start.9 = (bf16[2,64,128]{2,1,0:T(8,128)(2,1)S(1)}, bf16[2,64,128]{2,1,0:T(8,128)(2,1)S(1)}, u32[]{:S(2)}, u32[]{:S(2)}) collective-permute-start(bf16[2,64,128]{2,1,0:T(8,128)(2,1)S(1)} %get-tuple-element.60), channel_id=1, source_target_pairs={{0,4},{4,0},{8,12},{12,8},{1,5},{5,1},{9,13},{13,9},{2,6},{6,2},{1... | collective-permute-start | bytes 98312 | tf_op jit(solution)/shard_map/ppermute | solution.py:393
  36.1 1.7 %shard_map.121 = (f32[128,512]{1,0:T(8,128)S(1)}, bf16[64,3584]{1,0:T(8,128)(2,1)S(1)}) custom-call(bf16[64,3584]{1,0:T(8,128)(2,1)S(1)} %shard_map.120.refs_0_, s32[28,128]{1,0:T(8,128)S(1)} %pad.11.source_ref.refs_1_, s32[28,128]{1,0:T(8,128)S(1)} %pad.12.refs_2_.refs_3_, bf16[28,128,64]{2,1,0:T(8,128)(2,1)S(1)} %copy.13.refs_3_, ...), custom_call_target="tpu_custom_call" | custom-call | tf_op jit(solution)/shard_map/pallas_call | solution.py:539
  37.8 2.0 %all-gather = bf16[1,4,128,128]{3,2,1,0:T(8,128)(2,1)S(1)} all-gather(bf16[1,4,64,128]{3,2,1,0:T(8,128)(2,1)S(1)} %copy-done.4), channel_id=2, replica_groups=mesh['groups'=2,'tile'=4,'depth'=2,'chan'=2] {'chan'}, dimensions={2}, use_global_device_ids=true | all-gather | bytes 196608 | tf_op jit(solution)/shard_map/all_gather | solution.py:449
  39.9 2.0 %shard_map.122 = (bf16[4,64,128]{2,1,0:T(8,128)(2,1)}, bf16[128,3584]{1,0:T(8,128)(2,1)S(1)}, f32[896,128]{1,0:T(8,128)S(1)}, bf16[896,128]{1,0:T(8,128)(2,1)S(1)}) custom-call(f32[128,512]{1,0:T(8,128)S(1)} %get-tuple-element.63.refs_0_, f32[128,512]{1,0:T(8,128)S(1)} %collective-permute-done.12.refs_1_, bf16[4,128,128]{2,1,0:T(8,128)(2,1)S(1)} %bitcast.35, ...), custom_call_target="tpu_custom_call" | custom-call | tf_op jit(solution)/shard_map/pallas_call | solution.py:554
  42.4 1.5 %shard_map.123 = (f32[4,64,128]{2,1,0:T(8,128)S(1)}, bf16[2,64,128]{2,1,0:T(8,128)(2,1)S(1)}, bf16[2,64,128]{2,1,0:T(8,128)(2,1)S(1)}, bf16[2,64,128]{2,1,0:T(8,128)(2,1)S(1)}) custom-call(bf16[128,3584]{1,0:T(8,128)(2,1)S(1)} %get-tuple-element.66.grad_columns_ref, s32[28,128]{1,0:T(8,128)S(1)} %pad.11.source_ref.refs_1_, ...), custom_call_target="tpu_custom_call" | custom-call | tf_op jit(solution)/shard_map/pallas_call | solution.py:564
  43.9 2.1 %collective-permute-start.14 = (bf16[2,64,128]{2,1,0:T(8,128)(2,1)S(1)}, bf16[2,64,128]{2,1,0:T(8,128)(2,1)S(1)}, u32[]{:S(2)}, u32[]{:S(2)}) collective-permute-start(bf16[2,64,128]{2,1,0:T(8,128)(2,1)S(1)} %get-tuple-element.70), channel_id=1, source_target_pairs={{0,4},{4,0},{8,12},{12,8},{1,5},{5,1},{9,13},{13,9},{2,6},{6,2},{1... | collective-permute-start | bytes 98312 | tf_op jit(solution)/shard_map/ppermute | solution.py:393
  46.7 1.5 %collective-permute-start.16 = (bf16[2,64,128]{2,1,0:T(8,128)(2,1)S(1)}, bf16[2,64,128]{2,1,0:T(8,128)(2,1)S(1)}, u32[]{:S(2)}, u32[]{:S(2)}) collective-permute-start(bf16[2,64,128]{2,1,0:T(8,128)(2,1)S(1)} %get-tuple-element.72), channel_id=1, source_target_pairs={{0,2},{2,0},{1,3},{3,1},{4,6},{6,4},{5,7},{7,5},{8,10},{10,8},{9,1... | collective-permute-start | bytes 98312 | tf_op jit(solution)/shard_map/ppermute | solution.py:393
  48.2 2.4 %collective-permute-done.16.refs_2_ = bf16[2,64,128]{2,1,0:T(8,128)(2,1)S(1)} collective-permute-done((bf16[2,64,128]{2,1,0:T(8,128)(2,1)S(1)}, bf16[2,64,128]{2,1,0:T(8,128)(2,1)S(1)}, u32[]{:S(2)}, u32[]{:S(2)}) %collective-permute-start.16) | collective-permute-done | bytes 32800 | tf_op jit(solution)/shard_map/ppermute | solution.py:393
  51.4 3.2 %collective-permute-start.17 = (bf16[480,128]{1,0:T(8,128)(2,1)S(1)}, bf16[480,128]{1,0:T(8,128)(2,1)S(1)}, u32[]{:S(2)}, u32[]{:S(2)}) collective-permute-start(bf16[480,128]{1,0:T(8,128)(2,1)S(1)} %get-tuple-element.74), channel_id=1, source_target_pairs={{0,4},{4,0},{8,12},{12,8},{1,5},{5,1},{9,13},{13,9},{2,6},{6,2},{1... | collective-permute-start | bytes 368648 | tf_op jit(solution)/shard_map/ppermute | solution.py:399
  54.8 2.2 %collective-permute-start.19 = (bf16[480,128]{1,0:T(8,128)(2,1)S(1)}, bf16[480,128]{1,0:T(8,128)(2,1)S(1)}, u32[]{:S(2)}, u32[]{:S(2)}) collective-permute-start(bf16[480,128]{1,0:T(8,128)(2,1)S(1)} %get-tuple-element.76), channel_id=1, source_target_pairs={{0,12},{4,8},{8,4},{12,0},{1,13},{5,9},{9,5},{13,1},{2,14},{6,10},... | collective-permute-start | bytes 368648 | tf_op jit(solution)/shard_map/ppermute | solution.py:399
  57.0 1.7 %collective-permute-done.17.refs_0_.refs_1_ = bf16[480,128]{1,0:T(8,128)(2,1)S(1)} collective-permute-done((bf16[480,128]{1,0:T(8,128)(2,1)S(1)}, bf16[480,128]{1,0:T(8,128)(2,1)S(1)}, u32[]{:S(2)}, u32[]{:S(2)}) %collective-permute-start.17) | collective-permute-done | bytes 122912 | tf_op jit(solution)/shard_map/ppermute | solution.py:399
  60.8 3.6 %collective-permute-done.20.refs_3_ = bf16[256,128]{1,0:T(8,128)(2,1)S(1)} collective-permute-done((bf16[256,128]{1,0:T(8,128)(2,1)S(1)}, bf16[256,128]{1,0:T(8,128)(2,1)S(1)}, u32[]{:S(2)}, u32[]{:S(2)}) %collective-permute-start.20) | collective-permute-done | bytes 65568 | tf_op jit(solution)/shard_map/ppermute | solution.py:404
  64.4 1.3 %collective-permute-done.18.refs_1_ = bf16[480,128]{1,0:T(8,128)(2,1)S(1)} collective-permute-done((bf16[480,128]{1,0:T(8,128)(2,1)S(1)}, bf16[480,128]{1,0:T(8,128)(2,1)S(1)}, u32[]{:S(2)}, u32[]{:S(2)}) %collective-permute-start.18) | collective-permute-done | bytes 122912 | tf_op jit(solution)/shard_map/ppermute | solution.py:399
  66.9 2.2 %collective-permute-start.22 = (bf16[224,128]{1,0:T(8,128)(2,1)S(1)}, bf16[224,128]{1,0:T(8,128)(2,1)S(1)}, u32[]{:S(2)}, u32[]{:S(2)}) collective-permute-start(bf16[224,128]{1,0:T(8,128)(2,1)S(1)} %get-tuple-element.82.refs_0_), channel_id=1, source_target_pairs={{0,4},{4,0},{8,12},{12,8},{1,5},{5,1},{9,13},{13,9},{2,6},{6,2},{1... | collective-permute-start | bytes 172040 | tf_op jit(solution)/shard_map/ppermute | solution.py:399
  69.1 2.3 %collective-permute-start.26 = (bf16[224,128]{1,0:T(8,128)(2,1)S(1)}, bf16[224,128]{1,0:T(8,128)(2,1)S(1)}, u32[]{:S(2)}, u32[]{:S(2)}) collective-permute-start(bf16[224,128]{1,0:T(8,128)(2,1)S(1)} %get-tuple-element.82.refs_0_), channel_id=1, source_target_pairs={{0,12},{4,8},{8,4},{12,0},{1,13},{5,9},{9,5},{13,1},{2,14},{6,10},... | collective-permute-start | bytes 172040 | tf_op jit(solution)/shard_map/ppermute | solution.py:399
  72.6 2.0 %collective-permute-done.24.refs_2_ = bf16[224,128]{1,0:T(8,128)(2,1)S(1)} collective-permute-done((bf16[224,128]{1,0:T(8,128)(2,1)S(1)}, bf16[224,128]{1,0:T(8,128)(2,1)S(1)}, u32[]{:S(2)}, u32[]{:S(2)}) %collective-permute-start.24) | collective-permute-done | bytes 57376 | tf_op jit(solution)/shard_map/ppermute | solution.py:399
  74.6 1.3 %collective-permute-start.25 = (bf16[224,128]{1,0:T(8,128)(2,1)S(1)}, bf16[224,128]{1,0:T(8,128)(2,1)S(1)}, u32[]{:S(2)}, u32[]{:S(2)}) collective-permute-start(bf16[224,128]{1,0:T(8,128)(2,1)S(1)} %collective-permute-done.24.refs_2_), channel_id=1, source_target_pairs={{0,2},{2,0},{1,3},{3,1},{4,6},{6,4},{5,7},{7,5},{8,10},{10,8},{9,1... | collective-permute-start | bytes 172040 | tf_op jit(solution)/shard_map/ppermute | solution.py:404
  76.6 1.6 %shard_map.126 = bf16[64,64,128]{2,1,0:T(8,128)(2,1)} custom-call(s32[65]{0:T(128)S(1)} %shard_map.118.place_ref, bf16[256,128]{1,0:T(8,128)(2,1)S(1)} %get-tuple-element.77.refs_0_, bf16[480,128]{1,0:T(8,128)(2,1)S(1)} %collective-permute-done.17.refs_0_.refs_1_, bf16[736,128]{1,0:T(8,128)(2,1)S(1)} %get-tuple-element.84.refs_2_, ...), custom_call_target="tpu_custom_call" | custom-call | tf_op jit(solution)/shard_map/pallas_call | solution.py:607
  78.8 1.3 %collective-permute-done.27.refs_7_ = bf16[224,128]{1,0:T(8,128)(2,1)S(1)} collective-permute-done((bf16[224,128]{1,0:T(8,128)(2,1)S(1)}, bf16[224,128]{1,0:T(8,128)(2,1)S(1)}, u32[]{:S(2)}, u32[]{:S(2)}) %collective-permute-start.27) | collective-permute-done | bytes 57376 | tf_op jit(solution)/shard_map/ppermute | solution.py:404
  (69 shorter events, 18.0 us)
Async XLA Ops:
  0.6 25.1 %copy-start = (bf16[27,128,128]{2,1,0:T(8,128)(2,1)S(1)}, bf16[27,128,128]{2,1,0:T(8,128)(2,1)}, u32[]{:S(2)}) copy-start(bf16[27,128,128]{2,1,0:T(8,128)(2,1)} %param.16) | copy-start | bytes 2654212
  0.6 7.0 %collective-permute-start = (s32[8,16]{1,0:T(8,128)}, s32[8,16]{1,0:T(8,128)S(1)}, u32[]{:S(2)}, u32[]{:S(2)}) collective-permute-start(s32[8,16]{1,0:T(8,128)} %bitcast.40), channel_id=1, source_target_pairs={{0,4},{4,0},{8,12},{12,8},{1,5},{5,1},{9,13},{13,9},{2,6},{6,2},{1... | collective-permute-start | bytes 1544 | tf_op jit(solution)/shard_map/ppermute | solution.py:399
  3.7 4.7 %collective-permute-start.1 = (s32[8,16]{1,0:T(8,128)}, s32[8,16]{1,0:T(8,128)S(1)}, u32[]{:S(2)}, u32[]{:S(2)}) collective-permute-start(s32[8,16]{1,0:T(8,128)} %bitcast.41), channel_id=1, source_target_pairs={{0,8},{4,12},{8,0},{12,4},{1,9},{5,13},{9,1},{13,5},{2,10},{6,14},... | collective-permute-start | bytes 1544 | tf_op jit(solution)/shard_map/ppermute | solution.py:399
  6.3 5.6 %collective-permute-start.2 = (s32[8,16]{1,0:T(8,128)}, s32[8,16]{1,0:T(8,128)S(1)}, u32[]{:S(2)}, u32[]{:S(2)}) collective-permute-start(s32[8,16]{1,0:T(8,128)} %bitcast.42), channel_id=1, source_target_pairs={{0,12},{4,8},{8,4},{12,0},{1,13},{5,9},{9,5},{13,1},{2,14},{6,10},... | collective-permute-start | bytes 1544 | tf_op jit(solution)/shard_map/ppermute | solution.py:399
  7.6 4.3 %copy-start.3 = (s32[1,8,16]{2,1,0:T(8,128)S(1)}, s32[1,8,16]{2,1,0:T(8,128)}, u32[]{:S(2)}) copy-start(s32[1,8,16]{2,1,0:T(8,128)} %param.11) | copy-start | bytes 1540
  12.0 3.8 %collective-permute-start.3 = (s32[4,8,16]{2,1,0:T(8,128)S(1)}, s32[4,8,16]{2,1,0:T(8,128)S(1)}, u32[]{:S(2)}, u32[]{:S(2)}) collective-permute-start(s32[4,8,16]{2,1,0:T(8,128)S(1)} %pad_add_fusion), channel_id=1, source_target_pairs={{0,2},{2,0},{1,3},{3,1},{4,6},{6,4},{5,7},{7,5},{8,10},{10,8},{9,1... | collective-permute-start | bytes 6152 | tf_op jit(solution)/shard_map/ppermute | solution.py:404
  17.0 3.4 %copy-start.5 = (s32[1,27,128]{2,0,1:T(1,128)S(1)}, s32[1,27,128]{2,0,1:T(1,128)}, u32[]{:S(2)}) copy-start(s32[1,27,128]{2,0,1:T(1,128)} %param.14) | copy-start | bytes 41476
  17.0 5.0 %collective-permute-start.6 = (bf16[8,64,128]{2,1,0:T(8,128)(2,1)S(1)}, bf16[8,64,128]{2,1,0:T(8,128)(2,1)S(1)}, u32[]{:S(2)}, u32[]{:S(2)}) collective-permute-start(bf16[8,64,128]{2,1,0:T(8,128)(2,1)S(1)} %shard_map.116), channel_id=1, source_target_pairs={{0,2},{2,0},{1,3},{3,1},{4,6},{6,4},{5,7},{7,5},{8,10},{10,8},{9,1... | collective-permute-start | bytes 393224 | tf_op jit(solution)/shard_map/ppermute | solution.py:404
  19.8 5.0 %collective-permute-start.4 = (bf16[8,64,128]{2,1,0:T(8,128)(2,1)S(1)}, bf16[8,64,128]{2,1,0:T(8,128)(2,1)S(1)}, u32[]{:S(2)}, u32[]{:S(2)}) collective-permute-start(bf16[8,64,128]{2,1,0:T(8,128)(2,1)S(1)} %shard_map.114), channel_id=1, source_target_pairs={{0,2},{2,0},{1,3},{3,1},{4,6},{6,4},{5,7},{7,5},{8,10},{10,8},{9,1... | collective-permute-start | bytes 393224 | tf_op jit(solution)/shard_map/ppermute | solution.py:404
  22.1 5.8 %collective-permute-start.7 = (bf16[4,64,128]{2,1,0:T(8,128)(2,1)S(1)}, bf16[4,64,128]{2,1,0:T(8,128)(2,1)S(1)}, u32[]{:S(2)}, u32[]{:S(2)}) collective-permute-start(bf16[4,64,128]{2,1,0:T(8,128)(2,1)S(1)} %get-tuple-element.53), channel_id=1, source_target_pairs={{0,8},{4,12},{8,0},{12,4},{1,9},{5,13},{9,1},{13,5},{2,10},{6,14},... | collective-permute-start | bytes 196616 | tf_op jit(solution)/shard_map/ppermute | solution.py:399
  22.2 6.2 %collective-permute-start.8 = (bf16[4,64,128]{2,1,0:T(8,128)(2,1)S(1)}, bf16[4,64,128]{2,1,0:T(8,128)(2,1)S(1)}, u32[]{:S(2)}, u32[]{:S(2)}) collective-permute-start(bf16[4,64,128]{2,1,0:T(8,128)(2,1)S(1)} %get-tuple-element.54), channel_id=1, source_target_pairs={{0,12},{4,8},{8,4},{12,0},{1,13},{5,9},{9,5},{13,1},{2,14},{6,10},... | collective-permute-start | bytes 196616 | tf_op jit(solution)/shard_map/ppermute | solution.py:399
  24.9 4.3 %collective-permute-start.5 = (bf16[4,64,128]{2,1,0:T(8,128)(2,1)S(1)}, bf16[4,64,128]{2,1,0:T(8,128)(2,1)S(1)}, u32[]{:S(2)}, u32[]{:S(2)}) collective-permute-start(bf16[4,64,128]{2,1,0:T(8,128)(2,1)S(1)} %get-tuple-element.51), channel_id=1, source_target_pairs={{0,4},{4,0},{8,12},{12,8},{1,5},{5,1},{9,13},{13,9},{2,6},{6,2},{1... | collective-permute-start | bytes 196616 | tf_op jit(solution)/shard_map/ppermute | solution.py:399
  29.8 5.5 %collective-permute-start.10 = (bf16[2,64,128]{2,1,0:T(8,128)(2,1)S(1)}, bf16[2,64,128]{2,1,0:T(8,128)(2,1)S(1)}, u32[]{:S(2)}, u32[]{:S(2)}) collective-permute-start(bf16[2,64,128]{2,1,0:T(8,128)(2,1)S(1)} %get-tuple-element.61), channel_id=1, source_target_pairs={{4,8},{8,4},{5,9},{9,5},{6,10},{10,6},{7,11},{11,7},{20,24},{24,20... | collective-permute-start | bytes 98312 | tf_op jit(solution)/shard_map/ppermute | solution.py:393
  30.5 4.8 %collective-permute-start.11 = (bf16[2,64,128]{2,1,0:T(8,128)(2,1)S(1)}, bf16[2,64,128]{2,1,0:T(8,128)(2,1)S(1)}, u32[]{:S(2)}, u32[]{:S(2)}) collective-permute-start(bf16[2,64,128]{2,1,0:T(8,128)(2,1)S(1)} %get-tuple-element.62), channel_id=1, source_target_pairs={{0,2},{2,0},{1,3},{3,1},{4,6},{6,4},{5,7},{7,5},{8,10},{10,8},{9,1... | collective-permute-start | bytes 98312 | tf_op jit(solution)/shard_map/ppermute | solution.py:393
  31.8 4.3 %collective-permute-start.9 = (bf16[2,64,128]{2,1,0:T(8,128)(2,1)S(1)}, bf16[2,64,128]{2,1,0:T(8,128)(2,1)S(1)}, u32[]{:S(2)}, u32[]{:S(2)}) collective-permute-start(bf16[2,64,128]{2,1,0:T(8,128)(2,1)S(1)} %get-tuple-element.60), channel_id=1, source_target_pairs={{0,4},{4,0},{8,12},{12,8},{1,5},{5,1},{9,13},{13,9},{2,6},{6,2},{1... | collective-permute-start | bytes 98312 | tf_op jit(solution)/shard_map/ppermute | solution.py:393
  37.7 2.1 %collective-permute-start.12 = (f32[128,512]{1,0:T(8,128)S(1)}, f32[128,512]{1,0:T(8,128)S(1)}, u32[]{:S(2)}, u32[]{:S(2)}) collective-permute-start(f32[128,512]{1,0:T(8,128)S(1)} %get-tuple-element.63.refs_0_), channel_id=1, source_target_pairs={{0,1},{1,0},{2,3},{3,2},{4,5},{5,4},{6,7},{7,6},{8,9},{9,8},{10,11... | collective-permute-start | bytes 786440 | tf_op jit(solution)/shard_map/ppermute | solution.py:550
  41.9 8.8 %collective-permute-start.13 = (bf16[896,128]{1,0:T(8,128)(2,1)S(1)}, bf16[896,128]{1,0:T(8,128)(2,1)S(1)}, u32[]{:S(2)}, u32[]{:S(2)}) collective-permute-start(bf16[896,128]{1,0:T(8,128)(2,1)S(1)} %get-tuple-element.69), channel_id=1, source_target_pairs={{0,2},{2,0},{1,3},{3,1},{4,6},{6,4},{5,7},{7,5},{8,10},{10,8},{9,1... | collective-permute-start | bytes 688136 | tf_op jit(solution)/shard_map/ppermute | solution.py:404
  43.9 4.3 %collective-permute-start.14 = (bf16[2,64,128]{2,1,0:T(8,128)(2,1)S(1)}, bf16[2,64,128]{2,1,0:T(8,128)(2,1)S(1)}, u32[]{:S(2)}, u32[]{:S(2)}) collective-permute-start(bf16[2,64,128]{2,1,0:T(8,128)(2,1)S(1)} %get-tuple-element.70), channel_id=1, source_target_pairs={{0,4},{4,0},{8,12},{12,8},{1,5},{5,1},{9,13},{13,9},{2,6},{6,2},{1... | collective-permute-start | bytes 98312 | tf_op jit(solution)/shard_map/ppermute | solution.py:393
  46.0 2.2 %collective-permute-start.15 = (bf16[2,64,128]{2,1,0:T(8,128)(2,1)S(1)}, bf16[2,64,128]{2,1,0:T(8,128)(2,1)S(1)}, u32[]{:S(2)}, u32[]{:S(2)}) collective-permute-start(bf16[2,64,128]{2,1,0:T(8,128)(2,1)S(1)} %get-tuple-element.71), channel_id=1, source_target_pairs={{4,8},{8,4},{5,9},{9,5},{6,10},{10,6},{7,11},{11,7},{20,24},{24,20... | collective-permute-start | bytes 98312 | tf_op jit(solution)/shard_map/ppermute | solution.py:393
  46.7 4.0 %collective-permute-start.16 = (bf16[2,64,128]{2,1,0:T(8,128)(2,1)S(1)}, bf16[2,64,128]{2,1,0:T(8,128)(2,1)S(1)}, u32[]{:S(2)}, u32[]{:S(2)}) collective-permute-start(bf16[2,64,128]{2,1,0:T(8,128)(2,1)S(1)} %get-tuple-element.72), channel_id=1, source_target_pairs={{0,2},{2,0},{1,3},{3,1},{4,6},{6,4},{5,7},{7,5},{8,10},{10,8},{9,1... | collective-permute-start | bytes 98312 | tf_op jit(solution)/shard_map/ppermute | solution.py:393
  51.4 7.4 %collective-permute-start.17 = (bf16[480,128]{1,0:T(8,128)(2,1)S(1)}, bf16[480,128]{1,0:T(8,128)(2,1)S(1)}, u32[]{:S(2)}, u32[]{:S(2)}) collective-permute-start(bf16[480,128]{1,0:T(8,128)(2,1)S(1)} %get-tuple-element.74), channel_id=1, source_target_pairs={{0,4},{4,0},{8,12},{12,8},{1,5},{5,1},{9,13},{13,9},{2,6},{6,2},{1... | collective-permute-start | bytes 368648 | tf_op jit(solution)/shard_map/ppermute | solution.py:399
  54.6 11.1 %collective-permute-start.18 = (bf16[480,128]{1,0:T(8,128)(2,1)S(1)}, bf16[480,128]{1,0:T(8,128)(2,1)S(1)}, u32[]{:S(2)}, u32[]{:S(2)}) collective-permute-start(bf16[480,128]{1,0:T(8,128)(2,1)S(1)} %get-tuple-element.75), channel_id=1, source_target_pairs={{0,8},{4,12},{8,0},{12,4},{1,9},{5,13},{9,1},{13,5},{2,10},{6,14},... | collective-permute-start | bytes 368648 | tf_op jit(solution)/shard_map/ppermute | solution.py:399
  54.8 10.9 %collective-permute-start.19 = (bf16[480,128]{1,0:T(8,128)(2,1)S(1)}, bf16[480,128]{1,0:T(8,128)(2,1)S(1)}, u32[]{:S(2)}, u32[]{:S(2)}) collective-permute-start(bf16[480,128]{1,0:T(8,128)(2,1)S(1)} %get-tuple-element.76), channel_id=1, source_target_pairs={{0,12},{4,8},{8,4},{12,0},{1,13},{5,9},{9,5},{13,1},{2,14},{6,10},... | collective-permute-start | bytes 368648 | tf_op jit(solution)/shard_map/ppermute | solution.py:399
  58.8 6.9 %collective-permute-start.21 = (bf16[480,128]{1,0:T(8,128)(2,1)S(1)}, bf16[480,128]{1,0:T(8,128)(2,1)S(1)}, u32[]{:S(2)}, u32[]{:S(2)}) collective-permute-start(bf16[480,128]{1,0:T(8,128)(2,1)S(1)} %collective-permute-done.17.refs_0_.refs_1_), channel_id=1, source_target_pairs={{0,2},{2,0},{1,3},{3,1},{4,6},{6,4},{5,7},{7,5},{8,10},{10,8},{9,1... | collective-permute-start | bytes 368648 | tf_op jit(solution)/shard_map/ppermute | solution.py:404
  59.9 4.5 %collective-permute-start.20 = (bf16[256,128]{1,0:T(8,128)(2,1)S(1)}, bf16[256,128]{1,0:T(8,128)(2,1)S(1)}, u32[]{:S(2)}, u32[]{:S(2)}) collective-permute-start(bf16[256,128]{1,0:T(8,128)(2,1)S(1)} %get-tuple-element.77.refs_0_), channel_id=1, source_target_pairs={{0,2},{2,0},{1,3},{3,1},{4,6},{6,4},{5,7},{7,5},{8,10},{10,8},{9,1... | collective-permute-start | bytes 196616 | tf_op jit(solution)/shard_map/ppermute | solution.py:404
  65.8 10.9 %collective-permute-start.28 = (bf16[736,128]{1,0:T(8,128)(2,1)S(1)}, bf16[736,128]{1,0:T(8,128)(2,1)S(1)}, u32[]{:S(2)}, u32[]{:S(2)}) collective-permute-start(bf16[736,128]{1,0:T(8,128)(2,1)S(1)} %get-tuple-element.84.refs_2_), channel_id=1, source_target_pairs={{0,2},{2,0},{1,3},{3,1},{4,6},{6,4},{5,7},{7,5},{8,10},{10,8},{9,1... | collective-permute-start | bytes 565256 | tf_op jit(solution)/shard_map/ppermute | solution.py:404
  66.9 4.6 %collective-permute-start.22 = (bf16[224,128]{1,0:T(8,128)(2,1)S(1)}, bf16[224,128]{1,0:T(8,128)(2,1)S(1)}, u32[]{:S(2)}, u32[]{:S(2)}) collective-permute-start(bf16[224,128]{1,0:T(8,128)(2,1)S(1)} %get-tuple-element.82.refs_0_), channel_id=1, source_target_pairs={{0,4},{4,0},{8,12},{12,8},{1,5},{5,1},{9,13},{13,9},{2,6},{6,2},{1... | collective-permute-start | bytes 172040 | tf_op jit(solution)/shard_map/ppermute | solution.py:399
  69.1 5.5 %collective-permute-start.24 = (bf16[224,128]{1,0:T(8,128)(2,1)S(1)}, bf16[224,128]{1,0:T(8,128)(2,1)S(1)}, u32[]{:S(2)}, u32[]{:S(2)}) collective-permute-start(bf16[224,128]{1,0:T(8,128)(2,1)S(1)} %get-tuple-element.82.refs_0_), channel_id=1, source_target_pairs={{0,8},{4,12},{8,0},{12,4},{1,9},{5,13},{9,1},{13,5},{2,10},{6,14},... | collective-permute-start | bytes 172040 | tf_op jit(solution)/shard_map/ppermute | solution.py:399
  69.1 6.8 %collective-permute-start.26 = (bf16[224,128]{1,0:T(8,128)(2,1)S(1)}, bf16[224,128]{1,0:T(8,128)(2,1)S(1)}, u32[]{:S(2)}, u32[]{:S(2)}) collective-permute-start(bf16[224,128]{1,0:T(8,128)(2,1)S(1)} %get-tuple-element.82.refs_0_), channel_id=1, source_target_pairs={{0,12},{4,8},{8,4},{12,0},{1,13},{5,9},{9,5},{13,1},{2,14},{6,10},... | collective-permute-start | bytes 172040 | tf_op jit(solution)/shard_map/ppermute | solution.py:399
  71.5 6.8 %collective-permute-start.23 = (bf16[224,128]{1,0:T(8,128)(2,1)S(1)}, bf16[224,128]{1,0:T(8,128)(2,1)S(1)}, u32[]{:S(2)}, u32[]{:S(2)}) collective-permute-start(bf16[224,128]{1,0:T(8,128)(2,1)S(1)} %collective-permute-done.22.refs_1_), channel_id=1, source_target_pairs={{0,2},{2,0},{1,3},{3,1},{4,6},{6,4},{5,7},{7,5},{8,10},{10,8},{9,1... | collective-permute-start | bytes 172040 | tf_op jit(solution)/shard_map/ppermute | solution.py:404
  74.6 4.2 %collective-permute-start.25 = (bf16[224,128]{1,0:T(8,128)(2,1)S(1)}, bf16[224,128]{1,0:T(8,128)(2,1)S(1)}, u32[]{:S(2)}, u32[]{:S(2)}) collective-permute-start(bf16[224,128]{1,0:T(8,128)(2,1)S(1)} %collective-permute-done.24.refs_2_), channel_id=1, source_target_pairs={{0,2},{2,0},{1,3},{3,1},{4,6},{6,4},{5,7},{7,5},{8,10},{10,8},{9,1... | collective-permute-start | bytes 172040 | tf_op jit(solution)/shard_map/ppermute | solution.py:404
  75.9 4.2 %collective-permute-start.27 = (bf16[224,128]{1,0:T(8,128)(2,1)S(1)}, bf16[224,128]{1,0:T(8,128)(2,1)S(1)}, u32[]{:S(2)}, u32[]{:S(2)}) collective-permute-start(bf16[224,128]{1,0:T(8,128)(2,1)S(1)} %collective-permute-done.26.refs_3_), channel_id=1, source_target_pairs={{0,2},{2,0},{1,3},{3,1},{4,6},{6,4},{5,7},{7,5},{8,10},{10,8},{9,1... | collective-permute-start | bytes 172040 | tf_op jit(solution)/shard_map/ppermute | solution.py:404
  (6 other events, 10.0 us)

commit v7 on v6

--- a/solution.py
+++ b/solution.py
@@ -384,8 +384,8 @@
             else:
                 shard = far[d - 1][...]
             start = pl.multiple_of(((j ^ jx) * tile_rows + (i ^ d)) * rows, rows)
-            held[pl.ds(start, rows), :] = shard.astype(F32) * scale
-    out_ref[...] = held[: out_ref.shape[0], :]
+            held[pl.ds(start, rows), :] = shard
+    out_ref[...] = held[: out_ref.shape[0], :].astype(F32) * scale
 
 
 def swap_all(swaps, arrays):
@@ -619,7 +619,7 @@
             out_shape=shape((offsets * half, channels), F32),
             in_specs=[VMEM] * (2 * tile_rows),
             out_specs=VMEM,
-            scratch_shapes=[pltpu.VMEM((padded * half, channels), F32)],
+            scratch_shapes=[pltpu.VMEM((padded * half, channels), BF16)],
             compiler_params=PARAMS,
         )(*shards, other_bulk, *far_shards)
     else:

time: 81.4 us -> 81.4 us (level)
  no operation moved by 1% of the time
where the time goes in v7:
time: 81.4 us; the launch traced here: 81.2 us
  starting transfers between devices  37.4 us (46%)
  waiting for transfers between devices  22.3 us (27%)
  Pallas kernels  15.8 us (19%)
  local copies, waits for them, and re-layouts  2.68 us (3%)
  blocking collectives  2.03 us (2%)
  between operations  0.9 us (1%)
    ppermute x12, starting transfers between devices, to_rows(): lax.ppermute(arrays[d], 'tile', xor_pairs(tile_rows, d))  18.1 us
    ppermute x12, waiting for transfers between devices, to_rows(): lax.ppermute(arrays[d], 'tile', xor_pairs(tile_rows, d))  10.7 us
    ppermute x10, starting transfers between devices, across(): return lax.ppermute(array, 'depth', [(0, 1), (1, 0)])  10.6 us
    ppermute x6, starting transfers between devices, swap_all(): lax.ppermute(array, axis, pairs)  8.66 us
    ppermute x10, waiting for transfers between devices, across(): return lax.ppermute(array, 'depth', [(0, 1), (1, 0)])  8.35 us
    ppermute x6, waiting for transfers between devices, swap_all(): lax.ppermute(array, axis, pairs)  3.25 us
    pallas_call x2, Pallas kernels, far_sums(): pl.pallas_call(functools.partial(far_kernel, rows_away, depths, tile_bloc...  2.42 us
    pallas_call x1, Pallas kernels, local(): pl.pallas_call(functools.partial(place_kernel, tile_rows, depths, tile_bl...  2.04 us
  transfers between devices with their start and end apart: 29, of which 14 were waited for; matrix products, arithmetic and copies ran while one was open for 1% of the time, Pallas kernels for 10%

profile of v7, /device:TPU:0, one launch (start us, length us, event | category | flops | bytes accessed | tf_op | source)
XLA Modules:
  0.0 81.2 jit_solution(8347993073403030759)
XLA Ops:
  0.6 3.1 %collective-permute-start = (s32[8,16]{1,0:T(8,128)}, s32[8,16]{1,0:T(8,128)S(1)}, u32[]{:S(2)}, u32[]{:S(2)}) collective-permute-start(s32[8,16]{1,0:T(8,128)} %bitcast.40), channel_id=1, source_target_pairs={{0,4},{4,0},{8,12},{12,8},{1,5},{5,1},{9,13},{13,9},{2,6},{6,2},{1... | collective-permute-start | bytes 1544 | tf_op jit(solution)/shard_map/ppermute | solution.py:399
  3.7 2.6 %collective-permute-start.1 = (s32[8,16]{1,0:T(8,128)}, s32[8,16]{1,0:T(8,128)S(1)}, u32[]{:S(2)}, u32[]{:S(2)}) collective-permute-start(s32[8,16]{1,0:T(8,128)} %bitcast.41), channel_id=1, source_target_pairs={{0,8},{4,12},{8,0},{12,4},{1,9},{5,13},{9,1},{13,5},{2,10},{6,14},... | collective-permute-start | bytes 1544 | tf_op jit(solution)/shard_map/ppermute | solution.py:399
  6.3 1.2 %copy-done.1 = bf16[1,64,64,128]{3,2,1,0:T(8,128)(2,1)S(1)} copy-done((bf16[1,64,64,128]{3,2,1,0:T(8,128)(2,1)S(1)}, bf16[1,64,64,128]{3,2,1,0:T(8,128)(2,1)}, u32[]{:S(2)}) %copy-start.1) | copy-done | bytes 1048600
  8.5 3.5 %collective-permute-done.2.refs_4_ = s32[8,16]{1,0:T(8,128)S(1)} collective-permute-done((s32[8,16]{1,0:T(8,128)}, s32[8,16]{1,0:T(8,128)S(1)}, u32[]{:S(2)}, u32[]{:S(2)}) %collective-permute-start.2) | collective-permute-done | bytes 544 | tf_op jit(solution)/shard_map/ppermute | solution.py:399
  12.0 1.6 %collective-permute-start.3 = (s32[4,8,16]{2,1,0:T(8,128)S(1)}, s32[4,8,16]{2,1,0:T(8,128)S(1)}, u32[]{:S(2)}, u32[]{:S(2)}) collective-permute-start(s32[4,8,16]{2,1,0:T(8,128)S(1)} %pad_add_fusion), channel_id=1, source_target_pairs={{0,2},{2,0},{1,3},{3,1},{4,6},{6,4},{5,7},{7,5},{8,10},{10,8},{9,1... | collective-permute-start | bytes 6152 | tf_op jit(solution)/shard_map/ppermute | solution.py:404
  14.3 1.5 %collective-permute-done.3.far_ref.refs_5_ = s32[4,8,16]{2,1,0:T(8,128)S(1)} collective-permute-done((s32[4,8,16]{2,1,0:T(8,128)S(1)}, s32[4,8,16]{2,1,0:T(8,128)S(1)}, u32[]{:S(2)}, u32[]{:S(2)}) %collective-permute-start.3) | collective-permute-done | bytes 2080 | tf_op jit(solution)/shard_map/ppermute | solution.py:404
  15.8 1.2 %shard_map.116 = bf16[8,64,128]{2,1,0:T(8,128)(2,1)S(1)} custom-call(s32[8,16]{1,0:T(8,128)S(1)} %bitcast.36, s32[4,8,16]{2,1,0:T(8,128)S(1)} %collective-permute-done.3.far_ref.refs_5_, bf16[64,64,128]{2,1,0:T(8,128)(2,1)S(1)} %shard_map.112.refs_5_.log_ref), custom_call_target="tpu_custom_call" | custom-call | tf_op jit(solution)/shard_map/pallas_call | solution.py:467
  17.0 1.6 %collective-permute-start.6 = (bf16[8,64,128]{2,1,0:T(8,128)(2,1)S(1)}, bf16[8,64,128]{2,1,0:T(8,128)(2,1)S(1)}, u32[]{:S(2)}, u32[]{:S(2)}) collective-permute-start(bf16[8,64,128]{2,1,0:T(8,128)(2,1)S(1)} %shard_map.116), channel_id=1, source_target_pairs={{0,2},{2,0},{1,3},{3,1},{4,6},{6,4},{5,7},{7,5},{8,10},{10,8},{9,1... | collective-permute-start | bytes 393224 | tf_op jit(solution)/shard_map/ppermute | solution.py:404
  18.6 1.2 %shard_map.114 = bf16[8,64,128]{2,1,0:T(8,128)(2,1)S(1)} custom-call(s32[8,16]{1,0:T(8,128)S(1)} %bitcast.37, s32[4,8,16]{2,1,0:T(8,128)S(1)} %collective-permute-done.3.far_ref.refs_5_, bf16[64,64,128]{2,1,0:T(8,128)(2,1)S(1)} %shard_map.112.refs_5_.log_ref), custom_call_target="tpu_custom_call" | custom-call | tf_op jit(solution)/shard_map/pallas_call | solution.py:467
  20.5 1.5 %shard_map.113 = (f32[8,64,128]{2,1,0:T(8,128)S(1)}, f32[8,64,128]{2,1,0:T(8,128)S(1)}) custom-call(s32[8,16]{1,0:T(8,128)S(1)} %bitcast.38, s32[8,16]{1,0:T(8,128)S(1)} %bitcast.43, s32[8,16]{1,0:T(8,128)S(1)} %collective-permute-done.refs_2_, s32[8,16]{1,0:T(8,128)S(1)} %collective-permute-done.1.refs_3_, s32[8,16]{1,0:T(8,128)S(1)} %collective-permute-done.2.refs_4_, ...), custom_call_target="tpu_custom_call" | custom-call | tf_op jit(solution)/shard_map/pallas_call | solution.py:478
  23.4 1.5 %collective-permute-done.4.far_ref = bf16[8,64,128]{2,1,0:T(8,128)(2,1)S(1)} collective-permute-done((bf16[8,64,128]{2,1,0:T(8,128)(2,1)S(1)}, bf16[8,64,128]{2,1,0:T(8,128)(2,1)S(1)}, u32[]{:S(2)}, u32[]{:S(2)}) %collective-permute-start.4) | collective-permute-done | bytes 131104 | tf_op jit(solution)/shard_map/ppermute | solution.py:404
  25.8 2.0 %shard_map.118.place_ref = s32[65]{0:T(128)S(1)} custom-call(s32[8,16]{1,0:T(8,128)S(1)} %bitcast.39, s32[8,16]{1,0:T(8,128)S(1)} %bitcast.44, s32[8,16]{1,0:T(8,128)S(1)} %collective-permute-done.refs_2_, s32[8,16]{1,0:T(8,128)S(1)} %collective-permute-done.1.refs_3_, s32[8,16]{1,0:T(8,128)S(1)} %collective-permute-done.2.refs_4_, ...), custom_call_target="tpu_custom_call" | custom-call | tf_op jit(solution)/shard_map/pallas_call | solution.py:485
  30.5 1.3 %collective-permute-start.11 = (bf16[2,64,128]{2,1,0:T(8,128)(2,1)S(1)}, bf16[2,64,128]{2,1,0:T(8,128)(2,1)S(1)}, u32[]{:S(2)}, u32[]{:S(2)}) collective-permute-start(bf16[2,64,128]{2,1,0:T(8,128)(2,1)S(1)} %get-tuple-element.62), channel_id=1, source_target_pairs={{0,2},{2,0},{1,3},{3,1},{4,6},{6,4},{5,7},{7,5},{8,10},{10,8},{9,1... | collective-permute-start | bytes 98312 | tf_op jit(solution)/shard_map/ppermute | solution.py:393
  31.8 2.4 %collective-permute-start.9 = (bf16[2,64,128]{2,1,0:T(8,128)(2,1)S(1)}, bf16[2,64,128]{2,1,0:T(8,128)(2,1)S(1)}, u32[]{:S(2)}, u32[]{:S(2)}) collective-permute-start(bf16[2,64,128]{2,1,0:T(8,128)(2,1)S(1)} %get-tuple-element.60), channel_id=1, source_target_pairs={{0,4},{4,0},{8,12},{12,8},{1,5},{5,1},{9,13},{13,9},{2,6},{6,2},{1... | collective-permute-start | bytes 98312 | tf_op jit(solution)/shard_map/ppermute | solution.py:393
  36.1 1.7 %shard_map.121 = (f32[128,512]{1,0:T(8,128)S(1)}, bf16[64,3584]{1,0:T(8,128)(2,1)S(1)}) custom-call(bf16[64,3584]{1,0:T(8,128)(2,1)S(1)} %shard_map.120.refs_0_, s32[28,128]{1,0:T(8,128)S(1)} %pad.11.source_ref.refs_1_, s32[28,128]{1,0:T(8,128)S(1)} %pad.12.refs_2_.refs_3_, bf16[28,128,64]{2,1,0:T(8,128)(2,1)S(1)} %copy.13.refs_3_, ...), custom_call_target="tpu_custom_call" | custom-call | tf_op jit(solution)/shard_map/pallas_call | solution.py:539
  37.8 2.0 %all-gather = bf16[1,4,128,128]{3,2,1,0:T(8,128)(2,1)S(1)} all-gather(bf16[1,4,64,128]{3,2,1,0:T(8,128)(2,1)S(1)} %copy-done.4), channel_id=2, replica_groups=mesh['groups'=2,'tile'=4,'depth'=2,'chan'=2] {'chan'}, dimensions={2}, use_global_device_ids=true | all-gather | bytes 196608 | tf_op jit(solution)/shard_map/all_gather | solution.py:449
  39.9 2.0 %shard_map.122 = (bf16[4,64,128]{2,1,0:T(8,128)(2,1)}, bf16[128,3584]{1,0:T(8,128)(2,1)S(1)}, f32[896,128]{1,0:T(8,128)S(1)}, bf16[896,128]{1,0:T(8,128)(2,1)S(1)}) custom-call(f32[128,512]{1,0:T(8,128)S(1)} %get-tuple-element.63.refs_0_, f32[128,512]{1,0:T(8,128)S(1)} %collective-permute-done.12.refs_1_, bf16[4,128,128]{2,1,0:T(8,128)(2,1)S(1)} %bitcast.35, ...), custom_call_target="tpu_custom_call" | custom-call | tf_op jit(solution)/shard_map/pallas_call | solution.py:554
  42.4 1.5 %shard_map.123 = (f32[4,64,128]{2,1,0:T(8,128)S(1)}, bf16[2,64,128]{2,1,0:T(8,128)(2,1)S(1)}, bf16[2,64,128]{2,1,0:T(8,128)(2,1)S(1)}, bf16[2,64,128]{2,1,0:T(8,128)(2,1)S(1)}) custom-call(bf16[128,3584]{1,0:T(8,128)(2,1)S(1)} %get-tuple-element.66.grad_columns_ref, s32[28,128]{1,0:T(8,128)S(1)} %pad.11.source_ref.refs_1_, ...), custom_call_target="tpu_custom_call" | custom-call | tf_op jit(solution)/shard_map/pallas_call | solution.py:564
  43.9 2.1 %collective-permute-start.14 = (bf16[2,64,128]{2,1,0:T(8,128)(2,1)S(1)}, bf16[2,64,128]{2,1,0:T(8,128)(2,1)S(1)}, u32[]{:S(2)}, u32[]{:S(2)}) collective-permute-start(bf16[2,64,128]{2,1,0:T(8,128)(2,1)S(1)} %get-tuple-element.70), channel_id=1, source_target_pairs={{0,4},{4,0},{8,12},{12,8},{1,5},{5,1},{9,13},{13,9},{2,6},{6,2},{1... | collective-permute-start | bytes 98312 | tf_op jit(solution)/shard_map/ppermute | solution.py:393
  46.7 1.5 %collective-permute-start.16 = (bf16[2,64,128]{2,1,0:T(8,128)(2,1)S(1)}, bf16[2,64,128]{2,1,0:T(8,128)(2,1)S(1)}, u32[]{:S(2)}, u32[]{:S(2)}) collective-permute-start(bf16[2,64,128]{2,1,0:T(8,128)(2,1)S(1)} %get-tuple-element.72), channel_id=1, source_target_pairs={{0,2},{2,0},{1,3},{3,1},{4,6},{6,4},{5,7},{7,5},{8,10},{10,8},{9,1... | collective-permute-start | bytes 98312 | tf_op jit(solution)/shard_map/ppermute | solution.py:393
  48.2 2.4 %collective-permute-done.16.refs_2_ = bf16[2,64,128]{2,1,0:T(8,128)(2,1)S(1)} collective-permute-done((bf16[2,64,128]{2,1,0:T(8,128)(2,1)S(1)}, bf16[2,64,128]{2,1,0:T(8,128)(2,1)S(1)}, u32[]{:S(2)}, u32[]{:S(2)}) %collective-permute-start.16) | collective-permute-done | bytes 32800 | tf_op jit(solution)/shard_map/ppermute | solution.py:393
  51.4 3.2 %collective-permute-start.17 = (bf16[480,128]{1,0:T(8,128)(2,1)S(1)}, bf16[480,128]{1,0:T(8,128)(2,1)S(1)}, u32[]{:S(2)}, u32[]{:S(2)}) collective-permute-start(bf16[480,128]{1,0:T(8,128)(2,1)S(1)} %get-tuple-element.74), channel_id=1, source_target_pairs={{0,4},{4,0},{8,12},{12,8},{1,5},{5,1},{9,13},{13,9},{2,6},{6,2},{1... | collective-permute-start | bytes 368648 | tf_op jit(solution)/shard_map/ppermute | solution.py:399
  54.8 2.3 %collective-permute-start.19 = (bf16[480,128]{1,0:T(8,128)(2,1)S(1)}, bf16[480,128]{1,0:T(8,128)(2,1)S(1)}, u32[]{:S(2)}, u32[]{:S(2)}) collective-permute-start(bf16[480,128]{1,0:T(8,128)(2,1)S(1)} %get-tuple-element.76), channel_id=1, source_target_pairs={{0,12},{4,8},{8,4},{12,0},{1,13},{5,9},{9,5},{13,1},{2,14},{6,10},... | collective-permute-start | bytes 368648 | tf_op jit(solution)/shard_map/ppermute | solution.py:399
  57.0 1.7 %collective-permute-done.17.refs_0_.refs_1_ = bf16[480,128]{1,0:T(8,128)(2,1)S(1)} collective-permute-done((bf16[480,128]{1,0:T(8,128)(2,1)S(1)}, bf16[480,128]{1,0:T(8,128)(2,1)S(1)}, u32[]{:S(2)}, u32[]{:S(2)}) %collective-permute-start.17) | collective-permute-done | bytes 122912 | tf_op jit(solution)/shard_map/ppermute | solution.py:399
  60.8 3.6 %collective-permute-done.20.refs_3_ = bf16[256,128]{1,0:T(8,128)(2,1)S(1)} collective-permute-done((bf16[256,128]{1,0:T(8,128)(2,1)S(1)}, bf16[256,128]{1,0:T(8,128)(2,1)S(1)}, u32[]{:S(2)}, u32[]{:S(2)}) %collective-permute-start.20) | collective-permute-done | bytes 65568 | tf_op jit(solution)/shard_map/ppermute | solution.py:404
  64.4 1.3 %collective-permute-done.18.refs_1_ = bf16[480,128]{1,0:T(8,128)(2,1)S(1)} collective-permute-done((bf16[480,128]{1,0:T(8,128)(2,1)S(1)}, bf16[480,128]{1,0:T(8,128)(2,1)S(1)}, u32[]{:S(2)}, u32[]{:S(2)}) %collective-permute-start.18) | collective-permute-done | bytes 122912 | tf_op jit(solution)/shard_map/ppermute | solution.py:399
  66.9 2.2 %collective-permute-start.22 = (bf16[224,128]{1,0:T(8,128)(2,1)S(1)}, bf16[224,128]{1,0:T(8,128)(2,1)S(1)}, u32[]{:S(2)}, u32[]{:S(2)}) collective-permute-start(bf16[224,128]{1,0:T(8,128)(2,1)S(1)} %get-tuple-element.82.refs_0_), channel_id=1, source_target_pairs={{0,4},{4,0},{8,12},{12,8},{1,5},{5,1},{9,13},{13,9},{2,6},{6,2},{1... | collective-permute-start | bytes 172040 | tf_op jit(solution)/shard_map/ppermute | solution.py:399
  69.1 2.3 %collective-permute-start.26 = (bf16[224,128]{1,0:T(8,128)(2,1)S(1)}, bf16[224,128]{1,0:T(8,128)(2,1)S(1)}, u32[]{:S(2)}, u32[]{:S(2)}) collective-permute-start(bf16[224,128]{1,0:T(8,128)(2,1)S(1)} %get-tuple-element.82.refs_0_), channel_id=1, source_target_pairs={{0,12},{4,8},{8,4},{12,0},{1,13},{5,9},{9,5},{13,1},{2,14},{6,10},... | collective-permute-start | bytes 172040 | tf_op jit(solution)/shard_map/ppermute | solution.py:399
  72.6 2.0 %collective-permute-done.24.refs_2_ = bf16[224,128]{1,0:T(8,128)(2,1)S(1)} collective-permute-done((bf16[224,128]{1,0:T(8,128)(2,1)S(1)}, bf16[224,128]{1,0:T(8,128)(2,1)S(1)}, u32[]{:S(2)}, u32[]{:S(2)}) %collective-permute-start.24) | collective-permute-done | bytes 57376 | tf_op jit(solution)/shard_map/ppermute | solution.py:399
  74.6 1.3 %collective-permute-start.25 = (bf16[224,128]{1,0:T(8,128)(2,1)S(1)}, bf16[224,128]{1,0:T(8,128)(2,1)S(1)}, u32[]{:S(2)}, u32[]{:S(2)}) collective-permute-start(bf16[224,128]{1,0:T(8,128)(2,1)S(1)} %collective-permute-done.24.refs_2_), channel_id=1, source_target_pairs={{0,2},{2,0},{1,3},{3,1},{4,6},{6,4},{5,7},{7,5},{8,10},{10,8},{9,1... | collective-permute-start | bytes 172040 | tf_op jit(solution)/shard_map/ppermute | solution.py:404
  76.6 1.6 %shard_map.126 = bf16[64,64,128]{2,1,0:T(8,128)(2,1)} custom-call(s32[65]{0:T(128)S(1)} %shard_map.118.place_ref, bf16[256,128]{1,0:T(8,128)(2,1)S(1)} %get-tuple-element.77.refs_0_, bf16[480,128]{1,0:T(8,128)(2,1)S(1)} %collective-permute-done.17.refs_0_.refs_1_, bf16[736,128]{1,0:T(8,128)(2,1)S(1)} %get-tuple-element.84.refs_2_, ...), custom_call_target="tpu_custom_call" | custom-call | tf_op jit(solution)/shard_map/pallas_call | solution.py:607
  78.8 1.3 %collective-permute-done.27.refs_7_ = bf16[224,128]{1,0:T(8,128)(2,1)S(1)} collective-permute-done((bf16[224,128]{1,0:T(8,128)(2,1)S(1)}, bf16[224,128]{1,0:T(8,128)(2,1)S(1)}, u32[]{:S(2)}, u32[]{:S(2)}) %collective-permute-start.27) | collective-permute-done | bytes 57376 | tf_op jit(solution)/shard_map/ppermute | solution.py:404
  (69 shorter events, 18.0 us)
Async XLA Ops:
  0.6 25.1 %copy-start = (bf16[27,128,128]{2,1,0:T(8,128)(2,1)S(1)}, bf16[27,128,128]{2,1,0:T(8,128)(2,1)}, u32[]{:S(2)}) copy-start(bf16[27,128,128]{2,1,0:T(8,128)(2,1)} %param.16) | copy-start | bytes 2654212
  0.6 7.0 %collective-permute-start = (s32[8,16]{1,0:T(8,128)}, s32[8,16]{1,0:T(8,128)S(1)}, u32[]{:S(2)}, u32[]{:S(2)}) collective-permute-start(s32[8,16]{1,0:T(8,128)} %bitcast.40), channel_id=1, source_target_pairs={{0,4},{4,0},{8,12},{12,8},{1,5},{5,1},{9,13},{13,9},{2,6},{6,2},{1... | collective-permute-start | bytes 1544 | tf_op jit(solution)/shard_map/ppermute | solution.py:399
  3.7 4.7 %collective-permute-start.1 = (s32[8,16]{1,0:T(8,128)}, s32[8,16]{1,0:T(8,128)S(1)}, u32[]{:S(2)}, u32[]{:S(2)}) collective-permute-start(s32[8,16]{1,0:T(8,128)} %bitcast.41), channel_id=1, source_target_pairs={{0,8},{4,12},{8,0},{12,4},{1,9},{5,13},{9,1},{13,5},{2,10},{6,14},... | collective-permute-start | bytes 1544 | tf_op jit(solution)/shard_map/ppermute | solution.py:399
  6.3 5.6 %collective-permute-start.2 = (s32[8,16]{1,0:T(8,128)}, s32[8,16]{1,0:T(8,128)S(1)}, u32[]{:S(2)}, u32[]{:S(2)}) collective-permute-start(s32[8,16]{1,0:T(8,128)} %bitcast.42), channel_id=1, source_target_pairs={{0,12},{4,8},{8,4},{12,0},{1,13},{5,9},{9,5},{13,1},{2,14},{6,10},... | collective-permute-start | bytes 1544 | tf_op jit(solution)/shard_map/ppermute | solution.py:399
  7.6 4.3 %copy-start.3 = (s32[1,8,16]{2,1,0:T(8,128)S(1)}, s32[1,8,16]{2,1,0:T(8,128)}, u32[]{:S(2)}) copy-start(s32[1,8,16]{2,1,0:T(8,128)} %param.11) | copy-start | bytes 1540
  12.0 3.8 %collective-permute-start.3 = (s32[4,8,16]{2,1,0:T(8,128)S(1)}, s32[4,8,16]{2,1,0:T(8,128)S(1)}, u32[]{:S(2)}, u32[]{:S(2)}) collective-permute-start(s32[4,8,16]{2,1,0:T(8,128)S(1)} %pad_add_fusion), channel_id=1, source_target_pairs={{0,2},{2,0},{1,3},{3,1},{4,6},{6,4},{5,7},{7,5},{8,10},{10,8},{9,1... | collective-permute-start | bytes 6152 | tf_op jit(solution)/shard_map/ppermute | solution.py:404
  17.0 3.4 %copy-start.5 = (s32[1,27,128]{2,0,1:T(1,128)S(1)}, s32[1,27,128]{2,0,1:T(1,128)}, u32[]{:S(2)}) copy-start(s32[1,27,128]{2,0,1:T(1,128)} %param.14) | copy-start | bytes 41476
  17.0 5.0 %collective-permute-start.6 = (bf16[8,64,128]{2,1,0:T(8,128)(2,1)S(1)}, bf16[8,64,128]{2,1,0:T(8,128)(2,1)S(1)}, u32[]{:S(2)}, u32[]{:S(2)}) collective-permute-start(bf16[8,64,128]{2,1,0:T(8,128)(2,1)S(1)} %shard_map.116), channel_id=1, source_target_pairs={{0,2},{2,0},{1,3},{3,1},{4,6},{6,4},{5,7},{7,5},{8,10},{10,8},{9,1... | collective-permute-start | bytes 393224 | tf_op jit(solution)/shard_map/ppermute | solution.py:404
  19.8 5.0 %collective-permute-start.4 = (bf16[8,64,128]{2,1,0:T(8,128)(2,1)S(1)}, bf16[8,64,128]{2,1,0:T(8,128)(2,1)S(1)}, u32[]{:S(2)}, u32[]{:S(2)}) collective-permute-start(bf16[8,64,128]{2,1,0:T(8,128)(2,1)S(1)} %shard_map.114), channel_id=1, source_target_pairs={{0,2},{2,0},{1,3},{3,1},{4,6},{6,4},{5,7},{7,5},{8,10},{10,8},{9,1... | collective-permute-start | bytes 393224 | tf_op jit(solution)/shard_map/ppermute | solution.py:404
  22.1 5.8 %collective-permute-start.7 = (bf16[4,64,128]{2,1,0:T(8,128)(2,1)S(1)}, bf16[4,64,128]{2,1,0:T(8,128)(2,1)S(1)}, u32[]{:S(2)}, u32[]{:S(2)}) collective-permute-start(bf16[4,64,128]{2,1,0:T(8,128)(2,1)S(1)} %get-tuple-element.53), channel_id=1, source_target_pairs={{0,8},{4,12},{8,0},{12,4},{1,9},{5,13},{9,1},{13,5},{2,10},{6,14},... | collective-permute-start | bytes 196616 | tf_op jit(solution)/shard_map/ppermute | solution.py:399
  22.2 6.2 %collective-permute-start.8 = (bf16[4,64,128]{2,1,0:T(8,128)(2,1)S(1)}, bf16[4,64,128]{2,1,0:T(8,128)(2,1)S(1)}, u32[]{:S(2)}, u32[]{:S(2)}) collective-permute-start(bf16[4,64,128]{2,1,0:T(8,128)(2,1)S(1)} %get-tuple-element.54), channel_id=1, source_target_pairs={{0,12},{4,8},{8,4},{12,0},{1,13},{5,9},{9,5},{13,1},{2,14},{6,10},... | collective-permute-start | bytes 196616 | tf_op jit(solution)/shard_map/ppermute | solution.py:399
  24.9 4.3 %collective-permute-start.5 = (bf16[4,64,128]{2,1,0:T(8,128)(2,1)S(1)}, bf16[4,64,128]{2,1,0:T(8,128)(2,1)S(1)}, u32[]{:S(2)}, u32[]{:S(2)}) collective-permute-start(bf16[4,64,128]{2,1,0:T(8,128)(2,1)S(1)} %get-tuple-element.51), channel_id=1, source_target_pairs={{0,4},{4,0},{8,12},{12,8},{1,5},{5,1},{9,13},{13,9},{2,6},{6,2},{1... | collective-permute-start | bytes 196616 | tf_op jit(solution)/shard_map/ppermute | solution.py:399
  29.8 5.5 %collective-permute-start.10 = (bf16[2,64,128]{2,1,0:T(8,128)(2,1)S(1)}, bf16[2,64,128]{2,1,0:T(8,128)(2,1)S(1)}, u32[]{:S(2)}, u32[]{:S(2)}) collective-permute-start(bf16[2,64,128]{2,1,0:T(8,128)(2,1)S(1)} %get-tuple-element.61), channel_id=1, source_target_pairs={{4,8},{8,4},{5,9},{9,5},{6,10},{10,6},{7,11},{11,7},{20,24},{24,20... | collective-permute-start | bytes 98312 | tf_op jit(solution)/shard_map/ppermute | solution.py:393
  30.5 4.8 %collective-permute-start.11 = (bf16[2,64,128]{2,1,0:T(8,128)(2,1)S(1)}, bf16[2,64,128]{2,1,0:T(8,128)(2,1)S(1)}, u32[]{:S(2)}, u32[]{:S(2)}) collective-permute-start(bf16[2,64,128]{2,1,0:T(8,128)(2,1)S(1)} %get-tuple-element.62), channel_id=1, source_target_pairs={{0,2},{2,0},{1,3},{3,1},{4,6},{6,4},{5,7},{7,5},{8,10},{10,8},{9,1... | collective-permute-start | bytes 98312 | tf_op jit(solution)/shard_map/ppermute | solution.py:393
  31.8 4.3 %collective-permute-start.9 = (bf16[2,64,128]{2,1,0:T(8,128)(2,1)S(1)}, bf16[2,64,128]{2,1,0:T(8,128)(2,1)S(1)}, u32[]{:S(2)}, u32[]{:S(2)}) collective-permute-start(bf16[2,64,128]{2,1,0:T(8,128)(2,1)S(1)} %get-tuple-element.60), channel_id=1, source_target_pairs={{0,4},{4,0},{8,12},{12,8},{1,5},{5,1},{9,13},{13,9},{2,6},{6,2},{1... | collective-permute-start | bytes 98312 | tf_op jit(solution)/shard_map/ppermute | solution.py:393
  37.7 2.1 %collective-permute-start.12 = (f32[128,512]{1,0:T(8,128)S(1)}, f32[128,512]{1,0:T(8,128)S(1)}, u32[]{:S(2)}, u32[]{:S(2)}) collective-permute-start(f32[128,512]{1,0:T(8,128)S(1)} %get-tuple-element.63.refs_0_), channel_id=1, source_target_pairs={{0,1},{1,0},{2,3},{3,2},{4,5},{5,4},{6,7},{7,6},{8,9},{9,8},{10,11... | collective-permute-start | bytes 786440 | tf_op jit(solution)/shard_map/ppermute | solution.py:550
  41.9 8.8 %collective-permute-start.13 = (bf16[896,128]{1,0:T(8,128)(2,1)S(1)}, bf16[896,128]{1,0:T(8,128)(2,1)S(1)}, u32[]{:S(2)}, u32[]{:S(2)}) collective-permute-start(bf16[896,128]{1,0:T(8,128)(2,1)S(1)} %get-tuple-element.69), channel_id=1, source_target_pairs={{0,2},{2,0},{1,3},{3,1},{4,6},{6,4},{5,7},{7,5},{8,10},{10,8},{9,1... | collective-permute-start | bytes 688136 | tf_op jit(solution)/shard_map/ppermute | solution.py:404
  43.9 4.3 %collective-permute-start.14 = (bf16[2,64,128]{2,1,0:T(8,128)(2,1)S(1)}, bf16[2,64,128]{2,1,0:T(8,128)(2,1)S(1)}, u32[]{:S(2)}, u32[]{:S(2)}) collective-permute-start(bf16[2,64,128]{2,1,0:T(8,128)(2,1)S(1)} %get-tuple-element.70), channel_id=1, source_target_pairs={{0,4},{4,0},{8,12},{12,8},{1,5},{5,1},{9,13},{13,9},{2,6},{6,2},{1... | collective-permute-start | bytes 98312 | tf_op jit(solution)/shard_map/ppermute | solution.py:393
  46.0 2.2 %collective-permute-start.15 = (bf16[2,64,128]{2,1,0:T(8,128)(2,1)S(1)}, bf16[2,64,128]{2,1,0:T(8,128)(2,1)S(1)}, u32[]{:S(2)}, u32[]{:S(2)}) collective-permute-start(bf16[2,64,128]{2,1,0:T(8,128)(2,1)S(1)} %get-tuple-element.71), channel_id=1, source_target_pairs={{4,8},{8,4},{5,9},{9,5},{6,10},{10,6},{7,11},{11,7},{20,24},{24,20... | collective-permute-start | bytes 98312 | tf_op jit(solution)/shard_map/ppermute | solution.py:393
  46.7 4.0 %collective-permute-start.16 = (bf16[2,64,128]{2,1,0:T(8,128)(2,1)S(1)}, bf16[2,64,128]{2,1,0:T(8,128)(2,1)S(1)}, u32[]{:S(2)}, u32[]{:S(2)}) collective-permute-start(bf16[2,64,128]{2,1,0:T(8,128)(2,1)S(1)} %get-tuple-element.72), channel_id=1, source_target_pairs={{0,2},{2,0},{1,3},{3,1},{4,6},{6,4},{5,7},{7,5},{8,10},{10,8},{9,1... | collective-permute-start | bytes 98312 | tf_op jit(solution)/shard_map/ppermute | solution.py:393
  51.4 7.4 %collective-permute-start.17 = (bf16[480,128]{1,0:T(8,128)(2,1)S(1)}, bf16[480,128]{1,0:T(8,128)(2,1)S(1)}, u32[]{:S(2)}, u32[]{:S(2)}) collective-permute-start(bf16[480,128]{1,0:T(8,128)(2,1)S(1)} %get-tuple-element.74), channel_id=1, source_target_pairs={{0,4},{4,0},{8,12},{12,8},{1,5},{5,1},{9,13},{13,9},{2,6},{6,2},{1... | collective-permute-start | bytes 368648 | tf_op jit(solution)/shard_map/ppermute | solution.py:399
  54.6 11.1 %collective-permute-start.18 = (bf16[480,128]{1,0:T(8,128)(2,1)S(1)}, bf16[480,128]{1,0:T(8,128)(2,1)S(1)}, u32[]{:S(2)}, u32[]{:S(2)}) collective-permute-start(bf16[480,128]{1,0:T(8,128)(2,1)S(1)} %get-tuple-element.75), channel_id=1, source_target_pairs={{0,8},{4,12},{8,0},{12,4},{1,9},{5,13},{9,1},{13,5},{2,10},{6,14},... | collective-permute-start | bytes 368648 | tf_op jit(solution)/shard_map/ppermute | solution.py:399
  54.8 10.9 %collective-permute-start.19 = (bf16[480,128]{1,0:T(8,128)(2,1)S(1)}, bf16[480,128]{1,0:T(8,128)(2,1)S(1)}, u32[]{:S(2)}, u32[]{:S(2)}) collective-permute-start(bf16[480,128]{1,0:T(8,128)(2,1)S(1)} %get-tuple-element.76), channel_id=1, source_target_pairs={{0,12},{4,8},{8,4},{12,0},{1,13},{5,9},{9,5},{13,1},{2,14},{6,10},... | collective-permute-start | bytes 368648 | tf_op jit(solution)/shard_map/ppermute | solution.py:399
  58.8 6.9 %collective-permute-start.21 = (bf16[480,128]{1,0:T(8,128)(2,1)S(1)}, bf16[480,128]{1,0:T(8,128)(2,1)S(1)}, u32[]{:S(2)}, u32[]{:S(2)}) collective-permute-start(bf16[480,128]{1,0:T(8,128)(2,1)S(1)} %collective-permute-done.17.refs_0_.refs_1_), channel_id=1, source_target_pairs={{0,2},{2,0},{1,3},{3,1},{4,6},{6,4},{5,7},{7,5},{8,10},{10,8},{9,1... | collective-permute-start | bytes 368648 | tf_op jit(solution)/shard_map/ppermute | solution.py:404
  59.9 4.5 %collective-permute-start.20 = (bf16[256,128]{1,0:T(8,128)(2,1)S(1)}, bf16[256,128]{1,0:T(8,128)(2,1)S(1)}, u32[]{:S(2)}, u32[]{:S(2)}) collective-permute-start(bf16[256,128]{1,0:T(8,128)(2,1)S(1)} %get-tuple-element.77.refs_0_), channel_id=1, source_target_pairs={{0,2},{2,0},{1,3},{3,1},{4,6},{6,4},{5,7},{7,5},{8,10},{10,8},{9,1... | collective-permute-start | bytes 196616 | tf_op jit(solution)/shard_map/ppermute | solution.py:404
  65.8 10.9 %collective-permute-start.28 = (bf16[736,128]{1,0:T(8,128)(2,1)S(1)}, bf16[736,128]{1,0:T(8,128)(2,1)S(1)}, u32[]{:S(2)}, u32[]{:S(2)}) collective-permute-start(bf16[736,128]{1,0:T(8,128)(2,1)S(1)} %get-tuple-element.84.refs_2_), channel_id=1, source_target_pairs={{0,2},{2,0},{1,3},{3,1},{4,6},{6,4},{5,7},{7,5},{8,10},{10,8},{9,1... | collective-permute-start | bytes 565256 | tf_op jit(solution)/shard_map/ppermute | solution.py:404
  66.9 4.6 %collective-permute-start.22 = (bf16[224,128]{1,0:T(8,128)(2,1)S(1)}, bf16[224,128]{1,0:T(8,128)(2,1)S(1)}, u32[]{:S(2)}, u32[]{:S(2)}) collective-permute-start(bf16[224,128]{1,0:T(8,128)(2,1)S(1)} %get-tuple-element.82.refs_0_), channel_id=1, source_target_pairs={{0,4},{4,0},{8,12},{12,8},{1,5},{5,1},{9,13},{13,9},{2,6},{6,2},{1... | collective-permute-start | bytes 172040 | tf_op jit(solution)/shard_map/ppermute | solution.py:399
  69.1 5.5 %collective-permute-start.24 = (bf16[224,128]{1,0:T(8,128)(2,1)S(1)}, bf16[224,128]{1,0:T(8,128)(2,1)S(1)}, u32[]{:S(2)}, u32[]{:S(2)}) collective-permute-start(bf16[224,128]{1,0:T(8,128)(2,1)S(1)} %get-tuple-element.82.refs_0_), channel_id=1, source_target_pairs={{0,8},{4,12},{8,0},{12,4},{1,9},{5,13},{9,1},{13,5},{2,10},{6,14},... | collective-permute-start | bytes 172040 | tf_op jit(solution)/shard_map/ppermute | solution.py:399
  69.1 6.8 %collective-permute-start.26 = (bf16[224,128]{1,0:T(8,128)(2,1)S(1)}, bf16[224,128]{1,0:T(8,128)(2,1)S(1)}, u32[]{:S(2)}, u32[]{:S(2)}) collective-permute-start(bf16[224,128]{1,0:T(8,128)(2,1)S(1)} %get-tuple-element.82.refs_0_), channel_id=1, source_target_pairs={{0,12},{4,8},{8,4},{12,0},{1,13},{5,9},{9,5},{13,1},{2,14},{6,10},... | collective-permute-start | bytes 172040 | tf_op jit(solution)/shard_map/ppermute | solution.py:399
  71.5 6.8 %collective-permute-start.23 = (bf16[224,128]{1,0:T(8,128)(2,1)S(1)}, bf16[224,128]{1,0:T(8,128)(2,1)S(1)}, u32[]{:S(2)}, u32[]{:S(2)}) collective-permute-start(bf16[224,128]{1,0:T(8,128)(2,1)S(1)} %collective-permute-done.22.refs_1_), channel_id=1, source_target_pairs={{0,2},{2,0},{1,3},{3,1},{4,6},{6,4},{5,7},{7,5},{8,10},{10,8},{9,1... | collective-permute-start | bytes 172040 | tf_op jit(solution)/shard_map/ppermute | solution.py:404
  74.6 4.2 %collective-permute-start.25 = (bf16[224,128]{1,0:T(8,128)(2,1)S(1)}, bf16[224,128]{1,0:T(8,128)(2,1)S(1)}, u32[]{:S(2)}, u32[]{:S(2)}) collective-permute-start(bf16[224,128]{1,0:T(8,128)(2,1)S(1)} %collective-permute-done.24.refs_2_), channel_id=1, source_target_pairs={{0,2},{2,0},{1,3},{3,1},{4,6},{6,4},{5,7},{7,5},{8,10},{10,8},{9,1... | collective-permute-start | bytes 172040 | tf_op jit(solution)/shard_map/ppermute | solution.py:404
  75.9 4.2 %collective-permute-start.27 = (bf16[224,128]{1,0:T(8,128)(2,1)S(1)}, bf16[224,128]{1,0:T(8,128)(2,1)S(1)}, u32[]{:S(2)}, u32[]{:S(2)}) collective-permute-start(bf16[224,128]{1,0:T(8,128)(2,1)S(1)} %collective-permute-done.26.refs_3_), channel_id=1, source_target_pairs={{0,2},{2,0},{1,3},{3,1},{4,6},{6,4},{5,7},{7,5},{8,10},{10,8},{9,1... | collective-permute-start | bytes 172040 | tf_op jit(solution)/shard_map/ppermute | solution.py:404
  (6 other events, 10.0 us)
